TPU v7x, 256 devices: a whole 4x4x8 slice. The times are simulated.
256 devices in a mesh: pair: 32 (over x, y, core), win: 8 (over z).
Axes of the slice: x: 4, y: 4, z: 8, core: 2. Of those that a mesh axis runs over, the one named last changes fastest.
Arguments:
- spectra: bfloat16 [16, 2048, 2, 2048], P('win', 'pair')
- passband: float32 [2048], replicated, may hold values from 0.1 to 1
- pair_ends: int32 [32, 128, 2], replicated, may hold values from 0 to 2047, as said below
- live_pairs: int32 [32], P('pair'), may hold values from 32 to 128, as said below
Outputs:
- stacked: float32 [4096, 4096], P('pair', 'win')
Inputs may be any that keep to these rules, and one draw needn't show every extreme that they name: `pair_ends`: entries are channel numbers. The first channel of every slot of block b lies in b * 64 to (b + 1) * 64 - 1; the second lies in the channels of blocks b - 3 to b + 3, and in every block some second channel lies exactly 3 blocks away. How many second channels fall on each nearby block varies. `live_pairs`: some block uses all its slots and some block uses 128 // 4.
All inputs are finite; a program needn't handle non-finite values. Where the computation divides by a largest or mean magnitude, that divisor is 1e-20 or more.
Results may differ from a plain program's by a relative error of at most 0.0057.
Values may be sent and summed in bfloat16 or wider, within the bound.
No kernel may reach another device: no remote copies, remote signals or barrier semaphores. Data moves between devices by JAX's collectives and lax.ppermute only.
A program may use at most 64 MiB of HBM per device.

v0:
```python
import math

import jax
import jax.numpy as jnp
from jax import lax
from jax.sharding import PartitionSpec as P

HALF = 3


def from_behind(value, axis, steps):
    count = lax.axis_size(axis)
    initial, last = (max(0, -steps), min(count, count - steps))
    return lax.ppermute(value, axis, [(source, source + steps) for source in range(initial, last)])


def whiten(spectra):
    values = spectra.astype(jnp.float32)
    power = jnp.mean(values * values, axis=(2, 3), keepdims=True)
    return (values * lax.rsqrt(power + 1e-06)).astype(jnp.bfloat16)


def cross_spectra(endpoints, passband, live_mask):
    win_count = endpoints.shape[0]
    pair_count = endpoints.shape[1] // 2
    bin_count = endpoints.shape[3]
    split_ends = endpoints.reshape(win_count, pair_count, 2, 2, bin_count).astype(jnp.float32)
    first_end = split_ends[:, :, 0]
    second_end = split_ends[:, :, 1]
    weighting = passband[None, None, :] * live_mask[None, :, None]
    real_part = (
        first_end[:, :, 0] * second_end[:, :, 0] + first_end[:, :, 1] * second_end[:, :, 1]
    ) * weighting
    imag_part = (
        first_end[:, :, 1] * second_end[:, :, 0] - first_end[:, :, 0] * second_end[:, :, 1]
    ) * weighting
    return jnp.concatenate([real_part, imag_part], axis=2).astype(jnp.bfloat16)


def all_lags(cross_rows, bin_count):
    lag_total = 2 * bin_count
    block_width = min(256, lag_total)
    step_angle = 2.0 * math.pi / lag_total
    freqs = jnp.arange(bin_count, dtype=jnp.int32)
    factor = jnp.where(freqs == 0, 1.0, 2.0).astype(jnp.float32)[:, None]
    base_phase = freqs[:, None] * jnp.arange(block_width, dtype=jnp.int32)[None, :] % lag_total
    base_angle = base_phase.astype(jnp.float32) * step_angle
    base_cos = jnp.cos(base_angle)
    base_sin = jnp.sin(base_angle)

    def one_block(step_index, output):
        offset = step_index * block_width
        start_phase = (freqs * offset % lag_total).astype(jnp.float32) * step_angle
        start_cos = jnp.cos(start_phase)[:, None]
        start_sin = jnp.sin(start_phase)[:, None]
        cos_part = start_cos * base_cos - start_sin * base_sin
        sin_part = start_sin * base_cos + start_cos * base_sin
        lag_cols = jnp.concatenate([factor * cos_part, -factor * sin_part], axis=0).astype(
            jnp.bfloat16
        )
        lag_block = jnp.dot(cross_rows, lag_cols, preferred_element_type=jnp.float32)
        return lax.dynamic_update_slice_in_dim(output, lag_block, offset, 1)

    initial = jnp.zeros((cross_rows.shape[0], lag_total), jnp.float32)
    return lax.fori_loop(0, lag_total // block_width, one_block, initial)


def local(spectra, passband, pair_ends, live_pairs):
    win_count = lax.axis_size("win")
    win_dev = spectra.shape[0]
    ch_dev = spectra.shape[1]
    bin_count = spectra.shape[3]
    slot_count = pair_ends.shape[1]
    lag_total = 2 * bin_count
    norm_scale = 1.0 / math.sqrt(win_dev * win_count)
    whitened = whiten(spectra)
    live_mask = (jnp.arange(slot_count, dtype=jnp.int32) < live_pairs[0]).astype(jnp.float32)
    my_block = lax.axis_index("pair")
    my_ends = lax.dynamic_index_in_dim(pair_ends, my_block, 0, keepdims=False).reshape(
        2 * slot_count
    )
    above = []
    below = []
    for distance in range(1, HALF + 1):
        above.append(from_behind(whitened, "pair", -distance))
        below.append(from_behind(whitened, "pair", distance))
    nearby = jnp.concatenate(below[::-1] + [whitened] + above, axis=1)
    window_rows = (my_ends // ch_dev - my_block + HALF) * ch_dev + my_ends % ch_dev
    endpoints = jnp.take(nearby, window_rows, axis=1)
    cross_spec = cross_spectra(endpoints, passband, live_mask)
    corr = all_lags(cross_spec.reshape(-1, lag_total), bin_count)
    peak = jnp.max(jnp.abs(corr), axis=1, keepdims=True) + 1e-06
    summed = jnp.sum((corr / peak).reshape(win_dev, slot_count, lag_total), axis=0)
    return lax.psum_scatter(summed, "win", scatter_dimension=1, tiled=True) * norm_scale


def solution(mesh):
    placed = (P("win", "pair", None, None), P(), P(), P("pair"))
    return jax.shard_map(
        local, mesh=mesh, in_specs=placed, out_specs=P("pair", "win"), check_vma=False
    )
```

profile of v0, /device:TPU:6, one launch (start us, length us, event | category | flops | bytes accessed | tf_op | source)
XLA Modules:
  0.0 385.6 jit_solution(14020774373731779961)
XLA Ops:
  30.8 9.3 %collective-permute-done = bf16[2,64,2,2048]{3,2,1,0:T(2,128)(2,1)} collective-permute-done((bf16[2,64,2,2048]{3,2,1,0:T(2,128)(2,1)}, bf16[2,64,2,2048]{3,2,1,0:T(2,128)(2,1)}, u32[]{:S(2)}, u32[]{:S(2)}) %collective-permute-start) | collective-permute-done | bytes 1048608 | tf_op jit(solution)/shard_map/ppermute | solution.py:14
  40.1 13.6 %collective-permute-start.5 = (bf16[2,64,2,2048]{3,2,1,0:T(2,128)(2,1)}, bf16[2,64,2,2048]{3,2,1,0:T(2,128)(2,1)S(1)}, u32[]{:S(2)}, u32[]{:S(2)}) collective-permute-start(bf16[2,64,2,2048]{3,2,1,0:T(2,128)(2,1)} %fusion.40), channel_id=1, source_target_pairs={{24,0},{32,8},{40,16},{48,24},{56,32},{64,40},{72,48},{80,56},{88,... | collective-permute-start | bytes 3145736 | tf_op jit(solution)/shard_map/ppermute | solution.py:14
  68.2 10.9 %collective-permute-done.2 = bf16[2,64,2,2048]{3,2,1,0:T(2,128)(2,1)} collective-permute-done((bf16[2,64,2,2048]{3,2,1,0:T(2,128)(2,1)}, bf16[2,64,2,2048]{3,2,1,0:T(2,128)(2,1)}, u32[]{:S(2)}, u32[]{:S(2)}) %collective-permute-start.2) | collective-permute-done | bytes 1048608 | tf_op jit(solution)/shard_map/ppermute | solution.py:14
  87.4 9.9 %collective-permute-done.5 = bf16[2,64,2,2048]{3,2,1,0:T(2,128)(2,1)S(1)} collective-permute-done((bf16[2,64,2,2048]{3,2,1,0:T(2,128)(2,1)}, bf16[2,64,2,2048]{3,2,1,0:T(2,128)(2,1)S(1)}, u32[]{:S(2)}, u32[]{:S(2)}) %collective-permute-start.5) | collective-permute-done | bytes 1048608 | tf_op jit(solution)/shard_map/ppermute | solution.py:14
  99.0 17.4 %gather_fusion = bf16[256,2,2,2048]{3,2,1,0:T(2,128)(2,1)} fusion(bf16[2,448,2,2048]{3,2,1,0:T(2,128)(2,1)} %constant_dynamic-update-slice_fusion, s32[1024]{0:T(1024)S(1)} %pad_clamp_fusion), kind=kCustom, calls=%fused_computation | custom fusion | bytes 8389632 | tf_op jit(solution)/shard_map/jit(_take)/gather | solution.py:89
  128.4 173.3 %while.17 = (s32[]{:T(128)}, f32[256,4096]{0,1:T(8,128)}, bf16[256,4096]{1,0:T(8,128)(2,1)S(1)}, s32[]{:T(128)}, s32[]{:T(128)}, /*index=5*/s32[]{:T(128)}, s32[]{:T(128)}) while((s32[]{:T(128)}, f32[256,4096]{0,1:T(8,128)}, bf16[256,4096]{1,0:T(8,128)(2,1)S(1)}, s32[]{:T(128)}, s32[]{:T(128)}, /*index=5*/s32[]{:T(128)}, ...), condition=%wide.region_2.3_spmd.clone.clone, body=%wide.region_1.2_spmd.clone.clone.sunk | while | flops 553687040 | bytes 6619267 | solution.py:65
  128.4 9.2 %multiply_convert_fusion.3 = (bf16[2048,256]{1,0:T(8,128)(2,1)S(1)}, bf16[2048,256]{1,0:T(8,128)(2,1)S(1)}) fusion(f32[2048]{0:T(1024)S(1)} %get-tuple-element.271, f32[2048]{0:T(1024)S(1)} %get-tuple-element.272, f32[2048]{0:T(1024)S(1)} %bitcast.55, f32[2048]{0:T(1024)S(1)} %bitcast.56), kind=kLoop, calls=%fused_computation.19.clone.1 | loop fusion | flops 12582912 | bytes 2129920 | tf_op jit(solution)/shard_map/convert
  139.3 9.2 %multiply_convert_fusion.3 = (bf16[2048,256]{1,0:T(8,128)(2,1)S(1)}, bf16[2048,256]{1,0:T(8,128)(2,1)S(1)}) fusion(f32[2048]{0:T(1024)S(1)} %get-tuple-element.271, f32[2048]{0:T(1024)S(1)} %get-tuple-element.272, f32[2048]{0:T(1024)S(1)} %bitcast.55, f32[2048]{0:T(1024)S(1)} %bitcast.56), kind=kLoop, calls=%fused_computation.19.clone.1 | loop fusion | flops 12582912 | bytes 2129920 | tf_op jit(solution)/shard_map/convert
  150.1 9.2 %multiply_convert_fusion.3 = (bf16[2048,256]{1,0:T(8,128)(2,1)S(1)}, bf16[2048,256]{1,0:T(8,128)(2,1)S(1)}) fusion(f32[2048]{0:T(1024)S(1)} %get-tuple-element.271, f32[2048]{0:T(1024)S(1)} %get-tuple-element.272, f32[2048]{0:T(1024)S(1)} %bitcast.55, f32[2048]{0:T(1024)S(1)} %bitcast.56), kind=kLoop, calls=%fused_computation.19.clone.1 | loop fusion | flops 12582912 | bytes 2129920 | tf_op jit(solution)/shard_map/convert
  161.0 9.2 %multiply_convert_fusion.3 = (bf16[2048,256]{1,0:T(8,128)(2,1)S(1)}, bf16[2048,256]{1,0:T(8,128)(2,1)S(1)}) fusion(f32[2048]{0:T(1024)S(1)} %get-tuple-element.271, f32[2048]{0:T(1024)S(1)} %get-tuple-element.272, f32[2048]{0:T(1024)S(1)} %bitcast.55, f32[2048]{0:T(1024)S(1)} %bitcast.56), kind=kLoop, calls=%fused_computation.19.clone.1 | loop fusion | flops 12582912 | bytes 2129920 | tf_op jit(solution)/shard_map/convert
  171.8 9.2 %multiply_convert_fusion.3 = (bf16[2048,256]{1,0:T(8,128)(2,1)S(1)}, bf16[2048,256]{1,0:T(8,128)(2,1)S(1)}) fusion(f32[2048]{0:T(1024)S(1)} %get-tuple-element.271, f32[2048]{0:T(1024)S(1)} %get-tuple-element.272, f32[2048]{0:T(1024)S(1)} %bitcast.55, f32[2048]{0:T(1024)S(1)} %bitcast.56), kind=kLoop, calls=%fused_computation.19.clone.1 | loop fusion | flops 12582912 | bytes 2129920 | tf_op jit(solution)/shard_map/convert
  182.6 9.2 %multiply_convert_fusion.3 = (bf16[2048,256]{1,0:T(8,128)(2,1)S(1)}, bf16[2048,256]{1,0:T(8,128)(2,1)S(1)}) fusion(f32[2048]{0:T(1024)S(1)} %get-tuple-element.271, f32[2048]{0:T(1024)S(1)} %get-tuple-element.272, f32[2048]{0:T(1024)S(1)} %bitcast.55, f32[2048]{0:T(1024)S(1)} %bitcast.56), kind=kLoop, calls=%fused_computation.19.clone.1 | loop fusion | flops 12582912 | bytes 2129920 | tf_op jit(solution)/shard_map/convert
  193.5 9.2 %multiply_convert_fusion.3 = (bf16[2048,256]{1,0:T(8,128)(2,1)S(1)}, bf16[2048,256]{1,0:T(8,128)(2,1)S(1)}) fusion(f32[2048]{0:T(1024)S(1)} %get-tuple-element.271, f32[2048]{0:T(1024)S(1)} %get-tuple-element.272, f32[2048]{0:T(1024)S(1)} %bitcast.55, f32[2048]{0:T(1024)S(1)} %bitcast.56), kind=kLoop, calls=%fused_computation.19.clone.1 | loop fusion | flops 12582912 | bytes 2129920 | tf_op jit(solution)/shard_map/convert
  204.3 9.2 %multiply_convert_fusion.3 = (bf16[2048,256]{1,0:T(8,128)(2,1)S(1)}, bf16[2048,256]{1,0:T(8,128)(2,1)S(1)}) fusion(f32[2048]{0:T(1024)S(1)} %get-tuple-element.271, f32[2048]{0:T(1024)S(1)} %get-tuple-element.272, f32[2048]{0:T(1024)S(1)} %bitcast.55, f32[2048]{0:T(1024)S(1)} %bitcast.56), kind=kLoop, calls=%fused_computation.19.clone.1 | loop fusion | flops 12582912 | bytes 2129920 | tf_op jit(solution)/shard_map/convert
  215.1 9.2 %multiply_convert_fusion.3 = (bf16[2048,256]{1,0:T(8,128)(2,1)S(1)}, bf16[2048,256]{1,0:T(8,128)(2,1)S(1)}) fusion(f32[2048]{0:T(1024)S(1)} %get-tuple-element.271, f32[2048]{0:T(1024)S(1)} %get-tuple-element.272, f32[2048]{0:T(1024)S(1)} %bitcast.55, f32[2048]{0:T(1024)S(1)} %bitcast.56), kind=kLoop, calls=%fused_computation.19.clone.1 | loop fusion | flops 12582912 | bytes 2129920 | tf_op jit(solution)/shard_map/convert
  225.9 9.2 %multiply_convert_fusion.3 = (bf16[2048,256]{1,0:T(8,128)(2,1)S(1)}, bf16[2048,256]{1,0:T(8,128)(2,1)S(1)}) fusion(f32[2048]{0:T(1024)S(1)} %get-tuple-element.271, f32[2048]{0:T(1024)S(1)} %get-tuple-element.272, f32[2048]{0:T(1024)S(1)} %bitcast.55, f32[2048]{0:T(1024)S(1)} %bitcast.56), kind=kLoop, calls=%fused_computation.19.clone.1 | loop fusion | flops 12582912 | bytes 2129920 | tf_op jit(solution)/shard_map/convert
  236.8 9.2 %multiply_convert_fusion.3 = (bf16[2048,256]{1,0:T(8,128)(2,1)S(1)}, bf16[2048,256]{1,0:T(8,128)(2,1)S(1)}) fusion(f32[2048]{0:T(1024)S(1)} %get-tuple-element.271, f32[2048]{0:T(1024)S(1)} %get-tuple-element.272, f32[2048]{0:T(1024)S(1)} %bitcast.55, f32[2048]{0:T(1024)S(1)} %bitcast.56), kind=kLoop, calls=%fused_computation.19.clone.1 | loop fusion | flops 12582912 | bytes 2129920 | tf_op jit(solution)/shard_map/convert
  247.6 9.2 %multiply_convert_fusion.3 = (bf16[2048,256]{1,0:T(8,128)(2,1)S(1)}, bf16[2048,256]{1,0:T(8,128)(2,1)S(1)}) fusion(f32[2048]{0:T(1024)S(1)} %get-tuple-element.271, f32[2048]{0:T(1024)S(1)} %get-tuple-element.272, f32[2048]{0:T(1024)S(1)} %bitcast.55, f32[2048]{0:T(1024)S(1)} %bitcast.56), kind=kLoop, calls=%fused_computation.19.clone.1 | loop fusion | flops 12582912 | bytes 2129920 | tf_op jit(solution)/shard_map/convert
  258.5 9.2 %multiply_convert_fusion.3 = (bf16[2048,256]{1,0:T(8,128)(2,1)S(1)}, bf16[2048,256]{1,0:T(8,128)(2,1)S(1)}) fusion(f32[2048]{0:T(1024)S(1)} %get-tuple-element.271, f32[2048]{0:T(1024)S(1)} %get-tuple-element.272, f32[2048]{0:T(1024)S(1)} %bitcast.55, f32[2048]{0:T(1024)S(1)} %bitcast.56), kind=kLoop, calls=%fused_computation.19.clone.1 | loop fusion | flops 12582912 | bytes 2129920 | tf_op jit(solution)/shard_map/convert
  269.3 9.2 %multiply_convert_fusion.3 = (bf16[2048,256]{1,0:T(8,128)(2,1)S(1)}, bf16[2048,256]{1,0:T(8,128)(2,1)S(1)}) fusion(f32[2048]{0:T(1024)S(1)} %get-tuple-element.271, f32[2048]{0:T(1024)S(1)} %get-tuple-element.272, f32[2048]{0:T(1024)S(1)} %bitcast.55, f32[2048]{0:T(1024)S(1)} %bitcast.56), kind=kLoop, calls=%fused_computation.19.clone.1 | loop fusion | flops 12582912 | bytes 2129920 | tf_op jit(solution)/shard_map/convert
  280.1 9.2 %multiply_convert_fusion.3 = (bf16[2048,256]{1,0:T(8,128)(2,1)S(1)}, bf16[2048,256]{1,0:T(8,128)(2,1)S(1)}) fusion(f32[2048]{0:T(1024)S(1)} %get-tuple-element.271, f32[2048]{0:T(1024)S(1)} %get-tuple-element.272, f32[2048]{0:T(1024)S(1)} %bitcast.55, f32[2048]{0:T(1024)S(1)} %bitcast.56), kind=kLoop, calls=%fused_computation.19.clone.1 | loop fusion | flops 12582912 | bytes 2129920 | tf_op jit(solution)/shard_map/convert
  291.0 9.2 %multiply_convert_fusion.3 = (bf16[2048,256]{1,0:T(8,128)(2,1)S(1)}, bf16[2048,256]{1,0:T(8,128)(2,1)S(1)}) fusion(f32[2048]{0:T(1024)S(1)} %get-tuple-element.271, f32[2048]{0:T(1024)S(1)} %get-tuple-element.272, f32[2048]{0:T(1024)S(1)} %bitcast.55, f32[2048]{0:T(1024)S(1)} %bitcast.56), kind=kLoop, calls=%fused_computation.19.clone.1 | loop fusion | flops 12582912 | bytes 2129920 | tf_op jit(solution)/shard_map/convert
  313.2 17.8 %reduce_sum.19 = f32[128,4096]{0,1:T(8,128)} reduce(f32[2,128,4096]{1,0,2:T(2,128)} %reshape.242, f32[]{:T(128)} %constant.137.clone.1), dimensions={0}, to_apply=%region_4.5 | reduce | flops 524288 | bytes 6291460 | tf_op jit(solution)/shard_map/reduce_sum | solution.py:93
  331.0 45.9 %reduce-scatter.2.cloned.1.call-done = f32[128,512]{0,1:T(8,128)} async-done(((f32[128,4096]{0,1:T(8,128)}), f32[128,512]{0,1:T(8,128)}) %reduce-scatter.2.cloned.1.call-update) | async-done | bytes 262160 | tf_op jit(solution)/shard_map/reduce_scatter | solution.py:94
  (109 shorter events, 98.7 us)
Async XLA Ops:
  6.5 24.1 %copy-start.2 = (f32[2048]{0:T(1024)S(1)}, f32[2048]{0:T(1024)}, u32[]{:S(2)}) copy-start(f32[2048]{0:T(1024)} %param.7) | copy-start | bytes 24580
  6.5 370.4 %reduce-scatter.2.cloned.1.call-start = ((), (), s32[]{:S(2)}) async-start(), calls=%async_computation.1 | async-start | bytes 2359296 | tf_op jit(solution)/shard_map/reduce_scatter | solution.py:94
  12.2 27.9 %collective-permute-start = (bf16[2,64,2,2048]{3,2,1,0:T(2,128)(2,1)}, bf16[2,64,2,2048]{3,2,1,0:T(2,128)(2,1)}, u32[]{:S(2)}, u32[]{:S(2)}) collective-permute-start(bf16[2,64,2,2048]{3,2,1,0:T(2,128)(2,1)} %fusion.40), channel_id=1, source_target_pairs={{0,24},{8,32},{16,40},{24,48},{32,56},{40,64},{48,72},{56,80},{64,... | collective-permute-start | bytes 3145736 | tf_op jit(solution)/shard_map/ppermute | solution.py:14
  15.1 50.2 %collective-permute-start.1 = (bf16[2,64,2,2048]{3,2,1,0:T(2,128)(2,1)}, bf16[2,64,2,2048]{3,2,1,0:T(2,128)(2,1)}, u32[]{:S(2)}, u32[]{:S(2)}) collective-permute-start(bf16[2,64,2,2048]{3,2,1,0:T(2,128)(2,1)} %fusion.40), channel_id=1, source_target_pairs={{0,16},{8,24},{16,32},{24,40},{32,48},{40,56},{48,64},{56,72},{64,... | collective-permute-start | bytes 3145736 | tf_op jit(solution)/shard_map/ppermute | solution.py:14
  18.6 60.5 %collective-permute-start.2 = (bf16[2,64,2,2048]{3,2,1,0:T(2,128)(2,1)}, bf16[2,64,2,2048]{3,2,1,0:T(2,128)(2,1)}, u32[]{:S(2)}, u32[]{:S(2)}) collective-permute-start(bf16[2,64,2,2048]{3,2,1,0:T(2,128)(2,1)} %fusion.40), channel_id=1, source_target_pairs={{0,8},{8,16},{16,24},{24,32},{32,40},{40,48},{48,56},{56,64},{64,7... | collective-permute-start | bytes 3145736 | tf_op jit(solution)/shard_map/ppermute | solution.py:14
  21.6 62.3 %collective-permute-start.3 = (bf16[2,64,2,2048]{3,2,1,0:T(2,128)(2,1)}, bf16[2,64,2,2048]{3,2,1,0:T(2,128)(2,1)S(1)}, u32[]{:S(2)}, u32[]{:S(2)}) collective-permute-start(bf16[2,64,2,2048]{3,2,1,0:T(2,128)(2,1)} %fusion.40), channel_id=1, source_target_pairs={{8,0},{16,8},{24,16},{32,24},{40,32},{48,40},{56,48},{64,56},{72,6... | collective-permute-start | bytes 3145736 | tf_op jit(solution)/shard_map/ppermute | solution.py:14
  26.6 59.1 %collective-permute-start.4 = (bf16[2,64,2,2048]{3,2,1,0:T(2,128)(2,1)}, bf16[2,64,2,2048]{3,2,1,0:T(2,128)(2,1)S(1)}, u32[]{:S(2)}, u32[]{:S(2)}) collective-permute-start(bf16[2,64,2,2048]{3,2,1,0:T(2,128)(2,1)} %fusion.40), channel_id=1, source_target_pairs={{16,0},{24,8},{32,16},{40,24},{48,32},{56,40},{64,48},{72,56},{80,... | collective-permute-start | bytes 3145736 | tf_op jit(solution)/shard_map/ppermute | solution.py:14
  40.1 57.2 %collective-permute-start.5 = (bf16[2,64,2,2048]{3,2,1,0:T(2,128)(2,1)}, bf16[2,64,2,2048]{3,2,1,0:T(2,128)(2,1)S(1)}, u32[]{:S(2)}, u32[]{:S(2)}) collective-permute-start(bf16[2,64,2,2048]{3,2,1,0:T(2,128)(2,1)} %fusion.40), channel_id=1, source_target_pairs={{24,0},{32,8},{40,16},{48,24},{56,32},{64,40},{72,48},{80,56},{88,... | collective-permute-start | bytes 3145736 | tf_op jit(solution)/shard_map/ppermute | solution.py:14
  56.7 25.4 %copy-start.1 = (bf16[2,64,2,2048]{3,2,1,0:T(2,128)(2,1)S(1)}, bf16[2,64,2,2048]{3,2,1,0:T(2,128)(2,1)}, u32[]{:S(2)}) copy-start(bf16[2,64,2,2048]{3,2,1,0:T(2,128)(2,1)} %param.6) | copy-start | bytes 3145732
  301.7 3.4 copy-start
Sparse Core Ops, SparseCore 0:
  331.1 45.7 reduce-scatter.1
where the time goes:
time: 386 us
  other arithmetic  189 us (49%)
  waiting for transfers between devices  84.7 us (22%)
  local copies, waits for them, and re-layouts  42.4 us (11%)
  starting transfers between devices  30.3 us (8%)
  matrix products  24.3 us (6%)
  between operations  14.2 us (4%)
    another operation x17, other arithmetic  148 us
    reduce_scatter x1, waiting for transfers between devices, local(): lax.psum_scatter(summed, 'win', scatter_dimension=1, tiled=True)  45.9 us
    ppermute x6, waiting for transfers between devices, from_behind(): lax.ppermute(value, axis, [(source, source + steps) for source in range(i...  38.8 us
    ppermute x6, starting transfers between devices, from_behind(): lax.ppermute(value, axis, [(source, source + steps) for source in range(i...  30.3 us
    dot_general x16, matrix products, one_block(): jnp.dot(cross_rows, lag_cols, preferred_element_type=jnp.float32)  24.3 us
    reduce_sum x1, other arithmetic, local(): jnp.sum((corr / peak).reshape(win_dev, slot_count, lag_total), axis=0)  17.8 us
    gather x1, local copies, waits for them, and re-layouts, local(): endpoints = jnp.take(nearby, window_rows, axis=1)  17.4 us
    unnamed x11, local copies, waits for them, and re-layouts  13.2 us
  transfers between devices with their start and end apart: 7, of which 5 were waited for; matrix products, arithmetic and copies ran while one was open for 4% of the time, Pallas kernels for 0%

commit v1 on v0

v1 whole, which is shorter than its diff:
```python
import functools
import math

import jax
import jax.numpy as jnp
from jax import lax
from jax.experimental import pallas as pl
from jax.experimental.pallas import tpu as pltpu
from jax.sharding import PartitionSpec as P

HALF = 3
BF = jnp.bfloat16
F32 = jnp.float32
VM = pl.BlockSpec(memory_space=pltpu.VMEM)
SM = pl.BlockSpec(memory_space=pltpu.SMEM)
ANY = pl.BlockSpec(memory_space=pl.ANY)

LANES = 128
SUBS = 16
LOW = 2 * SUBS
GROUP = 8


def shift(value, steps):
    count = lax.axis_size("pair")
    return lax.ppermute(
        value, "pair", [(i, i + steps) for i in range(max(0, -steps), min(count, count - steps))]
    )


def swap(value):
    count = lax.axis_size("pair")
    return lax.ppermute(value, "pair", [(i, i ^ 1) for i in range(count)])


def outward(value):
    count = lax.axis_size("pair")
    pairs = [(i, i - 1 if i % 2 == 0 else i + 1) for i in range(count)]
    return lax.ppermute(value, "pair", [(a, b) for a, b in pairs if 0 <= b < count])


def whiten_kernel(perm_ref, x_ref, *out_refs):
    rows = 2 * SUBS
    for window, out_ref in enumerate(out_refs):
        def step(c, _, window=window, out_ref=out_ref):
            values = x_ref[window, pl.ds(c * GROUP, GROUP)].astype(F32)
            power = jnp.mean(jnp.mean(values * values, axis=2, keepdims=True), axis=1, keepdims=True)
            scaled = (values * lax.rsqrt(power + 1e-06)).astype(BF)
            flat = scaled.reshape(GROUP * rows, LANES)
            ordered = jnp.dot(perm_ref[...], flat, preferred_element_type=F32)
            out_ref[pl.ds(c * GROUP, GROUP)] = ordered.astype(BF).reshape(GROUP, rows, LANES)
            return 0

        lax.fori_loop(0, x_ref.shape[1] // GROUP, step, 0)


def corr_kernel(last, first_ref, second_ref, live_ref, *refs):
    near_refs, refs = refs[:7], refs[7:]
    weight_ref, fold_ref, wave_ref, *refs = refs
    prev_ref = None
    if last:
        prev_ref, *refs = refs
    out_ref, near, cross, mid, corr, sem = refs
    channels = near_refs[0].shape[0]
    slots = mid.shape[1]
    for n, ref in enumerate(near_refs):
        pltpu.make_async_copy(ref, near.at[pl.ds(n * channels, channels)], sem.at[n]).start()
    for n, ref in enumerate(near_refs):
        pltpu.make_async_copy(ref, near.at[pl.ds(n * channels, channels)], sem.at[n]).wait()
    weight = weight_ref[...]
    for g in range(slots // (2 * GROUP)):
        buf = g % 2
        for half in range(2):
            for q in range(GROUP):
                p = g * 2 * GROUP + half * GROUP + q
                a = near[first_ref[p]].astype(F32)
                b = near[second_ref[p]].astype(F32)
                ar, ai, br, bi = a[:SUBS], a[SUBS:], b[:SUBS], b[SUBS:]
                re = (ar * br + ai * bi) * weight
                im = (ai * br - ar * bi) * weight
                at = pl.ds(half * LANES, LANES)
                cross[buf, pl.ds(q * 2 * SUBS, SUBS), at] = re.astype(BF)
                cross[buf, pl.ds(q * 2 * SUBS + SUBS, SUBS), at] = im.astype(BF)
        y = jnp.dot(fold_ref[...], cross[buf], preferred_element_type=F32)
        for part in range(2):
            z = y[part * LOW * GROUP : (part + 1) * LOW * GROUP]
            z = jnp.concatenate(
                [
                    z[:, :LANES].reshape(LOW, GROUP, LANES),
                    z[:, LANES:].reshape(LOW, GROUP, LANES),
                ],
                axis=1,
            )
            mid[:, pl.ds(g * 2 * GROUP, 2 * GROUP), pl.ds(part * LANES, LANES)] = z.astype(BF)

    def lags(t2, top):
        c = lax.dot_general(
            wave_ref[t2], mid[t2], (((1,), (1,)), ((), ())), preferred_element_type=F32
        )
        corr[t2] = c
        return jnp.maximum(top, jnp.abs(c))

    top = lax.fori_loop(0, LOW, lags, jnp.zeros((LANES, slots), F32), unroll=4)
    peak = jnp.max(top, axis=0, keepdims=True) + 1e-06
    alive = lax.broadcasted_iota(jnp.int32, (1, slots), 1) < live_ref[0]
    scale = jnp.where(alive, 0.25 / peak, 0.0)
    parts = out_ref.shape[0]
    wide = LANES // parts

    def emit(t2, _):
        for z in range(parts):
            c = corr[t2, pl.ds(z * wide, wide)] * scale
            if last:
                c = c + prev_ref[z, t2]
            out_ref[z, t2] = c.astype(out_ref.dtype)
        return 0

    lax.fori_loop(0, LOW, emit, 0, unroll=2)


def final_kernel(x_ref, out_ref):
    low, wide, slots = x_ref.shape
    rows = jnp.concatenate([x_ref[:, t, :] for t in range(wide)], axis=0)
    out_ref[...] = rows.astype(F32).T


def tables():
    i32 = jnp.int32
    lags = LOW * LANES
    row = jnp.arange(2 * LOW * GROUP, dtype=i32)[:, None]
    col = jnp.arange(2 * SUBS * GROUP, dtype=i32)[None, :]
    out_part, t2, q_row = row // (LOW * GROUP), (row // GROUP) % LOW, row % GROUP
    q_col, in_part, s = col // (2 * SUBS), (col // SUBS) % 2, col % SUBS
    angle = ((s * t2) % LOW).astype(F32) * (2.0 * math.pi / LOW)
    same = jnp.cos(angle)
    cross = jnp.where(out_part == 0, -jnp.sin(angle), jnp.sin(angle))
    fold = jnp.where(out_part == in_part, same, cross)
    fold = jnp.where(q_row == q_col, fold, 0.0).astype(BF)
    t = jnp.arange(LOW, dtype=i32)[:, None, None] + LOW * jnp.arange(LANES, dtype=i32)[None, :, None]
    l = jnp.arange(LANES, dtype=i32)[None, None, :]
    angle = ((l * t) % lags).astype(F32) * (2.0 * math.pi / lags)
    wave = jnp.concatenate([jnp.cos(angle), -jnp.sin(angle)], axis=2).astype(BF)
    return fold, wave


def local(spectra, passband, pair_ends, live_pairs):
    win_count = lax.axis_size("win")
    win_dev, ch_dev, _, bins = spectra.shape
    slots = pair_ends.shape[1]
    rows = 2 * SUBS
    x = spectra.reshape(win_dev, ch_dev, 2, SUBS, LANES).transpose(0, 1, 3, 2, 4)
    x = x.reshape(win_dev, ch_dev, rows, LANES)
    r = jnp.arange(GROUP * rows, dtype=jnp.int32)
    source = (r // rows) * rows + 2 * (r % SUBS) + (r // SUBS) % 2
    perm = (source[:, None] == r[None, :]).astype(BF)
    whitened = pl.pallas_call(
        whiten_kernel,
        out_shape=[jax.ShapeDtypeStruct((ch_dev, rows, LANES), BF)] * win_dev,
        in_specs=[VM, VM],
        out_specs=[VM] * win_dev,
        compiler_params=pltpu.CompilerParams(vmem_limit_bytes=16 << 20),
    )(perm, x)

    me = lax.axis_index("pair")
    odd = me % 2
    near = []
    for w in whitened:
        up, down = shift(w, -2), shift(w, 2)
        near.append([w, swap(w), up, down])
    for n in near:
        n.extend([swap(n[2]), swap(n[3]), outward(jnp.where(odd == 0, n[2], n[3]))])

    ends = lax.dynamic_index_in_dim(pair_ends, me, 0, keepdims=False)
    first = ends[:, 0] % ch_dev
    away = ends[:, 1] // ch_dev - me
    even_at = {0: 0, 1: 1, 2: 2, -2: 3, 3: 4, -1: 5, -3: 6}
    odd_at = {0: 0, -1: 1, 2: 2, -2: 3, 1: 4, -3: 5, 3: 6}
    place = jnp.zeros_like(away)
    for d in range(-HALF, HALF + 1):
        place = jnp.where(away == d, jnp.where(odd == 0, even_at[d], odd_at[d]), place)
    second = place * ch_dev + ends[:, 1] % ch_dev

    fold, wave = tables()
    factor = jnp.where(jnp.arange(bins) == 0, 1.0, 2.0).astype(F32)
    weight = (passband * factor).reshape(SUBS, LANES)

    total = None
    for v in range(win_dev):
        last = v == win_dev - 1
        args = [first, second, live_pairs, *near[v], weight, fold, wave]
        specs = [SM, SM, SM] + [ANY] * 7 + [VM, VM, VM]
        if last:
            args.append(total)
            specs.append(VM)
        total = pl.pallas_call(
            functools.partial(corr_kernel, last),
            out_shape=jax.ShapeDtypeStruct(
                (win_count, LOW, LANES // win_count, slots), BF if last else F32
            ),
            in_specs=specs,
            out_specs=VM,
            scratch_shapes=[
                pltpu.VMEM((7 * ch_dev, rows, LANES), BF),
                pltpu.VMEM((2, GROUP * rows, 2 * LANES), BF),
                pltpu.VMEM((LOW, slots, 2 * LANES), BF),
                pltpu.VMEM((LOW, LANES, slots), F32),
                pltpu.SemaphoreType.DMA((7,)),
            ],
            compiler_params=pltpu.CompilerParams(vmem_limit_bytes=40 << 20),
            cost_estimate=pl.CostEstimate(
                flops=2 * slots * 64 * 4096, bytes_accessed=8 << 20, transcendentals=0
            ),
        )(*args)

    mine = lax.psum_scatter(total, "win", scatter_dimension=0, tiled=True)[0]
    return pl.pallas_call(
        final_kernel,
        out_shape=jax.ShapeDtypeStruct((slots, LOW * LANES // win_count), F32),
        in_specs=[VM],
        out_specs=VM,
    )(mine)


def solution(mesh):
    placed = (P("win", "pair", None, None), P(), P(), P("pair"))
    return jax.shard_map(
        local, mesh=mesh, in_specs=placed, out_specs=P("pair", "win"), check_vma=False
    )
```

time: 386 us -> 119 us (0.31)
  other arithmetic: 189 us -> 14.2 us
  local copies, waits for them, and re-layouts: 42.4 us -> 1.24 us
  waiting for transfers between devices: 84.7 us -> 45.8 us
  matrix products: 24.3 us -> 0 us
  Pallas kernels: 0 us -> 18.8 us
  starting transfers between devices: 30.3 us -> 23.9 us
    another operation x17 -> x1, other arithmetic: 148 us -> 9.1 us
    ppermute x6 -> x12, waiting for transfers between devices: 38.8 us -> 4.14 us  [the longest x2 3.46 us: outward(): lax.ppermute(value, 'pair', [(a, b) for a, b in pairs if 0 <= b < count])]
    dot_general x16 -> x0, matrix products: 24.3 us -> none  [one_block(): jnp.dot(cross_rows, lag_cols, preferred_element_type=jnp.float32)]
    reduce_sum x2 -> x0, other arithmetic: 20.3 us -> none  [the longest x1 17.8 us: local(): jnp.sum((corr / peak).reshape(win_dev, slot_count, lag_total), axis=0)]
    pallas_call x0 -> x4, Pallas kernels: none -> 18.8 us  [the longest x2 11.5 us: local(): pl.pallas_call(functools.partial(corr_kernel, last), out_shape=jax.ShapeD...]
    gather x1 -> x0, local copies, waits for them, and re-layouts: 17.4 us -> none  [local(): endpoints = jnp.take(nearby, window_rows, axis=1)]
    unnamed x11 -> x6, local copies, waits for them, and re-layouts: 13.2 us -> 1.23 us
    convert_element_type x3 -> x2, other arithmetic: 10.2 us -> 2.81 us  [the longest x1 2.71 us: tables(): fold = jnp.where(q_row == q_col, fold, 0.0).astype(BF)]
  transfers between devices with their start and end apart: 7 -> 13, of which waited for: 5 -> 3; matrix products, arithmetic and copies ran while one was open for 4% -> 12% of each run, Pallas kernels for 0% -> 5%
where the time goes in v1:
time: 119 us; the launch traced here: 118 us
  waiting for transfers between devices  45.8 us (38%)
  starting transfers between devices  23.9 us (20%)
  Pallas kernels  18.8 us (16%)
  between operations  14.3 us (12%)
  other arithmetic  14.2 us (12%)
  local copies, waits for them, and re-layouts  1.24 us (1%)
    reduce_scatter x1, waiting for transfers between devices, local(): mine = lax.psum_scatter(total, 'win', scatter_dimension=0, tiled=True)[0]  41.6 us
    ppermute x4, starting transfers between devices, shift(): lax.ppermute(value, 'pair', [(i, i + steps) for i in range(max(0, -steps)...  15.1 us
    pallas_call x2, Pallas kernels, local(): pl.pallas_call(functools.partial(corr_kernel, last), out_shape=jax.ShapeD...  11.5 us
    another operation x1, other arithmetic  9.1 us
    ppermute x2, starting transfers between devices, outward(): lax.ppermute(value, 'pair', [(a, b) for a, b in pairs if 0 <= b < count])  7.47 us
    pallas_call x1, Pallas kernels, local(): pl.pallas_call(whiten_kernel, out_shape=[jax.ShapeDtypeStruct((ch_dev, ro...  5.39 us
    ppermute x2, waiting for transfers between devices, outward(): lax.ppermute(value, 'pair', [(a, b) for a, b in pairs if 0 <= b < count])  3.46 us
    convert_element_type x1, other arithmetic, tables(): fold = jnp.where(q_row == q_col, fold, 0.0).astype(BF)  2.71 us
  transfers between devices with their start and end apart: 13, of which 3 were waited for; matrix products, arithmetic and copies ran while one was open for 12% of the time, Pallas kernels for 5%

profile of v1, /device:TPU:6, one launch (start us, length us, event | category | flops | bytes accessed | tf_op | source)
XLA Modules:
  0.0 118.2 jit_solution(3684568445937463892)
XLA Ops:
  6.5 0.1 fusion.12.perm_ref
  6.7 1.2 %copy-done.1 = bf16[2,64,2,2048]{3,2,1,0:T(2,128)(2,1)S(1)} copy-done((bf16[2,64,2,2048]{3,2,1,0:T(2,128)(2,1)S(1)}, bf16[2,64,2,2048]{3,2,1,0:T(2,128)(2,1)}, u32[]{:S(2)}) %copy-start.1) | copy-done | bytes 1048600
  7.9 5.4 %shard_map.46 = (bf16[64,32,128]{2,1,0:T(8,128)(2,1)}, bf16[64,32,128]{2,1,0:T(8,128)(2,1)}) custom-call(bf16[256,256]{1,0:T(8,128)(2,1)S(1)} %fusion.12.perm_ref, bf16[2,64,32,128]{3,2,1,0:T(8,128)(2,1)S(1)} %bitcast.25), custom_call_target="tpu_custom_call" | custom-call | tf_op jit(solution)/shard_map/pallas_call | solution.py:156
  13.3 5.2 %collective-permute-start.7 = (bf16[64,32,128]{2,1,0:T(8,128)(2,1)}, bf16[64,32,128]{2,1,0:T(8,128)(2,1)}, u32[]{:S(2)}, u32[]{:S(2)}) collective-permute-start(bf16[64,32,128]{2,1,0:T(8,128)(2,1)} %get-tuple-element.8.refs_0_), channel_id=1, source_target_pairs={{16,0},{24,8},{32,16},{40,24},{48,32},{56,40},{64,48},{72,56},{80,... | collective-permute-start | bytes 1572872 | tf_op jit(solution)/shard_map/ppermute | solution.py:26
  18.5 1.9 %collective-permute-start.8 = (bf16[64,32,128]{2,1,0:T(8,128)(2,1)}, bf16[64,32,128]{2,1,0:T(8,128)(2,1)}, u32[]{:S(2)}, u32[]{:S(2)}) collective-permute-start(bf16[64,32,128]{2,1,0:T(8,128)(2,1)} %get-tuple-element.8.refs_0_), channel_id=1, source_target_pairs={{0,16},{8,24},{16,32},{24,40},{32,48},{40,56},{48,64},{56,72},{64,... | collective-permute-start | bytes 1572872 | tf_op jit(solution)/shard_map/ppermute | solution.py:26
  20.4 0.1 collective-permute-start.6
  20.5 6.0 %collective-permute-start.1 = (bf16[64,32,128]{2,1,0:T(8,128)(2,1)}, bf16[64,32,128]{2,1,0:T(8,128)(2,1)S(1)}, u32[]{:S(2)}, u32[]{:S(2)}) collective-permute-start(bf16[64,32,128]{2,1,0:T(8,128)(2,1)} %get-tuple-element.7.refs_0_), channel_id=1, source_target_pairs={{16,0},{24,8},{32,16},{40,24},{48,32},{56,40},{64,48},{72,56},{80,... | collective-permute-start | bytes 1572872 | tf_op jit(solution)/shard_map/ppermute | solution.py:26
  26.5 1.9 %collective-permute-start.2 = (bf16[64,32,128]{2,1,0:T(8,128)(2,1)}, bf16[64,32,128]{2,1,0:T(8,128)(2,1)S(1)}, u32[]{:S(2)}, u32[]{:S(2)}) collective-permute-start(bf16[64,32,128]{2,1,0:T(8,128)(2,1)} %get-tuple-element.7.refs_0_), channel_id=1, source_target_pairs={{0,16},{8,24},{16,32},{24,40},{32,48},{40,56},{48,64},{56,72},{64,... | collective-permute-start | bytes 1572872 | tf_op jit(solution)/shard_map/ppermute | solution.py:26
  28.6 9.1 %cosine_convert_fusion = (bf16[32,128,128]{2,1,0:T(8,128)(2,1)S(1)}, bf16[32,128,128]{2,1,0:T(8,128)(2,1)S(1)}) fusion(s32[32,128]{1,0:T(8,128)S(1)} %iota_add_fusion), kind=kLoop, calls=%fused_computation.8 | loop fusion | flops 8912896 | bytes 2113536 | tf_op jit(solution)/shard_map/convert
  37.7 0.3 pad_maximum_fusion.refs_9_
  38.0 1.9 %broadcast_select_fusion = bf16[64,32,128]{2,1,0:T(8,128)(2,1)} fusion(bf16[64,32,128]{2,1,0:T(8,128)(2,1)} %collective-permute-done.7.refs_2_, bf16[64,32,128]{2,1,0:T(8,128)(2,1)} %collective-permute-done.8.refs_3_, pred[]{:T(512)S(6)} %eq.134), kind=kLoop, calls=%fused_computation.24 | loop fusion | flops 262144 | bytes 1572865 | tf_op jit(solution)/shard_map/jit(_where)/select_n | solution.py:171
  39.9 5.6 %collective-permute-start.11 = (bf16[64,32,128]{2,1,0:T(8,128)(2,1)}, bf16[64,32,128]{2,1,0:T(8,128)(2,1)}, u32[]{:S(2)}, u32[]{:S(2)}) collective-permute-start(bf16[64,32,128]{2,1,0:T(8,128)(2,1)} %broadcast_select_fusion), channel_id=1, source_target_pairs={{8,16},{16,8},{24,32},{32,24},{40,48},{48,40},{56,64},{64,56},{72,... | collective-permute-start | bytes 1572872 | tf_op jit(solution)/shard_map/ppermute | solution.py:39
  45.4 0.1 collective-permute-start.10
  46.3 0.6 collective-permute-start
  46.8 0.7 collective-permute-done.2.refs_3_
  47.5 1.9 %collective-permute-start.5 = (bf16[64,32,128]{2,1,0:T(8,128)(2,1)S(1)}, bf16[64,32,128]{2,1,0:T(8,128)(2,1)S(1)}, u32[]{:S(2)}, u32[]{:S(2)}) collective-permute-start(bf16[64,32,128]{2,1,0:T(8,128)(2,1)S(1)} %broadcast_select_fusion.1), channel_id=1, source_target_pairs={{8,16},{16,8},{24,32},{32,24},{40,48},{48,40},{56,64},{64,56},{72,... | collective-permute-start | bytes 1572872 | tf_op jit(solution)/shard_map/ppermute | solution.py:39
  49.5 0.1 collective-permute-start.9
  49.6 3.5 %collective-permute-done.11.refs_6_ = bf16[64,32,128]{2,1,0:T(8,128)(2,1)} collective-permute-done((bf16[64,32,128]{2,1,0:T(8,128)(2,1)}, bf16[64,32,128]{2,1,0:T(8,128)(2,1)}, u32[]{:S(2)}, u32[]{:S(2)}) %collective-permute-start.11) | collective-permute-done | bytes 524320 | tf_op jit(solution)/shard_map/ppermute | solution.py:39
  53.0 0.5 collective-permute-start.4
  53.6 2.7 %fusion.10.refs_8_ = bf16[512,256]{1,0:T(8,128)(2,1)S(1)} fusion(s32[512]{0:T(512)S(1)} %get-tuple-element.13, s32[256]{0:T(256)S(1)} %get-tuple-element.16, s32[256]{0:T(256)S(1)} %get-tuple-element.15, s32[256]{0:T(256)S(1)} %and_select_fusion.3, s32[512]{0:T(512)S(1)} %get-tuple-element.14, s32[512]{0:T(512)S(1)} %add_select_fusion.5, ...), kind=kLoop, calls=%fused_computation.22 | loop fusion | flops 2752512 | bytes 271872 | tf_op jit(solution)/shard_map/convert_element_type | solution.py:138
  56.3 5.6 %shard_map.47.refs_10_ = f32[8,32,16,128]{3,2,1,0:T(8,128)S(1)} custom-call(s32[128]{0:T(128)S(1)} %get-tuple-element.12.first_ref, s32[128]{0:T(128)S(1)} %get-tuple-element.11.second_ref, s32[1]{0:T(128)S(6)} %copy.6.live_ref, bf16[64,32,128]{2,1,0:T(8,128)(2,1)} %get-tuple-element.8.refs_0_, bf16[64,32,128]{2,1,0:T(8,128)(2,1)} %collective-permute-done.6.refs_1_, ...), custom_call_target="tpu_custom_call" | custom-call | flops 67108864 | bytes 8388608 | tf_op jit(solution)/shard_map/pallas_call | solution.py:195
  62.0 5.9 %shard_map.48 = bf16[8,32,16,128]{3,2,1,0:T(8,128)(2,1)} custom-call(s32[128]{0:T(128)S(1)} %get-tuple-element.12.first_ref, s32[128]{0:T(128)S(1)} %get-tuple-element.11.second_ref, s32[1]{0:T(128)S(6)} %copy.6.live_ref, bf16[64,32,128]{2,1,0:T(8,128)(2,1)} %get-tuple-element.7.refs_0_, bf16[64,32,128]{2,1,0:T(8,128)(2,1)S(1)} %collective-permute-done.refs_1_, ...), custom_call_target="tpu_custom_call" | custom-call | flops 67108864 | bytes 8388608 | tf_op jit(solution)/shard_map/pallas_call | solution.py:195
  67.9 41.6 %reduce-scatter.2.cloned.1.call-done = bf16[1,32,16,128]{3,2,1,0:T(8,128)(2,1)} async-done(((bf16[8,32,16,128]{3,2,1,0:T(8,128)(2,1)}), bf16[1,32,16,128]{3,2,1,0:T(8,128)(2,1)}) %reduce-scatter.2.cloned.1.call-update) | async-done | bytes 131088 | tf_op jit(solution)/shard_map/reduce_scatter | solution.py:215
  109.5 1.9 %shard_map.49 = f32[128,512]{1,0:T(8,128)} custom-call(bf16[32,16,128]{2,1,0:T(8,128)(2,1)} %bitcast.26), custom_call_target="tpu_custom_call" | custom-call | tf_op jit(solution)/shard_map/pallas_call | solution.py:216
  (30 shorter events, 0.2 us)
Async XLA Ops:
  6.5 39.0 %copy-start = (s32[32,128,2]{1,2,0:T(2,128)S(1)}, s32[32,128,2]{1,2,0:T(2,128)}, u32[]{:S(2)}) copy-start(s32[32,128,2]{1,2,0:T(2,128)} %param.6) | copy-start | bytes 98308
  6.5 103.0 %reduce-scatter.2.cloned.1.call-start = ((), (), s32[]{:S(2)}) async-start(), calls=%async_computation.1 | async-start | bytes 1179648 | tf_op jit(solution)/shard_map/reduce_scatter | solution.py:215
  6.7 1.2 %copy-start.1 = (bf16[2,64,2,2048]{3,2,1,0:T(2,128)(2,1)S(1)}, bf16[2,64,2,2048]{3,2,1,0:T(2,128)(2,1)}, u32[]{:S(2)}) copy-start(bf16[2,64,2,2048]{3,2,1,0:T(2,128)(2,1)} %param.4) | copy-start | bytes 3145732
  13.3 24.7 %collective-permute-start.7 = (bf16[64,32,128]{2,1,0:T(8,128)(2,1)}, bf16[64,32,128]{2,1,0:T(8,128)(2,1)}, u32[]{:S(2)}, u32[]{:S(2)}) collective-permute-start(bf16[64,32,128]{2,1,0:T(8,128)(2,1)} %get-tuple-element.8.refs_0_), channel_id=1, source_target_pairs={{16,0},{24,8},{32,16},{40,24},{48,32},{56,40},{64,48},{72,56},{80,... | collective-permute-start | bytes 1572872 | tf_op jit(solution)/shard_map/ppermute | solution.py:26
  18.5 19.5 %collective-permute-start.8 = (bf16[64,32,128]{2,1,0:T(8,128)(2,1)}, bf16[64,32,128]{2,1,0:T(8,128)(2,1)}, u32[]{:S(2)}, u32[]{:S(2)}) collective-permute-start(bf16[64,32,128]{2,1,0:T(8,128)(2,1)} %get-tuple-element.8.refs_0_), channel_id=1, source_target_pairs={{0,16},{8,24},{16,32},{24,40},{32,48},{40,56},{48,64},{56,72},{64,... | collective-permute-start | bytes 1572872 | tf_op jit(solution)/shard_map/ppermute | solution.py:26
  20.4 29.1 %collective-permute-start.6 = (bf16[64,32,128]{2,1,0:T(8,128)(2,1)}, bf16[64,32,128]{2,1,0:T(8,128)(2,1)}, u32[]{:S(2)}, u32[]{:S(2)}) collective-permute-start(bf16[64,32,128]{2,1,0:T(8,128)(2,1)} %get-tuple-element.8.refs_0_), channel_id=1, source_target_pairs={{0,8},{8,0},{16,24},{24,16},{32,40},{40,32},{48,56},{56,48},{64,72... | collective-permute-start | bytes 1572872 | tf_op jit(solution)/shard_map/ppermute | solution.py:33
  20.5 25.8 %collective-permute-start.1 = (bf16[64,32,128]{2,1,0:T(8,128)(2,1)}, bf16[64,32,128]{2,1,0:T(8,128)(2,1)S(1)}, u32[]{:S(2)}, u32[]{:S(2)}) collective-permute-start(bf16[64,32,128]{2,1,0:T(8,128)(2,1)} %get-tuple-element.7.refs_0_), channel_id=1, source_target_pairs={{16,0},{24,8},{32,16},{40,24},{48,32},{56,40},{64,48},{72,56},{80,... | collective-permute-start | bytes 1572872 | tf_op jit(solution)/shard_map/ppermute | solution.py:26
  26.5 20.9 %collective-permute-start.2 = (bf16[64,32,128]{2,1,0:T(8,128)(2,1)}, bf16[64,32,128]{2,1,0:T(8,128)(2,1)S(1)}, u32[]{:S(2)}, u32[]{:S(2)}) collective-permute-start(bf16[64,32,128]{2,1,0:T(8,128)(2,1)} %get-tuple-element.7.refs_0_), channel_id=1, source_target_pairs={{0,16},{8,24},{16,32},{24,40},{32,48},{40,56},{48,64},{56,72},{64,... | collective-permute-start | bytes 1572872 | tf_op jit(solution)/shard_map/ppermute | solution.py:26
  37.9 15.6 %copy-start.2 = (f32[2048]{0:T(1024)S(1)}, f32[2048]{0:T(1024)}, u32[]{:S(2)}) copy-start(f32[2048]{0:T(1024)} %param.5) | copy-start | bytes 24580
  39.9 13.2 %collective-permute-start.11 = (bf16[64,32,128]{2,1,0:T(8,128)(2,1)}, bf16[64,32,128]{2,1,0:T(8,128)(2,1)}, u32[]{:S(2)}, u32[]{:S(2)}) collective-permute-start(bf16[64,32,128]{2,1,0:T(8,128)(2,1)} %broadcast_select_fusion), channel_id=1, source_target_pairs={{8,16},{16,8},{24,32},{32,24},{40,48},{48,40},{56,64},{64,56},{72,... | collective-permute-start | bytes 1572872 | tf_op jit(solution)/shard_map/ppermute | solution.py:39
  45.4 7.6 %collective-permute-start.10 = (bf16[64,32,128]{2,1,0:T(8,128)(2,1)}, bf16[64,32,128]{2,1,0:T(8,128)(2,1)}, u32[]{:S(2)}, u32[]{:S(2)}) collective-permute-start(bf16[64,32,128]{2,1,0:T(8,128)(2,1)} %collective-permute-done.8.refs_3_), channel_id=1, source_target_pairs={{0,8},{8,0},{16,24},{24,16},{32,40},{40,32},{48,56},{56,48},{64,72... | collective-permute-start | bytes 1572872 | tf_op jit(solution)/shard_map/ppermute | solution.py:33
  46.3 15.7 %collective-permute-start = (bf16[64,32,128]{2,1,0:T(8,128)(2,1)}, bf16[64,32,128]{2,1,0:T(8,128)(2,1)S(1)}, u32[]{:S(2)}, u32[]{:S(2)}) collective-permute-start(bf16[64,32,128]{2,1,0:T(8,128)(2,1)} %get-tuple-element.7.refs_0_), channel_id=1, source_target_pairs={{0,8},{8,0},{16,24},{24,16},{32,40},{40,32},{48,56},{56,48},{64,72... | collective-permute-start | bytes 1572872 | tf_op jit(solution)/shard_map/ppermute | solution.py:33
  47.5 14.4 %collective-permute-start.5 = (bf16[64,32,128]{2,1,0:T(8,128)(2,1)S(1)}, bf16[64,32,128]{2,1,0:T(8,128)(2,1)S(1)}, u32[]{:S(2)}, u32[]{:S(2)}) collective-permute-start(bf16[64,32,128]{2,1,0:T(8,128)(2,1)S(1)} %broadcast_select_fusion.1), channel_id=1, source_target_pairs={{8,16},{16,8},{24,32},{32,24},{40,48},{48,40},{56,64},{64,56},{72,... | collective-permute-start | bytes 1572872 | tf_op jit(solution)/shard_map/ppermute | solution.py:39
  49.5 6.8 %collective-permute-start.9 = (bf16[64,32,128]{2,1,0:T(8,128)(2,1)}, bf16[64,32,128]{2,1,0:T(8,128)(2,1)S(1)}, u32[]{:S(2)}, u32[]{:S(2)}) collective-permute-start(bf16[64,32,128]{2,1,0:T(8,128)(2,1)} %collective-permute-done.7.refs_2_), channel_id=1, source_target_pairs={{0,8},{8,0},{16,24},{24,16},{32,40},{40,32},{48,56},{56,48},{64,72... | collective-permute-start | bytes 1572872 | tf_op jit(solution)/shard_map/ppermute | solution.py:33
  53.0 8.9 %collective-permute-start.3 = (bf16[64,32,128]{2,1,0:T(8,128)(2,1)S(1)}, bf16[64,32,128]{2,1,0:T(8,128)(2,1)S(1)}, u32[]{:S(2)}, u32[]{:S(2)}) collective-permute-start(bf16[64,32,128]{2,1,0:T(8,128)(2,1)S(1)} %collective-permute-done.1.refs_2_), channel_id=1, source_target_pairs={{0,8},{8,0},{16,24},{24,16},{32,40},{40,32},{48,56},{56,48},{64,72... | collective-permute-start | bytes 1572872 | tf_op jit(solution)/shard_map/ppermute | solution.py:33
  53.0 8.9 %collective-permute-start.4 = (bf16[64,32,128]{2,1,0:T(8,128)(2,1)S(1)}, bf16[64,32,128]{2,1,0:T(8,128)(2,1)S(1)}, u32[]{:S(2)}, u32[]{:S(2)}) collective-permute-start(bf16[64,32,128]{2,1,0:T(8,128)(2,1)S(1)} %collective-permute-done.2.refs_3_), channel_id=1, source_target_pairs={{0,8},{8,0},{16,24},{24,16},{32,40},{40,32},{48,56},{56,48},{64,72... | collective-permute-start | bytes 1572872 | tf_op jit(solution)/shard_map/ppermute | solution.py:33
Sparse Core Ops, SparseCore 0:
  68.0 41.4 reduce-scatter.1

commit v2 on v0

v2 whole, which is shorter than its diff:
```python
import functools
import math

import jax
import jax.numpy as jnp
from jax import lax
from jax.experimental import pallas as pl
from jax.experimental.pallas import tpu as pltpu
from jax.sharding import PartitionSpec as P

HALF = 3
BF = jnp.bfloat16
F32 = jnp.float32
VM = pl.BlockSpec(memory_space=pltpu.VMEM)
SM = pl.BlockSpec(memory_space=pltpu.SMEM)
ANY = pl.BlockSpec(memory_space=pl.ANY)

LANES = 128
SUBS = 16
LOW = 2 * SUBS
GROUP = 8


def moved(value, where):
    count = lax.axis_size("pair")
    pairs = [(i, where(i)) for i in range(count)]
    return lax.ppermute(value, "pair", [(a, b) for a, b in pairs if 0 <= b < count])


def swap(value):
    count = lax.axis_size("pair")
    return lax.ppermute(value, "pair", [(i, i ^ 1) for i in range(count)])


def whiten_kernel(x_ref, out_ref):
    rows = 2 * SUBS
    size = GROUP * rows
    r = lax.broadcasted_iota(jnp.int32, (size, size), 0)
    c = lax.broadcasted_iota(jnp.int32, (size, size), 1)
    source = (r // rows) * rows + 2 * (r % SUBS) + (r // SUBS) % 2
    perm = jnp.where(c == source, 1.0, 0.0).astype(BF)

    for window in range(x_ref.shape[0]):
        for g in range(x_ref.shape[1] // GROUP):
            at = pl.ds(g * GROUP, GROUP)
            values = x_ref[window, at].astype(F32)
            power = jnp.sum(jnp.sum(values * values, axis=1), axis=1, keepdims=True)
            power = power * (1.0 / (rows * LANES))
            scaled = (values * lax.rsqrt(power + 1e-06)[:, :, None]).astype(BF)
            ordered = jnp.dot(perm, scaled.reshape(size, LANES), preferred_element_type=F32)
            out_ref[window, at] = ordered.astype(BF).reshape(GROUP, rows, LANES)


def stage_kernel(*refs):
    *near_refs, out_ref, sem = refs
    channels = near_refs[0].shape[1]
    copies = [
        pltpu.make_async_copy(
            ref.at[v], out_ref.at[v, pl.ds(n * channels, channels)], sem.at[n, v]
        )
        for n, ref in enumerate(near_refs)
        for v in range(ref.shape[0])
    ]
    for copy in copies:
        copy.start()
    for copy in copies:
        copy.wait()


def corr_kernel(
    first_ref,
    second_ref,
    live_ref,
    z_ref,
    near_ref,
    weight_ref,
    fold_ref,
    wave_ref,
    keep_ref,
    up_ref,
    down_ref,
    cross,
    mid,
    corr,
):
    windows = near_ref.shape[0]
    slots = mid.shape[1] // windows
    weight = weight_ref[...]
    alive = lax.broadcasted_iota(jnp.int32, (1, slots), 1) < live_ref[0]
    _, half_rows, wide, _ = up_ref.shape
    count = LANES // wide

    for v in range(windows):
        for g in range(slots // (2 * GROUP)):
            buf = g % 2
            for half in range(2):
                for q in range(GROUP):
                    p = g * 2 * GROUP + half * GROUP + q
                    a = near_ref[v, first_ref[p]].astype(F32)
                    b = near_ref[v, second_ref[p]].astype(F32)
                    ar, ai, br, bi = a[:SUBS], a[SUBS:], b[:SUBS], b[SUBS:]
                    re = (ar * br + ai * bi) * weight
                    im = (ai * br - ar * bi) * weight
                    cols = pl.ds(half * LANES, LANES)
                    cross[buf, pl.ds(q * 2 * SUBS, SUBS), cols] = re.astype(BF)
                    cross[buf, pl.ds(q * 2 * SUBS + SUBS, SUBS), cols] = im.astype(BF)
            y = jnp.dot(fold_ref[...], cross[buf], preferred_element_type=F32)
            for part in range(2):
                z = y[part * LOW * GROUP : (part + 1) * LOW * GROUP]
                z = jnp.concatenate(
                    [
                        z[:, :LANES].reshape(LOW, GROUP, LANES),
                        z[:, LANES:].reshape(LOW, GROUP, LANES),
                    ],
                    axis=1,
                )
                rows = pl.ds(v * slots + g * 2 * GROUP, 2 * GROUP)
                mid[:, rows, pl.ds(part * LANES, LANES)] = z.astype(BF)

    def lags(t2, top):
        c = lax.dot_general(
            wave_ref[t2], mid[t2], (((1,), (1,)), ((), ())), preferred_element_type=F32
        )
        corr[t2] = c
        return jnp.maximum(top, jnp.abs(c))

    top = jnp.zeros((LANES, windows * slots), F32)
    top = lax.fori_loop(0, LOW, lags, top, unroll=True)
    peak = jnp.max(top, axis=0, keepdims=True) + 1e-06
    scale = [
        jnp.where(alive, 0.25 / peak[:, v * slots : (v + 1) * slots], 0.0)
        for v in range(windows)
    ]

    jobs = []
    for step, give_ref in ((1, up_ref), (-1, down_ref)):
        jobs += [(step, n, give_ref, n) for n in range(2)]
        jobs += [(-2 * step, n, give_ref, 2 + n) for n in range(2)]
        jobs += [(4, (1 + step) // 2, give_ref, 4)]
    for k, step in enumerate((0, -3, 3)):
        jobs += [(step, n, keep_ref, 2 * k + n) for n in range(2)]
    for step, n, ref, at in jobs:
        rows = pl.ds(lax.rem(z_ref[0] + step + count, count) * wide, wide)

        def emit(t, _, n=n, ref=ref, at=at, rows=rows):
            t2 = t + n * half_rows
            value = corr[t2, rows, pl.ds(0, slots)] * scale[0]
            for v in range(1, windows):
                value = value + corr[t2, rows, pl.ds(v * slots, slots)] * scale[v]
            ref[at, t] = value.astype(ref.dtype)
            return 0

        lax.fori_loop(0, half_rows, emit, 0, unroll=True)


def merge_kernel(keep_ref, left_ref, right_ref, own_ref, behind_ref, ahead_ref):
    for n in range(2):
        own_ref[n] = keep_ref[n] + left_ref[n].astype(F32) + right_ref[n].astype(F32)
        behind = keep_ref[2 + n] + left_ref[2 + n].astype(F32)
        ahead = keep_ref[4 + n] + right_ref[2 + n].astype(F32)
        if n == 0:
            behind = behind + right_ref[4].astype(F32)
        else:
            ahead = ahead + left_ref[4].astype(F32)
        behind_ref[n] = behind.astype(BF)
        ahead_ref[n] = ahead.astype(BF)


def final_kernel(own_ref, *refs):
    *other_refs, out_ref, total = refs
    halves, half_rows, wide, _ = own_ref.shape
    low = halves * half_rows
    for t2 in range(low):
        n, t = divmod(t2, half_rows)
        rows = own_ref[n, t]
        for ref in other_refs:
            rows = rows + ref[n, t].astype(F32)
        total[pl.ds(t2 * wide, wide)] = rows
    group = LANES // low
    for g in range(wide // group):
        rows = [total[pl.ds(g * group + t, low, stride=wide)] for t in range(group)]
        out_ref[:, pl.ds(g * LANES, LANES)] = jnp.concatenate(rows, axis=0).T


def table_kernel(own_ref, _, fold_ref, wave_ref, again_ref):
    def turns(rows, cols, period):
        r = lax.broadcasted_iota(jnp.int32, (rows, cols), 0)
        c = lax.broadcasted_iota(jnp.int32, (rows, cols), 1)
        angle = lax.rem(r * c, period).astype(F32) * (2.0 * math.pi / period)
        return jnp.cos(angle), jnp.sin(angle)

    again_ref[...] = own_ref[...]

    cos, sin = turns(LOW, SUBS, LOW)
    base = jnp.concatenate(
        [jnp.concatenate([cos, -sin], axis=1), jnp.concatenate([sin, cos], axis=1)], axis=0
    ).astype(BF)
    rows, cols = fold_ref.shape
    spread_rows = lax.broadcasted_iota(jnp.int32, (rows, 2 * LOW), 0) // GROUP
    spread_rows = spread_rows == lax.broadcasted_iota(jnp.int32, (rows, 2 * LOW), 1)
    spread_cols = lax.rem(lax.broadcasted_iota(jnp.int32, (2 * SUBS, cols), 1), 2 * SUBS)
    spread_cols = spread_cols == lax.broadcasted_iota(jnp.int32, (2 * SUBS, cols), 0)
    fold = jnp.dot(spread_rows.astype(F32).astype(BF), base, preferred_element_type=F32)
    fold = jnp.dot(
        fold.astype(BF), spread_cols.astype(F32).astype(BF), preferred_element_type=F32
    )
    q_row = lax.rem(lax.broadcasted_iota(jnp.int32, (rows, cols), 0), GROUP)
    q_col = lax.broadcasted_iota(jnp.int32, (rows, cols), 1) // (2 * SUBS)
    fold_ref[...] = jnp.where(q_row == q_col, fold, 0.0).astype(BF)

    low_cos, low_sin = turns(LOW, LANES, LOW * LANES)
    high_cos, high_sin = turns(LANES, LANES, LANES)
    for t2 in range(LOW):
        c, s = low_cos[t2 : t2 + 1], low_sin[t2 : t2 + 1]
        wave_ref[t2, :, pl.ds(0, LANES)] = (c * high_cos - s * high_sin).astype(BF)
        wave_ref[t2, :, pl.ds(LANES, LANES)] = (-s * high_cos - c * high_sin).astype(BF)


def local(spectra, passband, pair_ends, live_pairs):
    win_count = lax.axis_size("win")
    win_dev, ch_dev, _, bins = spectra.shape
    slots = pair_ends.shape[1]
    rows = 2 * SUBS
    wide = LANES // win_count
    half = LOW // 2
    x = spectra.reshape(win_dev, ch_dev, 2, SUBS, LANES).transpose(0, 1, 3, 2, 4)
    x = x.reshape(win_dev, ch_dev, rows, LANES)
    own = pl.pallas_call(
        whiten_kernel,
        out_shape=jax.ShapeDtypeStruct(x.shape, BF),
        in_specs=[VM],
        out_specs=VM,
        compiler_params=pltpu.CompilerParams(vmem_limit_bytes=16 << 20),
    )(x)
    me = lax.axis_index("pair")
    odd = me % 2
    ahead = moved(own, lambda i: i - 2 if i % 2 == 0 else i + 2)
    sib = swap(own)
    fold, wave, again = pl.pallas_call(
        table_kernel,
        out_shape=[
            jax.ShapeDtypeStruct((2 * LOW * GROUP, 2 * SUBS * GROUP), BF),
            jax.ShapeDtypeStruct((LOW, LANES, 2 * LANES), BF),
            jax.ShapeDtypeStruct(own.shape, BF),
        ],
        in_specs=[VM, ANY],
        out_specs=[VM] * 3,
        compiler_params=pltpu.CompilerParams(vmem_limit_bytes=16 << 20),
        cost_estimate=pl.CostEstimate(
            flops=1 << 30, bytes_accessed=2 << 20, transcendentals=0
        ),
    )(own, sib)
    back = moved(again, lambda i: i + 2 if i % 2 == 0 else i - 2)
    far = moved(ahead, lambda i: i - 1 if i % 2 == 0 else i + 1)
    near = [own, sib, ahead, swap(ahead), back, swap(back), far]
    near = pl.pallas_call(
        stage_kernel,
        out_shape=jax.ShapeDtypeStruct((win_dev, len(near) * ch_dev, rows, LANES), BF),
        in_specs=[ANY] * len(near),
        out_specs=VM,
        scratch_shapes=[pltpu.SemaphoreType.DMA((len(near), win_dev))],
        compiler_params=pltpu.CompilerParams(vmem_limit_bytes=32 << 20),
        cost_estimate=pl.CostEstimate(
            flops=1 << 30, bytes_accessed=8 << 20, transcendentals=0
        ),
    )(*near)

    ends = lax.dynamic_index_in_dim(pair_ends, me, 0, keepdims=False)
    first = ends[:, 0] % ch_dev
    away = (ends[:, 1] // ch_dev - me) * (1 - 2 * odd)
    place = jnp.zeros_like(away)
    for n, d in enumerate((0, 1, 2, -1, -2, 3, -3)):
        place = jnp.where(away == d, n, place)
    second = place * ch_dev + ends[:, 1] % ch_dev

    factor = jnp.where(jnp.arange(bins) == 0, 1.0, 2.0).astype(F32)
    weight = (passband * factor).reshape(SUBS, LANES)

    z = lax.axis_index("win")
    give = jax.ShapeDtypeStruct((5, half, wide, slots), BF)
    keep, up, down = pl.pallas_call(
        corr_kernel,
        out_shape=[jax.ShapeDtypeStruct((6, half, wide, slots), F32), give, give],
        in_specs=[SM] * 4 + [VM] * 4,
        out_specs=[VM] * 3,
        scratch_shapes=[
            pltpu.VMEM((2, GROUP * rows, 2 * LANES), BF),
            pltpu.VMEM((LOW, win_dev * slots, 2 * LANES), BF),
            pltpu.VMEM((LOW, LANES, win_dev * slots), F32),
        ],
        compiler_params=pltpu.CompilerParams(vmem_limit_bytes=32 << 20),
        cost_estimate=pl.CostEstimate(
            flops=8 << 30, bytes_accessed=8 << 20, transcendentals=0
        ),
    )(first, second, live_pairs, z.reshape(1), near, weight, fold, wave)

    def along(value, step):
        return lax.ppermute(
            value, "win", [(i, (i + step) % win_count) for i in range(win_count)]
        )

    piece = (2, half, wide, slots)
    mine, behind, ahead = pl.pallas_call(
        merge_kernel,
        out_shape=[jax.ShapeDtypeStruct(piece, d) for d in (F32, BF, BF)],
        in_specs=[VM] * 3,
        out_specs=[VM] * 3,
        compiler_params=pltpu.CompilerParams(vmem_limit_bytes=16 << 20),
    )(keep, along(up, 1), along(down, -1))
    return pl.pallas_call(
        final_kernel,
        out_shape=jax.ShapeDtypeStruct((slots, LOW * wide), F32),
        in_specs=[VM] * 3,
        out_specs=VM,
        scratch_shapes=[pltpu.VMEM((LOW * wide, slots), F32)],
    )(mine, along(behind, -3), along(ahead, 3))


def solution(mesh):
    placed = (P("win", "pair", None, None), P(), P(), P("pair"))
    return jax.shard_map(
        local, mesh=mesh, in_specs=placed, out_specs=P("pair", "win"), check_vma=False
    )
```

time: 386 us -> 85.3 us (0.22)
  the two profiles are of different devices: /device:TPU:6 before, /device:TPU:61 now
where the time goes in v2:
time: 85.3 us; the launch traced here: 85 us
  waiting for transfers between devices  50 us (59%)
  starting transfers between devices  18.5 us (22%)
  Pallas kernels  11.1 us (13%)
  local copies, waits for them, and re-layouts  3.93 us (5%)
    ppermute x3, waiting for transfers between devices, moved(): lax.ppermute(value, 'pair', [(a, b) for a, b in pairs if 0 <= b < count])  28.3 us
    ppermute x4, waiting for transfers between devices, along(): lax.ppermute(value, 'win', [(i, (i + step) % win_count) for i in range(wi...  21.7 us
    ppermute x3, starting transfers between devices, moved(): lax.ppermute(value, 'pair', [(a, b) for a, b in pairs if 0 <= b < count])  7.17 us
    ppermute x4, starting transfers between devices, along(): lax.ppermute(value, 'win', [(i, (i + step) % win_count) for i in range(wi...  6.58 us
    ppermute x3, starting transfers between devices, swap(): return lax.ppermute(value, 'pair', [(i, i ^ 1) for i in range(count)])  4.78 us
    pallas_call x1, Pallas kernels, local(): pl.pallas_call(corr_kernel, out_shape=[jax.ShapeDtypeStruct((6, half, wid...  4.28 us
    unnamed x14, local copies, waits for them, and re-layouts  3.92 us
    pallas_call x1, Pallas kernels, local(): pl.pallas_call(stage_kernel, out_shape=jax.ShapeDtypeStruct((win_dev, len...  2.48 us
  transfers between devices with their start and end apart: 10, of which 7 were waited for; matrix products, arithmetic and copies ran while one was open for 1% of the time, Pallas kernels for 2%

profile of v2, /device:TPU:61, one launch (start us, length us, event | category | flops | bytes accessed | tf_op | source)
XLA Modules:
  0.0 85.0 jit_solution(18090915234386239213)
XLA Ops:
  0.0 1.2 %copy-done.1 = bf16[2,64,2,2048]{3,2,1,0:T(2,128)(2,1)S(1)} copy-done((bf16[2,64,2,2048]{3,2,1,0:T(2,128)(2,1)S(1)}, bf16[2,64,2,2048]{3,2,1,0:T(2,128)(2,1)}, u32[]{:S(2)}) %copy-start.1) | copy-done | bytes 1048600
  1.2 0.9 %shard_map.46.own_ref.refs_0_ = bf16[2,64,32,128]{3,2,1,0:T(8,128)(2,1)S(1)} custom-call(bf16[2,64,32,128]{3,2,1,0:T(8,128)(2,1)S(1)} %bitcast.25), custom_call_target="tpu_custom_call" | custom-call | tf_op jit(solution)/shard_map/pallas_call | solution.py:228
  2.1 0.8 collective-permute-start
  2.9 2.5 %collective-permute-start.1 = (bf16[2,64,32,128]{3,2,1,0:T(8,128)(2,1)S(1)}, bf16[2,64,32,128]{3,2,1,0:T(8,128)(2,1)S(1)}, u32[]{:S(2)}, u32[]{:S(2)}) collective-permute-start(bf16[2,64,32,128]{3,2,1,0:T(8,128)(2,1)S(1)} %shard_map.46.own_ref.refs_0_), channel_id=1, source_target_pairs={{8,24},{16,0},{24,40},{32,16},{40,56},{48,32},{56,72},{64,48},{72,... | collective-permute-start | bytes 3145736 | tf_op jit(solution)/shard_map/ppermute | solution.py:27
  5.4 1.3 %shard_map.47 = (bf16[512,256]{1,0:T(8,128)(2,1)S(1)}, bf16[32,128,256]{2,1,0:T(8,128)(2,1)S(1)}, bf16[2,64,32,128]{3,2,1,0:T(8,128)(2,1)S(1)}) custom-call(bf16[2,64,32,128]{3,2,1,0:T(8,128)(2,1)S(1)} %shard_map.46.own_ref.refs_0_, bf16[2,64,32,128]{3,2,1,0:T(8,128)(2,1)S(1)} %collective-permute-done._.refs_1_), custom_call_target="tpu_custom_call" | custom-call | flops 1073741824 | bytes 2097152 | tf_op jit(solution)/shard_map/pallas_call | solution.py:239
  6.7 1.3 %copy-done.3 = bf16[32,128,256]{2,1,0:T(8,128)(2,1)} copy-done((bf16[32,128,256]{2,1,0:T(8,128)(2,1)}, bf16[32,128,256]{2,1,0:T(8,128)(2,1)S(1)}, u32[]{:S(2)}) %copy-start.3) | copy-done | bytes 2097176
  8.1 2.8 %collective-permute-start.3 = (bf16[2,64,32,128]{3,2,1,0:T(8,128)(2,1)S(1)}, bf16[2,64,32,128]{3,2,1,0:T(8,128)(2,1)}, u32[]{:S(2)}, u32[]{:S(2)}) collective-permute-start(bf16[2,64,32,128]{3,2,1,0:T(8,128)(2,1)S(1)} %get-tuple-element.14), channel_id=1, source_target_pairs={{0,16},{16,32},{24,8},{32,48},{40,24},{48,64},{56,40},{64,80},{72,... | collective-permute-start | bytes 3145736 | tf_op jit(solution)/shard_map/ppermute | solution.py:27
  10.9 13.3 %collective-permute-done.1.refs_2_ = bf16[2,64,32,128]{3,2,1,0:T(8,128)(2,1)S(1)} collective-permute-done((bf16[2,64,32,128]{3,2,1,0:T(8,128)(2,1)S(1)}, bf16[2,64,32,128]{3,2,1,0:T(8,128)(2,1)S(1)}, u32[]{:S(2)}, u32[]{:S(2)}) %collective-permute-start.1) | collective-permute-done | bytes 1048608 | tf_op jit(solution)/shard_map/ppermute | solution.py:27
  24.2 4.0 %collective-permute-start.2 = (bf16[2,64,32,128]{3,2,1,0:T(8,128)(2,1)S(1)}, bf16[2,64,32,128]{3,2,1,0:T(8,128)(2,1)}, u32[]{:S(2)}, u32[]{:S(2)}) collective-permute-start(bf16[2,64,32,128]{3,2,1,0:T(8,128)(2,1)S(1)} %collective-permute-done.1.refs_2_), channel_id=1, source_target_pairs={{0,8},{8,0},{16,24},{24,16},{32,40},{40,32},{48,56},{56,48},{64,72... | collective-permute-start | bytes 3145736 | tf_op jit(solution)/shard_map/ppermute | solution.py:32
  28.2 1.9 %collective-permute-start.5 = (bf16[2,64,32,128]{3,2,1,0:T(8,128)(2,1)S(1)}, bf16[2,64,32,128]{3,2,1,0:T(8,128)(2,1)}, u32[]{:S(2)}, u32[]{:S(2)}) collective-permute-start(bf16[2,64,32,128]{3,2,1,0:T(8,128)(2,1)S(1)} %collective-permute-done.1.refs_2_), channel_id=1, source_target_pairs={{8,16},{16,8},{24,32},{32,24},{40,48},{48,40},{56,64},{64,56},{72,... | collective-permute-start | bytes 3145736 | tf_op jit(solution)/shard_map/ppermute | solution.py:27
  30.1 2.2 %collective-permute-done.3.refs_4_ = bf16[2,64,32,128]{3,2,1,0:T(8,128)(2,1)} collective-permute-done((bf16[2,64,32,128]{3,2,1,0:T(8,128)(2,1)S(1)}, bf16[2,64,32,128]{3,2,1,0:T(8,128)(2,1)}, u32[]{:S(2)}, u32[]{:S(2)}) %collective-permute-start.3) | collective-permute-done | bytes 1048608 | tf_op jit(solution)/shard_map/ppermute | solution.py:27
  33.1 0.7 multiply_bitcast_fusion.weight_ref
  33.8 12.7 %collective-permute-done.5.refs_6_ = bf16[2,64,32,128]{3,2,1,0:T(8,128)(2,1)} collective-permute-done((bf16[2,64,32,128]{3,2,1,0:T(8,128)(2,1)S(1)}, bf16[2,64,32,128]{3,2,1,0:T(8,128)(2,1)}, u32[]{:S(2)}, u32[]{:S(2)}) %collective-permute-start.5) | collective-permute-done | bytes 1048608 | tf_op jit(solution)/shard_map/ppermute | solution.py:27
  46.5 2.5 %shard_map.48.near_ref = bf16[2,448,32,128]{3,2,1,0:T(8,128)(2,1)S(1)} custom-call(bf16[2,64,32,128]{3,2,1,0:T(8,128)(2,1)S(1)} %shard_map.46.own_ref.refs_0_, bf16[2,64,32,128]{3,2,1,0:T(8,128)(2,1)S(1)} %collective-permute-done._.refs_1_, bf16[2,64,32,128]{3,2,1,0:T(8,128)(2,1)S(1)} %collective-permute-done.1.refs_2_, ...), custom_call_target="tpu_custom_call" | custom-call | flops 1073741824 | bytes 8388608 | tf_op jit(solution)/shard_map/pallas_call | solution.py:256
  49.0 4.3 %shard_map.49 = (f32[6,16,16,128]{3,2,1,0:T(8,128)S(1)}, bf16[5,16,16,128]{3,2,1,0:T(8,128)(2,1)S(1)}, bf16[5,16,16,128]{3,2,1,0:T(8,128)(2,1)S(1)}) custom-call(s32[128]{0:T(128)S(1)} %get-tuple-element.24.first_ref, s32[128]{0:T(128)S(1)} %get-tuple-element.23.second_ref, s32[1]{0:T(128)S(6)} %copy.6.live_ref, s32[1]{0:T(128)} %bitcast.3.z_ref, ...), custom_call_target="tpu_custom_call" | custom-call | flops 8589934592 | bytes 8388608 | tf_op jit(solution)/shard_map/pallas_call | solution.py:281
  53.3 1.7 %collective-permute-start.6 = (bf16[5,16,16,128]{3,2,1,0:T(8,128)(2,1)S(1)}, bf16[5,16,16,128]{3,2,1,0:T(8,128)(2,1)S(1)}, u32[]{:S(2)}, u32[]{:S(2)}) collective-permute-start(bf16[5,16,16,128]{3,2,1,0:T(8,128)(2,1)S(1)} %get-tuple-element.18), channel_id=1, source_target_pairs={{0,1},{1,2},{2,3},{3,4},{4,5},{5,6},{6,7},{7,0},{8,9},{9,10},{10,1... | collective-permute-start | bytes 983048 | tf_op jit(solution)/shard_map/ppermute | solution.py:298
  55.0 6.4 %collective-permute-done.6.left_ref = bf16[5,16,16,128]{3,2,1,0:T(8,128)(2,1)S(1)} collective-permute-done((bf16[5,16,16,128]{3,2,1,0:T(8,128)(2,1)S(1)}, bf16[5,16,16,128]{3,2,1,0:T(8,128)(2,1)S(1)}, u32[]{:S(2)}, u32[]{:S(2)}) %collective-permute-start.6) | collective-permute-done | bytes 327712 | tf_op jit(solution)/shard_map/ppermute | solution.py:298
  61.5 1.6 %collective-permute-done.7.right_ref = bf16[5,16,16,128]{3,2,1,0:T(8,128)(2,1)S(1)} collective-permute-done((bf16[5,16,16,128]{3,2,1,0:T(8,128)(2,1)S(1)}, bf16[5,16,16,128]{3,2,1,0:T(8,128)(2,1)S(1)}, u32[]{:S(2)}, u32[]{:S(2)}) %collective-permute-start.7) | collective-permute-done | bytes 327712 | tf_op jit(solution)/shard_map/ppermute | solution.py:298
  63.2 0.7 copy-done.2
  63.9 4.7 %collective-permute-start.8 = (bf16[2,16,16,128]{3,2,1,0:T(8,128)(2,1)S(1)}, bf16[2,16,16,128]{3,2,1,0:T(8,128)(2,1)S(1)}, u32[]{:S(2)}, u32[]{:S(2)}) collective-permute-start(bf16[2,16,16,128]{3,2,1,0:T(8,128)(2,1)S(1)} %get-tuple-element.21), channel_id=1, source_target_pairs={{0,5},{1,6},{2,7},{3,0},{4,1},{5,2},{6,3},{7,4},{8,13},{9,14},{10,... | collective-permute-start | bytes 393224 | tf_op jit(solution)/shard_map/ppermute | solution.py:298
  68.8 8.5 %collective-permute-done.8.refs_0_ = bf16[2,16,16,128]{3,2,1,0:T(8,128)(2,1)S(1)} collective-permute-done((bf16[2,16,16,128]{3,2,1,0:T(8,128)(2,1)S(1)}, bf16[2,16,16,128]{3,2,1,0:T(8,128)(2,1)S(1)}, u32[]{:S(2)}, u32[]{:S(2)}) %collective-permute-start.8) | collective-permute-done | bytes 131104 | tf_op jit(solution)/shard_map/ppermute | solution.py:298
  77.3 5.2 %collective-permute-done.9.refs_1_ = bf16[2,16,16,128]{3,2,1,0:T(8,128)(2,1)S(1)} collective-permute-done((bf16[2,16,16,128]{3,2,1,0:T(8,128)(2,1)S(1)}, bf16[2,16,16,128]{3,2,1,0:T(8,128)(2,1)S(1)}, u32[]{:S(2)}, u32[]{:S(2)}) %collective-permute-start.9) | collective-permute-done | bytes 131104 | tf_op jit(solution)/shard_map/ppermute | solution.py:298
  82.4 0.6 copy-done.6
  83.1 1.9 %shard_map.51 = f32[128,512]{1,0:T(8,128)} custom-call(f32[2,16,16,128]{3,2,1,0:T(8,128)} %copy-done.2, bf16[2,16,16,128]{3,2,1,0:T(8,128)(2,1)} %copy-done.5, bf16[2,16,16,128]{3,2,1,0:T(8,128)(2,1)} %copy-done.6), custom_call_target="tpu_custom_call" | custom-call | tf_op jit(solution)/shard_map/pallas_call | solution.py:310
  (19 shorter events, 0.4 us)
Async XLA Ops:
  0.0 33.0 %copy-start = (s32[32,128,2]{1,2,0:T(2,128)S(1)}, s32[32,128,2]{1,2,0:T(2,128)}, u32[]{:S(2)}) copy-start(s32[32,128,2]{1,2,0:T(2,128)} %param.6) | copy-start | bytes 98308
  0.0 1.2 %copy-start.1 = (bf16[2,64,2,2048]{3,2,1,0:T(2,128)(2,1)S(1)}, bf16[2,64,2,2048]{3,2,1,0:T(2,128)(2,1)}, u32[]{:S(2)}) copy-start(bf16[2,64,2,2048]{3,2,1,0:T(2,128)(2,1)} %param.4) | copy-start | bytes 3145732
  2.1 3.2 %collective-permute-start = (bf16[2,64,32,128]{3,2,1,0:T(8,128)(2,1)S(1)}, bf16[2,64,32,128]{3,2,1,0:T(8,128)(2,1)S(1)}, u32[]{:S(2)}, u32[]{:S(2)}) collective-permute-start(bf16[2,64,32,128]{3,2,1,0:T(8,128)(2,1)S(1)} %shard_map.46.own_ref.refs_0_), channel_id=1, source_target_pairs={{0,8},{8,0},{16,24},{24,16},{32,40},{40,32},{48,56},{56,48},{64,72... | collective-permute-start | bytes 3145736 | tf_op jit(solution)/shard_map/ppermute | solution.py:32
  2.9 21.3 %collective-permute-start.1 = (bf16[2,64,32,128]{3,2,1,0:T(8,128)(2,1)S(1)}, bf16[2,64,32,128]{3,2,1,0:T(8,128)(2,1)S(1)}, u32[]{:S(2)}, u32[]{:S(2)}) collective-permute-start(bf16[2,64,32,128]{3,2,1,0:T(8,128)(2,1)S(1)} %shard_map.46.own_ref.refs_0_), channel_id=1, source_target_pairs={{8,24},{16,0},{24,40},{32,16},{40,56},{48,32},{56,72},{64,48},{72,... | collective-permute-start | bytes 3145736 | tf_op jit(solution)/shard_map/ppermute | solution.py:27
  6.7 1.3 %copy-start.3 = (bf16[32,128,256]{2,1,0:T(8,128)(2,1)}, bf16[32,128,256]{2,1,0:T(8,128)(2,1)S(1)}, u32[]{:S(2)}) copy-start(bf16[32,128,256]{2,1,0:T(8,128)(2,1)S(1)} %get-tuple-element.16.wave_ref) | copy-start | bytes 6291460
  8.1 24.3 %collective-permute-start.3 = (bf16[2,64,32,128]{3,2,1,0:T(8,128)(2,1)S(1)}, bf16[2,64,32,128]{3,2,1,0:T(8,128)(2,1)}, u32[]{:S(2)}, u32[]{:S(2)}) collective-permute-start(bf16[2,64,32,128]{3,2,1,0:T(8,128)(2,1)S(1)} %get-tuple-element.14), channel_id=1, source_target_pairs={{0,16},{16,32},{24,8},{32,48},{40,24},{48,64},{56,40},{64,80},{72,... | collective-permute-start | bytes 3145736 | tf_op jit(solution)/shard_map/ppermute | solution.py:27
  24.2 9.6 %collective-permute-start.2 = (bf16[2,64,32,128]{3,2,1,0:T(8,128)(2,1)S(1)}, bf16[2,64,32,128]{3,2,1,0:T(8,128)(2,1)}, u32[]{:S(2)}, u32[]{:S(2)}) collective-permute-start(bf16[2,64,32,128]{3,2,1,0:T(8,128)(2,1)S(1)} %collective-permute-done.1.refs_2_), channel_id=1, source_target_pairs={{0,8},{8,0},{16,24},{24,16},{32,40},{40,32},{48,56},{56,48},{64,72... | collective-permute-start | bytes 3145736 | tf_op jit(solution)/shard_map/ppermute | solution.py:32
  28.2 18.3 %collective-permute-start.5 = (bf16[2,64,32,128]{3,2,1,0:T(8,128)(2,1)S(1)}, bf16[2,64,32,128]{3,2,1,0:T(8,128)(2,1)}, u32[]{:S(2)}, u32[]{:S(2)}) collective-permute-start(bf16[2,64,32,128]{3,2,1,0:T(8,128)(2,1)S(1)} %collective-permute-done.1.refs_2_), channel_id=1, source_target_pairs={{8,16},{16,8},{24,32},{32,24},{40,48},{48,40},{56,64},{64,56},{72,... | collective-permute-start | bytes 3145736 | tf_op jit(solution)/shard_map/ppermute | solution.py:27
  32.4 14.2 %collective-permute-start.4 = (bf16[2,64,32,128]{3,2,1,0:T(8,128)(2,1)}, bf16[2,64,32,128]{3,2,1,0:T(8,128)(2,1)}, u32[]{:S(2)}, u32[]{:S(2)}) collective-permute-start(bf16[2,64,32,128]{3,2,1,0:T(8,128)(2,1)} %collective-permute-done.3.refs_4_), channel_id=1, source_target_pairs={{0,8},{8,0},{16,24},{24,16},{32,40},{40,32},{48,56},{56,48},{64,72... | collective-permute-start | bytes 3145736 | tf_op jit(solution)/shard_map/ppermute | solution.py:32
  33.8 15.2 %copy-start.4 = (bf16[32,128,256]{2,1,0:T(8,128)(2,1)S(1)}, bf16[32,128,256]{2,1,0:T(8,128)(2,1)}, u32[]{:S(2)}) copy-start(bf16[32,128,256]{2,1,0:T(8,128)(2,1)} %copy-done.3) | copy-start | bytes 6291460
  53.3 8.2 %collective-permute-start.6 = (bf16[5,16,16,128]{3,2,1,0:T(8,128)(2,1)S(1)}, bf16[5,16,16,128]{3,2,1,0:T(8,128)(2,1)S(1)}, u32[]{:S(2)}, u32[]{:S(2)}) collective-permute-start(bf16[5,16,16,128]{3,2,1,0:T(8,128)(2,1)S(1)} %get-tuple-element.18), channel_id=1, source_target_pairs={{0,1},{1,2},{2,3},{3,4},{4,5},{5,6},{6,7},{7,0},{8,9},{9,10},{10,1... | collective-permute-start | bytes 983048 | tf_op jit(solution)/shard_map/ppermute | solution.py:298
  55.0 8.1 %collective-permute-start.7 = (bf16[5,16,16,128]{3,2,1,0:T(8,128)(2,1)S(1)}, bf16[5,16,16,128]{3,2,1,0:T(8,128)(2,1)S(1)}, u32[]{:S(2)}, u32[]{:S(2)}) collective-permute-start(bf16[5,16,16,128]{3,2,1,0:T(8,128)(2,1)S(1)} %get-tuple-element.19), channel_id=1, source_target_pairs={{0,7},{1,0},{2,1},{3,2},{4,3},{5,4},{6,5},{7,6},{8,15},{9,8},{10,9... | collective-permute-start | bytes 983048 | tf_op jit(solution)/shard_map/ppermute | solution.py:298
  63.2 0.7 copy-start.2
  63.9 13.3 %collective-permute-start.8 = (bf16[2,16,16,128]{3,2,1,0:T(8,128)(2,1)S(1)}, bf16[2,16,16,128]{3,2,1,0:T(8,128)(2,1)S(1)}, u32[]{:S(2)}, u32[]{:S(2)}) collective-permute-start(bf16[2,16,16,128]{3,2,1,0:T(8,128)(2,1)S(1)} %get-tuple-element.21), channel_id=1, source_target_pairs={{0,5},{1,6},{2,7},{3,0},{4,1},{5,2},{6,3},{7,4},{8,13},{9,14},{10,... | collective-permute-start | bytes 393224 | tf_op jit(solution)/shard_map/ppermute | solution.py:298
  68.6 13.8 %collective-permute-start.9 = (bf16[2,16,16,128]{3,2,1,0:T(8,128)(2,1)S(1)}, bf16[2,16,16,128]{3,2,1,0:T(8,128)(2,1)S(1)}, u32[]{:S(2)}, u32[]{:S(2)}) collective-permute-start(bf16[2,16,16,128]{3,2,1,0:T(8,128)(2,1)S(1)} %get-tuple-element.22), channel_id=1, source_target_pairs={{0,3},{1,4},{2,5},{3,6},{4,7},{5,0},{6,1},{7,2},{8,11},{9,12},{10,... | collective-permute-start | bytes 393224 | tf_op jit(solution)/shard_map/ppermute | solution.py:298
  77.3 5.2 %copy-start.5 = (bf16[2,16,16,128]{3,2,1,0:T(8,128)(2,1)}, bf16[2,16,16,128]{3,2,1,0:T(8,128)(2,1)S(1)}, u32[]{:S(2)}) copy-start(bf16[2,16,16,128]{3,2,1,0:T(8,128)(2,1)S(1)} %collective-permute-done.8.refs_0_) | copy-start | bytes 393220
  82.4 0.7 copy-start.6

commit v3 on v2

--- a/solution.py
+++ b/solution.py
@@ -18,6 +18,7 @@
 LANES = 128
 SUBS = 16
 LOW = 2 * SUBS
+FAR_ROWS = 40
 GROUP = 8
 
 
@@ -32,39 +33,64 @@
     return lax.ppermute(value, "pair", [(i, i ^ 1) for i in range(count)])
 
 
-def whiten_kernel(x_ref, out_ref):
-    rows = 2 * SUBS
+def whiten_into(ref, out_refs, first=0):
+    windows, channels, rows, _ = ref.shape
     size = GROUP * rows
     r = lax.broadcasted_iota(jnp.int32, (size, size), 0)
     c = lax.broadcasted_iota(jnp.int32, (size, size), 1)
     source = (r // rows) * rows + 2 * (r % SUBS) + (r // SUBS) % 2
     perm = jnp.where(c == source, 1.0, 0.0).astype(BF)
 
-    for window in range(x_ref.shape[0]):
-        for g in range(x_ref.shape[1] // GROUP):
-            at = pl.ds(g * GROUP, GROUP)
-            values = x_ref[window, at].astype(F32)
+    for v in range(windows):
+        for g in range(channels // GROUP):
+            values = ref[v, pl.ds(g * GROUP, GROUP)].astype(F32)
             power = jnp.sum(jnp.sum(values * values, axis=1), axis=1, keepdims=True)
             power = power * (1.0 / (rows * LANES))
             scaled = (values * lax.rsqrt(power + 1e-06)[:, :, None]).astype(BF)
             ordered = jnp.dot(perm, scaled.reshape(size, LANES), preferred_element_type=F32)
-            out_ref[window, at] = ordered.astype(BF).reshape(GROUP, rows, LANES)
-
-
-def stage_kernel(*refs):
-    *near_refs, out_ref, sem = refs
-    channels = near_refs[0].shape[1]
-    copies = [
-        pltpu.make_async_copy(
-            ref.at[v], out_ref.at[v, pl.ds(n * channels, channels)], sem.at[n, v]
-        )
-        for n, ref in enumerate(near_refs)
-        for v in range(ref.shape[0])
-    ]
-    for copy in copies:
-        copy.start()
-    for copy in copies:
-        copy.wait()
+            at = pl.ds(first + g * GROUP, GROUP)
+            out_refs[v][at] = ordered.astype(BF).reshape(GROUP, rows, LANES)
+
+
+def windows_of(ref):
+    return [ref.at[v] for v in range(ref.shape[0])]
+
+
+def own_kernel(own_ref, _, again_ref, out_ref):
+    again_ref[...] = own_ref[...]
+    whiten_into(own_ref, windows_of(out_ref))
+
+
+def gather_kernel(own_ref, sib_ref, *refs):
+    windows = own_ref.shape[0]
+    *in_refs, raw_ref, _, near_ref = refs[:-windows]
+    out_refs = refs[-windows:]
+    whiten_into(raw_ref, out_refs)
+    for v in range(windows):
+        at = 0
+        for ref in (own_ref.at[v], sib_ref.at[v], *in_refs[v::windows], out_refs[v]):
+            near_ref[v, pl.ds(at, ref.shape[0])] = ref[...]
+            at += ref.shape[0]
+
+
+def forward_kernel(order_ref, raw_ref, _, *refs):
+    *out_refs, head_ref, tail_ref = refs
+    whiten_into(raw_ref, out_refs)
+    head, tail = head_ref.shape[1], tail_ref.shape[1]
+    for v, out_ref in enumerate(out_refs):
+        for p in range(head):
+            head_ref[v, p] = out_ref[order_ref[p]]
+        for p in range(tail):
+            tail_ref[v, p] = out_ref[order_ref[head + p]]
+
+
+def late_kernel(*refs):
+    *swapped_refs, head_ref, tail_ref, out_ref = refs
+    for v in range(out_ref.shape[0]):
+        at = 0
+        for ref in (swapped_refs[v], head_ref.at[v], tail_ref.at[v]):
+            out_ref[v, pl.ds(at, ref.shape[0])] = ref[...]
+            at += ref.shape[0]
 
 
 def corr_kernel(
@@ -73,6 +99,7 @@
     live_ref,
     z_ref,
     near_ref,
+    late_ref,
     weight_ref,
     fold_ref,
     wave_ref,
@@ -83,7 +110,7 @@
     mid,
     corr,
 ):
-    windows = near_ref.shape[0]
+    windows, early = near_ref.shape[:2]
     slots = mid.shape[1] // windows
     weight = weight_ref[...]
     alive = lax.broadcasted_iota(jnp.int32, (1, slots), 1) < live_ref[0]
@@ -97,7 +124,12 @@
                 for q in range(GROUP):
                     p = g * 2 * GROUP + half * GROUP + q
                     a = near_ref[v, first_ref[p]].astype(F32)
-                    b = near_ref[v, second_ref[p]].astype(F32)
+                    at = second_ref[p]
+                    b = jnp.where(
+                        at < early,
+                        near_ref[v, jnp.minimum(at, early - 1)],
+                        late_ref[v, jnp.maximum(at - early, 0)],
+                    ).astype(F32)
                     ar, ai, br, bi = a[:SUBS], a[SUBS:], b[:SUBS], b[SUBS:]
                     re = (ar * br + ai * bi) * weight
                     im = (ai * br - ar * bi) * weight
@@ -182,14 +214,14 @@
         out_ref[:, pl.ds(g * LANES, LANES)] = jnp.concatenate(rows, axis=0).T
 
 
-def table_kernel(own_ref, _, fold_ref, wave_ref, again_ref):
+def table_kernel(sib_ref, _, fold_ref, wave_ref, sib_out_ref):
     def turns(rows, cols, period):
         r = lax.broadcasted_iota(jnp.int32, (rows, cols), 0)
         c = lax.broadcasted_iota(jnp.int32, (rows, cols), 1)
         angle = lax.rem(r * c, period).astype(F32) * (2.0 * math.pi / period)
         return jnp.cos(angle), jnp.sin(angle)
 
-    again_ref[...] = own_ref[...]
+    whiten_into(sib_ref, windows_of(sib_out_ref))
 
     cos, sin = turns(LOW, SUBS, LOW)
     base = jnp.concatenate(
@@ -216,6 +248,18 @@
         wave_ref[t2, :, pl.ds(LANES, LANES)] = (-s * high_cos - c * high_sin).astype(BF)
 
 
+def far_order(pair_ends, ch_dev):
+    block = jnp.arange(pair_ends.shape[0], dtype=jnp.int32)[:, None]
+    away = (pair_ends[:, :, 1] // ch_dev - block) * (1 - 2 * (block % 2))
+    named = jnp.where(away == -HALF, pair_ends[:, :, 1] % ch_dev, -1)
+    channel = jnp.arange(ch_dev, dtype=jnp.int32)
+    need = jnp.any(named[:, :, None] == channel, axis=1)
+    count = jnp.sum(need.astype(jnp.int32), axis=1, keepdims=True)
+    before = (channel[None, :] < channel[:, None])[None]
+    rank = jnp.sum((before & need[:, None, :]).astype(jnp.int32), axis=2)
+    return jnp.where(need, rank, count + channel - rank), count
+
+
 def local(spectra, passband, pair_ends, live_pairs):
     win_count = lax.axis_size("win")
     win_dev, ch_dev, _, bins = spectra.shape
@@ -225,23 +269,32 @@
     half = LOW // 2
     x = spectra.reshape(win_dev, ch_dev, 2, SUBS, LANES).transpose(0, 1, 3, 2, 4)
     x = x.reshape(win_dev, ch_dev, rows, LANES)
-    own = pl.pallas_call(
-        whiten_kernel,
-        out_shape=jax.ShapeDtypeStruct(x.shape, BF),
-        in_specs=[VM],
-        out_specs=VM,
-        compiler_params=pltpu.CompilerParams(vmem_limit_bytes=16 << 20),
-    )(x)
     me = lax.axis_index("pair")
     odd = me % 2
-    ahead = moved(own, lambda i: i - 2 if i % 2 == 0 else i + 2)
-    sib = swap(own)
-    fold, wave, again = pl.pallas_call(
+    place, named = far_order(pair_ends, ch_dev)
+    target = jnp.clip(me - 1 + 2 * odd, 0, pair_ends.shape[0] - 1)
+    channel = jnp.arange(ch_dev, dtype=jnp.int32)
+    order = lax.dynamic_index_in_dim(place, target, 0, keepdims=False)
+    order = jnp.sum(jnp.where(order[None, :] == channel[:, None], channel[None, :], 0), axis=1)
+
+    ahead = moved(x, lambda i: i - 2 if i % 2 == 0 else i + 2)
+    sib = swap(x)
+    again, own = pl.pallas_call(
+        own_kernel,
+        out_shape=[jax.ShapeDtypeStruct(x.shape, BF)] * 2,
+        in_specs=[VM, SM],
+        out_specs=[VM] * 2,
+        compiler_params=pltpu.CompilerParams(vmem_limit_bytes=16 << 20),
+        cost_estimate=pl.CostEstimate(
+            flops=1 << 30, bytes_accessed=2 << 20, transcendentals=0
+        ),
+    )(x, order)
+    fold, wave, sib = pl.pallas_call(
         table_kernel,
         out_shape=[
             jax.ShapeDtypeStruct((2 * LOW * GROUP, 2 * SUBS * GROUP), BF),
             jax.ShapeDtypeStruct((LOW, LANES, 2 * LANES), BF),
-            jax.ShapeDtypeStruct(own.shape, BF),
+            jax.ShapeDtypeStruct(x.shape, BF),
         ],
         in_specs=[VM, ANY],
         out_specs=[VM] * 3,
@@ -249,29 +302,58 @@
         cost_estimate=pl.CostEstimate(
             flops=1 << 30, bytes_accessed=2 << 20, transcendentals=0
         ),
-    )(own, sib)
+    )(sib, own)
     back = moved(again, lambda i: i + 2 if i % 2 == 0 else i - 2)
-    far = moved(ahead, lambda i: i - 1 if i % 2 == 0 else i + 1)
-    near = [own, sib, ahead, swap(ahead), back, swap(back), far]
-    near = pl.pallas_call(
-        stage_kernel,
-        out_shape=jax.ShapeDtypeStruct((win_dev, len(near) * ch_dev, rows, LANES), BF),
-        in_specs=[ANY] * len(near),
+    *ahead, head, tail = pl.pallas_call(
+        forward_kernel,
+        out_shape=[jax.ShapeDtypeStruct(x.shape[1:], BF)] * win_dev
+        + [
+            jax.ShapeDtypeStruct((win_dev, FAR_ROWS, rows, LANES), BF),
+            jax.ShapeDtypeStruct((win_dev, ch_dev - FAR_ROWS, rows, LANES), BF),
+        ],
+        in_specs=[SM, VM, ANY],
+        out_specs=[VM] * (win_dev + 2),
+        compiler_params=pltpu.CompilerParams(vmem_limit_bytes=16 << 20),
+        cost_estimate=pl.CostEstimate(flops=0, bytes_accessed=0, transcendentals=0),
+    )(order, ahead, fold)
+
+    def outward(value):
+        return moved(value, lambda i: i - 1 if i % 2 == 0 else i + 1)
+
+    head = outward(head)
+    tail = lax.cond(jnp.max(named) > FAR_ROWS, outward, jnp.zeros_like, tail)
+    near, *back = pl.pallas_call(
+        gather_kernel,
+        out_shape=[
+            jax.ShapeDtypeStruct((win_dev, 5 * ch_dev, rows, LANES), BF),
+        ]
+        + [jax.ShapeDtypeStruct(x.shape[1:], BF)] * win_dev,
+        in_specs=[VM] * (3 + 2 * win_dev) + [ANY],
+        out_specs=[VM] * (1 + win_dev),
+        compiler_params=pltpu.CompilerParams(vmem_limit_bytes=24 << 20),
+        cost_estimate=pl.CostEstimate(flops=0, bytes_accessed=0, transcendentals=0),
+    )(own, sib, *ahead, *[swap(a) for a in ahead], back, tail)
+    late = pl.pallas_call(
+        late_kernel,
+        out_shape=jax.ShapeDtypeStruct((win_dev, 2 * ch_dev, rows, LANES), BF),
+        in_specs=[VM] * (win_dev + 2),
         out_specs=VM,
-        scratch_shapes=[pltpu.SemaphoreType.DMA((len(near), win_dev))],
-        compiler_params=pltpu.CompilerParams(vmem_limit_bytes=32 << 20),
+        compiler_params=pltpu.CompilerParams(vmem_limit_bytes=16 << 20),
         cost_estimate=pl.CostEstimate(
-            flops=1 << 30, bytes_accessed=8 << 20, transcendentals=0
+            flops=20 << 30, bytes_accessed=0, transcendentals=0
         ),
-    )(*near)
+    )(*[swap(b) for b in back], head, tail)
 
     ends = lax.dynamic_index_in_dim(pair_ends, me, 0, keepdims=False)
     first = ends[:, 0] % ch_dev
     away = (ends[:, 1] // ch_dev - me) * (1 - 2 * odd)
-    place = jnp.zeros_like(away)
+    row = ends[:, 1] % ch_dev
+    mine = lax.dynamic_index_in_dim(place, me, 0, keepdims=False)
+    mine = jnp.sum(jnp.where(row[:, None] == channel[None, :], mine[None, :], 0), axis=1)
+    row = jnp.where(away == -HALF, mine, row)
+    second = jnp.zeros_like(away)
     for n, d in enumerate((0, 1, 2, -1, -2, 3, -3)):
-        place = jnp.where(away == d, n, place)
-    second = place * ch_dev + ends[:, 1] % ch_dev
+        second = jnp.where(away == d, n * ch_dev + row, second)
 
     factor = jnp.where(jnp.arange(bins) == 0, 1.0, 2.0).astype(F32)
     weight = (passband * factor).reshape(SUBS, LANES)
@@ -281,7 +363,7 @@
     keep, up, down = pl.pallas_call(
         corr_kernel,
         out_shape=[jax.ShapeDtypeStruct((6, half, wide, slots), F32), give, give],
-        in_specs=[SM] * 4 + [VM] * 4,
+        in_specs=[SM] * 4 + [VM] * 5,
         out_specs=[VM] * 3,
         scratch_shapes=[
             pltpu.VMEM((2, GROUP * rows, 2 * LANES), BF),
@@ -292,7 +374,7 @@
         cost_estimate=pl.CostEstimate(
             flops=8 << 30, bytes_accessed=8 << 20, transcendentals=0
         ),
-    )(first, second, live_pairs, z.reshape(1), near, weight, fold, wave)
+    )(first, second, live_pairs, z.reshape(1), near, late, weight, fold, wave)
 
     def along(value, step):
         return lax.ppermute(

time: 85.3 us -> 78.7 us (0.923)
  the two profiles are of different devices: /device:TPU:61 before, /device:TPU:6 now
where the time goes in v3:
time: 78.7 us; the launch traced here: 77.2 us
  starting transfers between devices  24.8 us (32%)
  waiting for transfers between devices  21.4 us (27%)
  Pallas kernels  18.7 us (24%)
  local copies, waits for them, and re-layouts  7.59 us (10%)
  other arithmetic  3.25 us (4%)
  between operations  1.49 us (2%)
    ppermute x4, waiting for transfers between devices, along(): lax.ppermute(value, 'win', [(i, (i + step) % win_count) for i in range(wi...  17.6 us
    ppermute x3, starting transfers between devices, moved(): lax.ppermute(value, 'pair', [(a, b) for a, b in pairs if 0 <= b < count])  13.1 us
    ppermute x4, starting transfers between devices, along(): lax.ppermute(value, 'win', [(i, (i + step) % win_count) for i in range(wi...  10.6 us
    unnamed x18, local copies, waits for them, and re-layouts  6.1 us
    pallas_call x1, Pallas kernels, local(): pl.pallas_call(corr_kernel, out_shape=[jax.ShapeDtypeStruct((6, half, wid...  4.36 us
    pallas_call x1, Pallas kernels, local(): pl.pallas_call(table_kernel, out_shape=[jax.ShapeDtypeStruct((2 * LOW * G...  3.32 us
    ppermute x3, waiting for transfers between devices, moved(): lax.ppermute(value, 'pair', [(a, b) for a, b in pairs if 0 <= b < count])  3.02 us
    pallas_call x1, Pallas kernels, local(): pl.pallas_call(gather_kernel, out_shape=[jax.ShapeDtypeStruct((win_dev, 5...  2.64 us
  transfers between devices with their start and end apart: 12, of which 7 were waited for; matrix products, arithmetic and copies ran while one was open for 6% of the time, Pallas kernels for 14%

profile of v3, /device:TPU:6, one launch (start us, length us, event | category | flops | bytes accessed | tf_op | source)
XLA Modules:
  0.0 77.2 jit_solution(14735365598673170484)
XLA Ops:
  0.0 5.2 %collective-permute-start.2 = (bf16[2,64,32,128]{3,2,1,0:T(8,128)(2,1)}, bf16[2,64,32,128]{3,2,1,0:T(8,128)(2,1)S(1)}, u32[]{:S(2)}, u32[]{:S(2)}) collective-permute-start(bf16[2,64,32,128]{3,2,1,0:T(8,128)(2,1)} %bitcast.33), channel_id=1, source_target_pairs={{8,24},{16,0},{24,40},{32,16},{40,56},{48,32},{56,72},{64,48},{72,... | collective-permute-start | bytes 3145736 | tf_op jit(solution)/shard_map/ppermute | solution.py:28
  5.2 0.9 %compare_select_fusion = s32[32,128,1]{1,2,0:T(1,128)S(1)} fusion(s32[32,128,2]{1,2,0:T(2,128)} %param.8, s32[32]{0:T(128)S(1)} %fusion.5), kind=kLoop, calls=%fused_computation.4 | loop fusion | flops 94208 | bytes 32896 | tf_op jit(solution)/shard_map/jit(_where)/select_n | solution.py:254
  7.7 1.2 %copy-done.3 = bf16[2,64,2,2048]{3,2,1,0:T(2,128)(2,1)S(1)} copy-done((bf16[2,64,2,2048]{3,2,1,0:T(2,128)(2,1)S(1)}, bf16[2,64,2,2048]{3,2,1,0:T(2,128)(2,1)}, u32[]{:S(2)}) %copy-start.3) | copy-done | bytes 1048600
  9.0 2.4 %shard_map.46 = (bf16[2,64,32,128]{3,2,1,0:T(8,128)(2,1)}, bf16[2,64,32,128]{3,2,1,0:T(8,128)(2,1)S(1)}) custom-call(bf16[2,64,32,128]{3,2,1,0:T(8,128)(2,1)S(1)} %bitcast.34, s32[64]{0:T(128)S(1)} %select_reduce_fusion._.order_ref), custom_call_target="tpu_custom_call" | custom-call | flops 1073741824 | bytes 2097152 | tf_op jit(solution)/shard_map/pallas_call | solution.py:282
  11.4 1.9 %collective-permute-start.5 = (bf16[2,64,32,128]{3,2,1,0:T(8,128)(2,1)}, bf16[2,64,32,128]{3,2,1,0:T(8,128)(2,1)S(1)}, u32[]{:S(2)}, u32[]{:S(2)}) collective-permute-start(bf16[2,64,32,128]{3,2,1,0:T(8,128)(2,1)} %get-tuple-element.32), channel_id=1, source_target_pairs={{0,16},{16,32},{24,8},{32,48},{40,24},{48,64},{56,40},{64,80},{72,... | collective-permute-start | bytes 3145736 | tf_op jit(solution)/shard_map/ppermute | solution.py:28
  13.3 3.3 %shard_map.47 = (bf16[512,256]{1,0:T(8,128)(2,1)S(1)}, bf16[32,128,256]{2,1,0:T(8,128)(2,1)S(1)}, bf16[2,64,32,128]{3,2,1,0:T(8,128)(2,1)S(1)}) custom-call(bf16[2,64,32,128]{3,2,1,0:T(8,128)(2,1)} %collective-permute-done.1.sib_ref, bf16[2,64,32,128]{3,2,1,0:T(8,128)(2,1)S(1)} %get-tuple-element.27._.own_ref), custom_call_target="tpu_custom_call" | custom-call | flops 1073741824 | bytes 2097152 | tf_op jit(solution)/shard_map/pallas_call | solution.py:292
  16.6 1.0 %copy-done = bf16[2,64,32,128]{3,2,1,0:T(8,128)(2,1)} copy-done((bf16[2,64,32,128]{3,2,1,0:T(8,128)(2,1)}, bf16[2,64,32,128]{3,2,1,0:T(8,128)(2,1)S(1)}, u32[]{:S(2)}) %copy-start) | copy-done | bytes 1048600
  17.6 1.3 %copy-done.4 = bf16[32,128,256]{2,1,0:T(8,128)(2,1)} copy-done((bf16[32,128,256]{2,1,0:T(8,128)(2,1)}, bf16[32,128,256]{2,1,0:T(8,128)(2,1)S(1)}, u32[]{:S(2)}) %copy-start.4) | copy-done | bytes 2097176
  18.9 1.8 %collective-permute-done.2.raw_ref = bf16[2,64,32,128]{3,2,1,0:T(8,128)(2,1)S(1)} collective-permute-done((bf16[2,64,32,128]{3,2,1,0:T(8,128)(2,1)}, bf16[2,64,32,128]{3,2,1,0:T(8,128)(2,1)S(1)}, u32[]{:S(2)}, u32[]{:S(2)}) %collective-permute-start.2) | collective-permute-done | bytes 1048608 | tf_op jit(solution)/shard_map/ppermute | solution.py:28
  20.8 2.6 %shard_map.48 = (bf16[64,32,128]{2,1,0:T(8,128)(2,1)}, bf16[64,32,128]{2,1,0:T(8,128)(2,1)}, bf16[2,40,32,128]{3,2,1,0:T(8,128)(2,1)}, bf16[2,24,32,128]{3,2,1,0:T(8,128)(2,1)}) custom-call(s32[64]{0:T(128)S(1)} %select_reduce_fusion._.order_ref, bf16[2,64,32,128]{3,2,1,0:T(8,128)(2,1)S(1)} %collective-permute-done.2.raw_ref, ...), custom_call_target="tpu_custom_call" | custom-call | tf_op jit(solution)/shard_map/pallas_call | solution.py:307
  24.6 6.0 %collective-permute-start.8 = (bf16[2,40,32,128]{3,2,1,0:T(8,128)(2,1)}, bf16[2,40,32,128]{3,2,1,0:T(8,128)(2,1)}, u32[]{:S(2)}, u32[]{:S(2)}) collective-permute-start(bf16[2,40,32,128]{3,2,1,0:T(8,128)(2,1)} %get-tuple-element.37), channel_id=1, source_target_pairs={{8,16},{16,8},{24,32},{32,24},{40,48},{48,40},{56,64},{64,56},{72,... | collective-permute-start | bytes 1966088 | tf_op jit(solution)/shard_map/ppermute | solution.py:28
  33.3 1.2 %copy-done.1 = bf16[2,64,32,128]{3,2,1,0:T(8,128)(2,1)S(1)} copy-done((bf16[2,64,32,128]{3,2,1,0:T(8,128)(2,1)S(1)}, bf16[2,64,32,128]{3,2,1,0:T(8,128)(2,1)}, u32[]{:S(2)}) %copy-start.1) | copy-done | bytes 1048600
  34.6 2.6 %shard_map.49 = (bf16[2,320,32,128]{3,2,1,0:T(8,128)(2,1)S(1)}, bf16[64,32,128]{2,1,0:T(8,128)(2,1)S(1)}, bf16[64,32,128]{2,1,0:T(8,128)(2,1)S(1)}) custom-call(bf16[2,64,32,128]{3,2,1,0:T(8,128)(2,1)S(1)} %get-tuple-element.27._.own_ref, bf16[2,64,32,128]{3,2,1,0:T(8,128)(2,1)S(1)} %copy-done.1, bf16[64,32,128]{2,1,0:T(8,128)(2,1)} %get-tuple-element.30.refs_0_, ...), custom_call_target="tpu_custom_call" | custom-call | tf_op jit(solution)/shard_map/pallas_call | solution.py:325
  38.0 1.2 %collective-permute-done.8.refs_2_ = bf16[2,40,32,128]{3,2,1,0:T(8,128)(2,1)} collective-permute-done((bf16[2,40,32,128]{3,2,1,0:T(8,128)(2,1)}, bf16[2,40,32,128]{3,2,1,0:T(8,128)(2,1)}, u32[]{:S(2)}, u32[]{:S(2)}) %collective-permute-start.8) | collective-permute-done | bytes 655392 | tf_op jit(solution)/shard_map/ppermute | solution.py:28
  40.0 1.3 %shard_map.50.late_ref = bf16[2,128,32,128]{3,2,1,0:T(8,128)(2,1)S(1)} custom-call(bf16[64,32,128]{2,1,0:T(8,128)(2,1)S(1)} %collective-permute-done.6.refs_0_, bf16[64,32,128]{2,1,0:T(8,128)(2,1)S(1)} %collective-permute-done.7.refs_1_, bf16[2,40,32,128]{3,2,1,0:T(8,128)(2,1)} %collective-permute-done.8.refs_2_, ...), custom_call_target="tpu_custom_call" | custom-call | flops 21474836480 | tf_op jit(solution)/shard_map/pallas_call | solution.py:336
  41.3 4.4 %shard_map.51 = (f32[6,16,16,128]{3,2,1,0:T(8,128)S(1)}, bf16[5,16,16,128]{3,2,1,0:T(8,128)(2,1)S(1)}, bf16[5,16,16,128]{3,2,1,0:T(8,128)(2,1)S(1)}) custom-call(s32[128]{0:T(128)S(1)} %get-tuple-element.48.first_ref, s32[128]{0:T(128)S(1)} %get-tuple-element.47.second_ref, s32[1]{0:T(128)S(6)} %copy.9.live_ref, s32[1]{0:T(128)} %bitcast.6.z_ref, ...), custom_call_target="tpu_custom_call" | custom-call | flops 8589934592 | bytes 8388608 | tf_op jit(solution)/shard_map/pallas_call | solution.py:363
  45.7 2.0 %collective-permute-start.9 = (bf16[5,16,16,128]{3,2,1,0:T(8,128)(2,1)S(1)}, bf16[5,16,16,128]{3,2,1,0:T(8,128)(2,1)S(1)}, u32[]{:S(2)}, u32[]{:S(2)}) collective-permute-start(bf16[5,16,16,128]{3,2,1,0:T(8,128)(2,1)S(1)} %get-tuple-element.40), channel_id=1, source_target_pairs={{0,1},{1,2},{2,3},{3,4},{4,5},{5,6},{6,7},{7,0},{8,9},{9,10},{10,1... | collective-permute-start | bytes 983048 | tf_op jit(solution)/shard_map/ppermute | solution.py:380
  47.7 4.0 %collective-permute-start.10 = (bf16[5,16,16,128]{3,2,1,0:T(8,128)(2,1)S(1)}, bf16[5,16,16,128]{3,2,1,0:T(8,128)(2,1)S(1)}, u32[]{:S(2)}, u32[]{:S(2)}) collective-permute-start(bf16[5,16,16,128]{3,2,1,0:T(8,128)(2,1)S(1)} %get-tuple-element.41), channel_id=1, source_target_pairs={{0,7},{1,0},{2,1},{3,2},{4,3},{5,4},{6,5},{7,6},{8,15},{9,8},{10,9... | collective-permute-start | bytes 983048 | tf_op jit(solution)/shard_map/ppermute | solution.py:380
  51.7 7.9 %collective-permute-done.9.left_ref = bf16[5,16,16,128]{3,2,1,0:T(8,128)(2,1)S(1)} collective-permute-done((bf16[5,16,16,128]{3,2,1,0:T(8,128)(2,1)S(1)}, bf16[5,16,16,128]{3,2,1,0:T(8,128)(2,1)S(1)}, u32[]{:S(2)}, u32[]{:S(2)}) %collective-permute-start.9) | collective-permute-done | bytes 327712 | tf_op jit(solution)/shard_map/ppermute | solution.py:380
  60.4 3.4 %collective-permute-start.11 = (bf16[2,16,16,128]{3,2,1,0:T(8,128)(2,1)S(1)}, bf16[2,16,16,128]{3,2,1,0:T(8,128)(2,1)S(1)}, u32[]{:S(2)}, u32[]{:S(2)}) collective-permute-start(bf16[2,16,16,128]{3,2,1,0:T(8,128)(2,1)S(1)} %get-tuple-element.43), channel_id=1, source_target_pairs={{0,5},{1,6},{2,7},{3,0},{4,1},{5,2},{6,3},{7,4},{8,13},{9,14},{10,... | collective-permute-start | bytes 393224 | tf_op jit(solution)/shard_map/ppermute | solution.py:380
  63.8 1.2 %collective-permute-start.12 = (bf16[2,16,16,128]{3,2,1,0:T(8,128)(2,1)S(1)}, bf16[2,16,16,128]{3,2,1,0:T(8,128)(2,1)S(1)}, u32[]{:S(2)}, u32[]{:S(2)}) collective-permute-start(bf16[2,16,16,128]{3,2,1,0:T(8,128)(2,1)S(1)} %get-tuple-element.44), channel_id=1, source_target_pairs={{0,3},{1,4},{2,5},{3,6},{4,7},{5,0},{6,1},{7,2},{8,11},{9,12},{10,... | collective-permute-start | bytes 393224 | tf_op jit(solution)/shard_map/ppermute | solution.py:380
  65.0 7.3 %collective-permute-done.11.refs_0_ = bf16[2,16,16,128]{3,2,1,0:T(8,128)(2,1)S(1)} collective-permute-done((bf16[2,16,16,128]{3,2,1,0:T(8,128)(2,1)S(1)}, bf16[2,16,16,128]{3,2,1,0:T(8,128)(2,1)S(1)}, u32[]{:S(2)}, u32[]{:S(2)}) %collective-permute-start.11) | collective-permute-done | bytes 131104 | tf_op jit(solution)/shard_map/ppermute | solution.py:380
  72.3 2.3 %collective-permute-done.12.refs_1_ = bf16[2,16,16,128]{3,2,1,0:T(8,128)(2,1)S(1)} collective-permute-done((bf16[2,16,16,128]{3,2,1,0:T(8,128)(2,1)S(1)}, bf16[2,16,16,128]{3,2,1,0:T(8,128)(2,1)S(1)}, u32[]{:S(2)}, u32[]{:S(2)}) %collective-permute-start.12) | collective-permute-done | bytes 131104 | tf_op jit(solution)/shard_map/ppermute | solution.py:380
  75.3 1.9 %shard_map.53 = f32[128,512]{1,0:T(8,128)} custom-call(f32[2,16,16,128]{3,2,1,0:T(8,128)} %copy-done.2, bf16[2,16,16,128]{3,2,1,0:T(8,128)(2,1)} %copy-done.6, bf16[2,16,16,128]{3,2,1,0:T(8,128)(2,1)} %copy-done.7), custom_call_target="tpu_custom_call" | custom-call | tf_op jit(solution)/shard_map/pallas_call | solution.py:392
  (43 shorter events, 8.0 us)
Async XLA Ops:
  0.0 13.3 %collective-permute-start.1 = (bf16[2,64,32,128]{3,2,1,0:T(8,128)(2,1)}, bf16[2,64,32,128]{3,2,1,0:T(8,128)(2,1)}, u32[]{:S(2)}, u32[]{:S(2)}) collective-permute-start(bf16[2,64,32,128]{3,2,1,0:T(8,128)(2,1)} %bitcast.32), channel_id=1, source_target_pairs={{0,8},{8,0},{16,24},{24,16},{32,40},{40,32},{48,56},{56,48},{64,72... | collective-permute-start | bytes 3145736 | tf_op jit(solution)/shard_map/ppermute | solution.py:33
  0.0 20.8 %collective-permute-start.2 = (bf16[2,64,32,128]{3,2,1,0:T(8,128)(2,1)}, bf16[2,64,32,128]{3,2,1,0:T(8,128)(2,1)S(1)}, u32[]{:S(2)}, u32[]{:S(2)}) collective-permute-start(bf16[2,64,32,128]{3,2,1,0:T(8,128)(2,1)} %bitcast.33), channel_id=1, source_target_pairs={{8,24},{16,0},{24,40},{32,16},{40,56},{48,32},{56,72},{64,48},{72,... | collective-permute-start | bytes 3145736 | tf_op jit(solution)/shard_map/ppermute | solution.py:28
  7.7 1.2 %copy-start.3 = (bf16[2,64,2,2048]{3,2,1,0:T(2,128)(2,1)S(1)}, bf16[2,64,2,2048]{3,2,1,0:T(2,128)(2,1)}, u32[]{:S(2)}) copy-start(bf16[2,64,2,2048]{3,2,1,0:T(2,128)(2,1)} %param.6) | copy-start | bytes 3145732
  11.4 22.0 %collective-permute-start.5 = (bf16[2,64,32,128]{3,2,1,0:T(8,128)(2,1)}, bf16[2,64,32,128]{3,2,1,0:T(8,128)(2,1)S(1)}, u32[]{:S(2)}, u32[]{:S(2)}) collective-permute-start(bf16[2,64,32,128]{3,2,1,0:T(8,128)(2,1)} %get-tuple-element.32), channel_id=1, source_target_pairs={{0,16},{16,32},{24,8},{32,48},{40,24},{48,64},{56,40},{64,80},{72,... | collective-permute-start | bytes 3145736 | tf_op jit(solution)/shard_map/ppermute | solution.py:28
  16.6 1.0 %copy-start = (bf16[2,64,32,128]{3,2,1,0:T(8,128)(2,1)}, bf16[2,64,32,128]{3,2,1,0:T(8,128)(2,1)S(1)}, u32[]{:S(2)}) copy-start(bf16[2,64,32,128]{3,2,1,0:T(8,128)(2,1)S(1)} %get-tuple-element.28.sib_ref) | copy-start | bytes 3145732
  17.6 1.3 %copy-start.4 = (bf16[32,128,256]{2,1,0:T(8,128)(2,1)}, bf16[32,128,256]{2,1,0:T(8,128)(2,1)S(1)}, u32[]{:S(2)}) copy-start(bf16[32,128,256]{2,1,0:T(8,128)(2,1)S(1)} %get-tuple-element.38.wave_ref) | copy-start | bytes 6291460
  23.4 9.9 %collective-permute-start.3 = (bf16[64,32,128]{2,1,0:T(8,128)(2,1)}, bf16[64,32,128]{2,1,0:T(8,128)(2,1)S(1)}, u32[]{:S(2)}, u32[]{:S(2)}) collective-permute-start(bf16[64,32,128]{2,1,0:T(8,128)(2,1)} %get-tuple-element.30.refs_0_), channel_id=1, source_target_pairs={{0,8},{8,0},{16,24},{24,16},{32,40},{40,32},{48,56},{56,48},{64,72... | collective-permute-start | bytes 1572872 | tf_op jit(solution)/shard_map/ppermute | solution.py:33
  23.4 9.9 %collective-permute-start.4 = (bf16[64,32,128]{2,1,0:T(8,128)(2,1)}, bf16[64,32,128]{2,1,0:T(8,128)(2,1)S(1)}, u32[]{:S(2)}, u32[]{:S(2)}) collective-permute-start(bf16[64,32,128]{2,1,0:T(8,128)(2,1)} %get-tuple-element.31.refs_1_), channel_id=1, source_target_pairs={{0,8},{8,0},{16,24},{24,16},{32,40},{40,32},{48,56},{56,48},{64,72... | collective-permute-start | bytes 1572872 | tf_op jit(solution)/shard_map/ppermute | solution.py:33
  24.6 14.6 %collective-permute-start.8 = (bf16[2,40,32,128]{3,2,1,0:T(8,128)(2,1)}, bf16[2,40,32,128]{3,2,1,0:T(8,128)(2,1)}, u32[]{:S(2)}, u32[]{:S(2)}) collective-permute-start(bf16[2,40,32,128]{3,2,1,0:T(8,128)(2,1)} %get-tuple-element.37), channel_id=1, source_target_pairs={{8,16},{16,8},{24,32},{32,24},{40,48},{48,40},{56,64},{64,56},{72,... | collective-permute-start | bytes 1966088 | tf_op jit(solution)/shard_map/ppermute | solution.py:28
  33.3 1.2 %copy-start.1 = (bf16[2,64,32,128]{3,2,1,0:T(8,128)(2,1)S(1)}, bf16[2,64,32,128]{3,2,1,0:T(8,128)(2,1)}, u32[]{:S(2)}) copy-start(bf16[2,64,32,128]{3,2,1,0:T(8,128)(2,1)} %copy-done) | copy-start | bytes 3145732
  34.6 3.4 %copy-start.8 = (f32[2048]{0:T(1024)S(1)}, f32[2048]{0:T(1024)}, u32[]{:S(2)}) copy-start(f32[2048]{0:T(1024)} %param.7) | copy-start | bytes 24580
  37.2 2.0 %collective-permute-start.6 = (bf16[64,32,128]{2,1,0:T(8,128)(2,1)S(1)}, bf16[64,32,128]{2,1,0:T(8,128)(2,1)S(1)}, u32[]{:S(2)}, u32[]{:S(2)}) collective-permute-start(bf16[64,32,128]{2,1,0:T(8,128)(2,1)S(1)} %get-tuple-element.35), channel_id=1, source_target_pairs={{0,8},{8,0},{16,24},{24,16},{32,40},{40,32},{48,56},{56,48},{64,72... | collective-permute-start | bytes 1572872 | tf_op jit(solution)/shard_map/ppermute | solution.py:33
  37.3 2.6 %collective-permute-start.7 = (bf16[64,32,128]{2,1,0:T(8,128)(2,1)S(1)}, bf16[64,32,128]{2,1,0:T(8,128)(2,1)S(1)}, u32[]{:S(2)}, u32[]{:S(2)}) collective-permute-start(bf16[64,32,128]{2,1,0:T(8,128)(2,1)S(1)} %get-tuple-element.36), channel_id=1, source_target_pairs={{0,8},{8,0},{16,24},{24,16},{32,40},{40,32},{48,56},{56,48},{64,72... | collective-permute-start | bytes 1572872 | tf_op jit(solution)/shard_map/ppermute | solution.py:33
  38.0 3.3 %copy-start.5 = (bf16[32,128,256]{2,1,0:T(8,128)(2,1)S(1)}, bf16[32,128,256]{2,1,0:T(8,128)(2,1)}, u32[]{:S(2)}) copy-start(bf16[32,128,256]{2,1,0:T(8,128)(2,1)} %copy-done.4) | copy-start | bytes 6291460
  45.7 14.0 %collective-permute-start.9 = (bf16[5,16,16,128]{3,2,1,0:T(8,128)(2,1)S(1)}, bf16[5,16,16,128]{3,2,1,0:T(8,128)(2,1)S(1)}, u32[]{:S(2)}, u32[]{:S(2)}) collective-permute-start(bf16[5,16,16,128]{3,2,1,0:T(8,128)(2,1)S(1)} %get-tuple-element.40), channel_id=1, source_target_pairs={{0,1},{1,2},{2,3},{3,4},{4,5},{5,6},{6,7},{7,0},{8,9},{9,10},{10,1... | collective-permute-start | bytes 983048 | tf_op jit(solution)/shard_map/ppermute | solution.py:380
  47.7 12.0 %collective-permute-start.10 = (bf16[5,16,16,128]{3,2,1,0:T(8,128)(2,1)S(1)}, bf16[5,16,16,128]{3,2,1,0:T(8,128)(2,1)S(1)}, u32[]{:S(2)}, u32[]{:S(2)}) collective-permute-start(bf16[5,16,16,128]{3,2,1,0:T(8,128)(2,1)S(1)} %get-tuple-element.41), channel_id=1, source_target_pairs={{0,7},{1,0},{2,1},{3,2},{4,3},{5,4},{6,5},{7,6},{8,15},{9,8},{10,9... | collective-permute-start | bytes 983048 | tf_op jit(solution)/shard_map/ppermute | solution.py:380
  59.8 0.7 copy-start.2
  60.4 11.9 %collective-permute-start.11 = (bf16[2,16,16,128]{3,2,1,0:T(8,128)(2,1)S(1)}, bf16[2,16,16,128]{3,2,1,0:T(8,128)(2,1)S(1)}, u32[]{:S(2)}, u32[]{:S(2)}) collective-permute-start(bf16[2,16,16,128]{3,2,1,0:T(8,128)(2,1)S(1)} %get-tuple-element.43), channel_id=1, source_target_pairs={{0,5},{1,6},{2,7},{3,0},{4,1},{5,2},{6,3},{7,4},{8,13},{9,14},{10,... | collective-permute-start | bytes 393224 | tf_op jit(solution)/shard_map/ppermute | solution.py:380
  63.8 10.9 %collective-permute-start.12 = (bf16[2,16,16,128]{3,2,1,0:T(8,128)(2,1)S(1)}, bf16[2,16,16,128]{3,2,1,0:T(8,128)(2,1)S(1)}, u32[]{:S(2)}, u32[]{:S(2)}) collective-permute-start(bf16[2,16,16,128]{3,2,1,0:T(8,128)(2,1)S(1)} %get-tuple-element.44), channel_id=1, source_target_pairs={{0,3},{1,4},{2,5},{3,6},{4,7},{5,0},{6,1},{7,2},{8,11},{9,12},{10,... | collective-permute-start | bytes 393224 | tf_op jit(solution)/shard_map/ppermute | solution.py:380
  72.3 2.3 %copy-start.6 = (bf16[2,16,16,128]{3,2,1,0:T(8,128)(2,1)}, bf16[2,16,16,128]{3,2,1,0:T(8,128)(2,1)S(1)}, u32[]{:S(2)}) copy-start(bf16[2,16,16,128]{3,2,1,0:T(8,128)(2,1)S(1)} %collective-permute-done.11.refs_0_) | copy-start | bytes 393220
  74.7 0.6 copy-start.7

commit v4 on v3

--- a/solution.py
+++ b/solution.py
@@ -387,7 +387,7 @@
         out_shape=[jax.ShapeDtypeStruct(piece, d) for d in (F32, BF, BF)],
         in_specs=[VM] * 3,
         out_specs=[VM] * 3,
-        compiler_params=pltpu.CompilerParams(vmem_limit_bytes=16 << 20),
+        compiler_params=pltpu.CompilerParams(vmem_limit_bytes=8 << 20),
     )(keep, along(up, 1), along(down, -1))
     return pl.pallas_call(
         final_kernel,
@@ -395,6 +395,7 @@
         in_specs=[VM] * 3,
         out_specs=VM,
         scratch_shapes=[pltpu.VMEM((LOW * wide, slots), F32)],
+        compiler_params=pltpu.CompilerParams(vmem_limit_bytes=8 << 20),
     )(mine, along(behind, -3), along(ahead, 3))
 
 

time: 78.7 us -> 76.5 us (0.972)
  local copies, waits for them, and re-layouts: 7.59 us -> 6.27 us
  Pallas kernels: 18.7 us -> 17.7 us
    unnamed x18 -> x12, local copies, waits for them, and re-layouts: 6.1 us -> 4.77 us
    pallas_call x1, Pallas kernels: 1.93 us -> 0.89 us  [local(): pl.pallas_call(final_kernel, out_shape=jax.ShapeDtypeStruct((slots, LOW *...]
  transfers between devices with their start and end apart: 12 -> 12, of which waited for: 7 -> 7; matrix products, arithmetic and copies ran while one was open for 6% -> 6% of each run, Pallas kernels for 14% -> 15%
where the time goes in v4:
time: 76.5 us; the launch traced here: 75.1 us
  starting transfers between devices  24.9 us (33%)
  waiting for transfers between devices  21.3 us (28%)
  Pallas kernels  17.7 us (23%)
  local copies, waits for them, and re-layouts  6.27 us (8%)
  other arithmetic  3.3 us (4%)
  between operations  1.56 us (2%)
    ppermute x4, waiting for transfers between devices, along(): lax.ppermute(value, 'win', [(i, (i + step) % win_count) for i in range(wi...  17.5 us
    ppermute x3, starting transfers between devices, moved(): lax.ppermute(value, 'pair', [(a, b) for a, b in pairs if 0 <= b < count])  13.1 us
    ppermute x4, starting transfers between devices, along(): lax.ppermute(value, 'win', [(i, (i + step) % win_count) for i in range(wi...  10.8 us
    unnamed x12, local copies, waits for them, and re-layouts  4.77 us
    pallas_call x1, Pallas kernels, local(): pl.pallas_call(corr_kernel, out_shape=[jax.ShapeDtypeStruct((6, half, wid...  4.36 us
    pallas_call x1, Pallas kernels, local(): pl.pallas_call(table_kernel, out_shape=[jax.ShapeDtypeStruct((2 * LOW * G...  3.31 us
    ppermute x3, waiting for transfers between devices, moved(): lax.ppermute(value, 'pair', [(a, b) for a, b in pairs if 0 <= b < count])  2.83 us
    pallas_call x1, Pallas kernels, local(): pl.pallas_call(gather_kernel, out_shape=[jax.ShapeDtypeStruct((win_dev, 5...  2.64 us
  transfers between devices with their start and end apart: 12, of which 7 were waited for; matrix products, arithmetic and copies ran while one was open for 6% of the time, Pallas kernels for 15%

profile of v4, /device:TPU:6, one launch (start us, length us, event | category | flops | bytes accessed | tf_op | source)
XLA Modules:
  0.0 75.1 jit_solution(11797655360647834597)
XLA Ops:
  0.0 5.2 %collective-permute-start.2 = (bf16[2,64,32,128]{3,2,1,0:T(8,128)(2,1)}, bf16[2,64,32,128]{3,2,1,0:T(8,128)(2,1)S(1)}, u32[]{:S(2)}, u32[]{:S(2)}) collective-permute-start(bf16[2,64,32,128]{3,2,1,0:T(8,128)(2,1)} %bitcast.33), channel_id=1, source_target_pairs={{8,24},{16,0},{24,40},{32,16},{40,56},{48,32},{56,72},{64,48},{72,... | collective-permute-start | bytes 3145736 | tf_op jit(solution)/shard_map/ppermute | solution.py:28
  5.2 0.9 %compare_select_fusion = s32[32,128,1]{1,2,0:T(1,128)S(1)} fusion(s32[32,128,2]{1,2,0:T(2,128)} %param.8, s32[32]{0:T(128)S(1)} %fusion.5), kind=kLoop, calls=%fused_computation.4 | loop fusion | flops 94208 | bytes 32896 | tf_op jit(solution)/shard_map/jit(_where)/select_n | solution.py:254
  7.7 1.2 %copy-done.2 = bf16[2,64,2,2048]{3,2,1,0:T(2,128)(2,1)S(1)} copy-done((bf16[2,64,2,2048]{3,2,1,0:T(2,128)(2,1)S(1)}, bf16[2,64,2,2048]{3,2,1,0:T(2,128)(2,1)}, u32[]{:S(2)}) %copy-start.2) | copy-done | bytes 1048600
  9.0 2.4 %shard_map.46 = (bf16[2,64,32,128]{3,2,1,0:T(8,128)(2,1)}, bf16[2,64,32,128]{3,2,1,0:T(8,128)(2,1)S(1)}) custom-call(bf16[2,64,32,128]{3,2,1,0:T(8,128)(2,1)S(1)} %bitcast.34, s32[64]{0:T(128)S(1)} %select_reduce_fusion._.order_ref), custom_call_target="tpu_custom_call" | custom-call | flops 1073741824 | bytes 2097152 | tf_op jit(solution)/shard_map/pallas_call | solution.py:282
  11.4 1.9 %collective-permute-start.5 = (bf16[2,64,32,128]{3,2,1,0:T(8,128)(2,1)}, bf16[2,64,32,128]{3,2,1,0:T(8,128)(2,1)S(1)}, u32[]{:S(2)}, u32[]{:S(2)}) collective-permute-start(bf16[2,64,32,128]{3,2,1,0:T(8,128)(2,1)} %get-tuple-element.32), channel_id=1, source_target_pairs={{0,16},{16,32},{24,8},{32,48},{40,24},{48,64},{56,40},{64,80},{72,... | collective-permute-start | bytes 3145736 | tf_op jit(solution)/shard_map/ppermute | solution.py:28
  13.3 3.3 %shard_map.47 = (bf16[512,256]{1,0:T(8,128)(2,1)S(1)}, bf16[32,128,256]{2,1,0:T(8,128)(2,1)S(1)}, bf16[2,64,32,128]{3,2,1,0:T(8,128)(2,1)S(1)}) custom-call(bf16[2,64,32,128]{3,2,1,0:T(8,128)(2,1)} %collective-permute-done.1.sib_ref, bf16[2,64,32,128]{3,2,1,0:T(8,128)(2,1)S(1)} %get-tuple-element.27._.own_ref), custom_call_target="tpu_custom_call" | custom-call | flops 1073741824 | bytes 2097152 | tf_op jit(solution)/shard_map/pallas_call | solution.py:292
  16.6 1.0 %copy-done = bf16[2,64,32,128]{3,2,1,0:T(8,128)(2,1)} copy-done((bf16[2,64,32,128]{3,2,1,0:T(8,128)(2,1)}, bf16[2,64,32,128]{3,2,1,0:T(8,128)(2,1)S(1)}, u32[]{:S(2)}) %copy-start) | copy-done | bytes 1048600
  17.6 1.3 %copy-done.3 = bf16[32,128,256]{2,1,0:T(8,128)(2,1)} copy-done((bf16[32,128,256]{2,1,0:T(8,128)(2,1)}, bf16[32,128,256]{2,1,0:T(8,128)(2,1)S(1)}, u32[]{:S(2)}) %copy-start.3) | copy-done | bytes 2097176
  19.0 1.8 %collective-permute-done.2.raw_ref = bf16[2,64,32,128]{3,2,1,0:T(8,128)(2,1)S(1)} collective-permute-done((bf16[2,64,32,128]{3,2,1,0:T(8,128)(2,1)}, bf16[2,64,32,128]{3,2,1,0:T(8,128)(2,1)S(1)}, u32[]{:S(2)}, u32[]{:S(2)}) %collective-permute-start.2) | collective-permute-done | bytes 1048608 | tf_op jit(solution)/shard_map/ppermute | solution.py:28
  20.8 2.6 %shard_map.48 = (bf16[64,32,128]{2,1,0:T(8,128)(2,1)}, bf16[64,32,128]{2,1,0:T(8,128)(2,1)}, bf16[2,40,32,128]{3,2,1,0:T(8,128)(2,1)}, bf16[2,24,32,128]{3,2,1,0:T(8,128)(2,1)}) custom-call(s32[64]{0:T(128)S(1)} %select_reduce_fusion._.order_ref, bf16[2,64,32,128]{3,2,1,0:T(8,128)(2,1)S(1)} %collective-permute-done.2.raw_ref, ...), custom_call_target="tpu_custom_call" | custom-call | tf_op jit(solution)/shard_map/pallas_call | solution.py:307
  24.6 6.0 %collective-permute-start.8 = (bf16[2,40,32,128]{3,2,1,0:T(8,128)(2,1)}, bf16[2,40,32,128]{3,2,1,0:T(8,128)(2,1)}, u32[]{:S(2)}, u32[]{:S(2)}) collective-permute-start(bf16[2,40,32,128]{3,2,1,0:T(8,128)(2,1)} %get-tuple-element.37), channel_id=1, source_target_pairs={{8,16},{16,8},{24,32},{32,24},{40,48},{48,40},{56,64},{64,56},{72,... | collective-permute-start | bytes 1966088 | tf_op jit(solution)/shard_map/ppermute | solution.py:28
  33.5 1.2 %copy-done.1 = bf16[2,64,32,128]{3,2,1,0:T(8,128)(2,1)S(1)} copy-done((bf16[2,64,32,128]{3,2,1,0:T(8,128)(2,1)S(1)}, bf16[2,64,32,128]{3,2,1,0:T(8,128)(2,1)}, u32[]{:S(2)}) %copy-start.1) | copy-done | bytes 1048600
  34.7 2.6 %shard_map.49 = (bf16[2,320,32,128]{3,2,1,0:T(8,128)(2,1)S(1)}, bf16[64,32,128]{2,1,0:T(8,128)(2,1)S(1)}, bf16[64,32,128]{2,1,0:T(8,128)(2,1)S(1)}) custom-call(bf16[2,64,32,128]{3,2,1,0:T(8,128)(2,1)S(1)} %get-tuple-element.27._.own_ref, bf16[2,64,32,128]{3,2,1,0:T(8,128)(2,1)S(1)} %copy-done.1, bf16[64,32,128]{2,1,0:T(8,128)(2,1)} %get-tuple-element.30.refs_0_, ...), custom_call_target="tpu_custom_call" | custom-call | tf_op jit(solution)/shard_map/pallas_call | solution.py:325
  38.1 1.0 %collective-permute-done.8.refs_2_ = bf16[2,40,32,128]{3,2,1,0:T(8,128)(2,1)} collective-permute-done((bf16[2,40,32,128]{3,2,1,0:T(8,128)(2,1)}, bf16[2,40,32,128]{3,2,1,0:T(8,128)(2,1)}, u32[]{:S(2)}, u32[]{:S(2)}) %collective-permute-start.8) | collective-permute-done | bytes 655392 | tf_op jit(solution)/shard_map/ppermute | solution.py:28
  40.1 1.3 %shard_map.50.late_ref = bf16[2,128,32,128]{3,2,1,0:T(8,128)(2,1)S(1)} custom-call(bf16[64,32,128]{2,1,0:T(8,128)(2,1)S(1)} %collective-permute-done.6.refs_0_, bf16[64,32,128]{2,1,0:T(8,128)(2,1)S(1)} %collective-permute-done.7.refs_1_, bf16[2,40,32,128]{3,2,1,0:T(8,128)(2,1)} %collective-permute-done.8.refs_2_, ...), custom_call_target="tpu_custom_call" | custom-call | flops 21474836480 | tf_op jit(solution)/shard_map/pallas_call | solution.py:336
  41.4 4.4 %shard_map.51 = (f32[6,16,16,128]{3,2,1,0:T(8,128)S(1)}, bf16[5,16,16,128]{3,2,1,0:T(8,128)(2,1)S(1)}, bf16[5,16,16,128]{3,2,1,0:T(8,128)(2,1)S(1)}) custom-call(s32[128]{0:T(128)S(1)} %get-tuple-element.48.first_ref, s32[128]{0:T(128)S(1)} %get-tuple-element.47.second_ref, s32[1]{0:T(128)S(6)} %copy.9.live_ref, s32[1]{0:T(128)} %bitcast.6.z_ref, ...), custom_call_target="tpu_custom_call" | custom-call | flops 8589934592 | bytes 8388608 | tf_op jit(solution)/shard_map/pallas_call | solution.py:363
  45.8 2.0 %collective-permute-start.9 = (bf16[5,16,16,128]{3,2,1,0:T(8,128)(2,1)S(1)}, bf16[5,16,16,128]{3,2,1,0:T(8,128)(2,1)S(1)}, u32[]{:S(2)}, u32[]{:S(2)}) collective-permute-start(bf16[5,16,16,128]{3,2,1,0:T(8,128)(2,1)S(1)} %get-tuple-element.40), channel_id=1, source_target_pairs={{0,1},{1,2},{2,3},{3,4},{4,5},{5,6},{6,7},{7,0},{8,9},{9,10},{10,1... | collective-permute-start | bytes 983048 | tf_op jit(solution)/shard_map/ppermute | solution.py:380
  47.8 4.0 %collective-permute-start.10 = (bf16[5,16,16,128]{3,2,1,0:T(8,128)(2,1)S(1)}, bf16[5,16,16,128]{3,2,1,0:T(8,128)(2,1)S(1)}, u32[]{:S(2)}, u32[]{:S(2)}) collective-permute-start(bf16[5,16,16,128]{3,2,1,0:T(8,128)(2,1)S(1)} %get-tuple-element.41), channel_id=1, source_target_pairs={{0,7},{1,0},{2,1},{3,2},{4,3},{5,4},{6,5},{7,6},{8,15},{9,8},{10,9... | collective-permute-start | bytes 983048 | tf_op jit(solution)/shard_map/ppermute | solution.py:380
  51.8 7.9 %collective-permute-done.9.left_ref = bf16[5,16,16,128]{3,2,1,0:T(8,128)(2,1)S(1)} collective-permute-done((bf16[5,16,16,128]{3,2,1,0:T(8,128)(2,1)S(1)}, bf16[5,16,16,128]{3,2,1,0:T(8,128)(2,1)S(1)}, u32[]{:S(2)}, u32[]{:S(2)}) %collective-permute-start.9) | collective-permute-done | bytes 327712 | tf_op jit(solution)/shard_map/ppermute | solution.py:380
  59.9 3.4 %collective-permute-start.11 = (bf16[2,16,16,128]{3,2,1,0:T(8,128)(2,1)S(1)}, bf16[2,16,16,128]{3,2,1,0:T(8,128)(2,1)S(1)}, u32[]{:S(2)}, u32[]{:S(2)}) collective-permute-start(bf16[2,16,16,128]{3,2,1,0:T(8,128)(2,1)S(1)} %get-tuple-element.43), channel_id=1, source_target_pairs={{0,5},{1,6},{2,7},{3,0},{4,1},{5,2},{6,3},{7,4},{8,13},{9,14},{10,... | collective-permute-start | bytes 393224 | tf_op jit(solution)/shard_map/ppermute | solution.py:380
  63.3 1.3 %collective-permute-start.12 = (bf16[2,16,16,128]{3,2,1,0:T(8,128)(2,1)S(1)}, bf16[2,16,16,128]{3,2,1,0:T(8,128)(2,1)S(1)}, u32[]{:S(2)}, u32[]{:S(2)}) collective-permute-start(bf16[2,16,16,128]{3,2,1,0:T(8,128)(2,1)S(1)} %get-tuple-element.44), channel_id=1, source_target_pairs={{0,3},{1,4},{2,5},{3,6},{4,7},{5,0},{6,1},{7,2},{8,11},{9,12},{10,... | collective-permute-start | bytes 393224 | tf_op jit(solution)/shard_map/ppermute | solution.py:380
  64.6 7.2 %collective-permute-done.11.refs_0_ = bf16[2,16,16,128]{3,2,1,0:T(8,128)(2,1)S(1)} collective-permute-done((bf16[2,16,16,128]{3,2,1,0:T(8,128)(2,1)S(1)}, bf16[2,16,16,128]{3,2,1,0:T(8,128)(2,1)S(1)}, u32[]{:S(2)}, u32[]{:S(2)}) %collective-permute-start.11) | collective-permute-done | bytes 131104 | tf_op jit(solution)/shard_map/ppermute | solution.py:380
  71.9 2.3 %collective-permute-done.12.refs_1_ = bf16[2,16,16,128]{3,2,1,0:T(8,128)(2,1)S(1)} collective-permute-done((bf16[2,16,16,128]{3,2,1,0:T(8,128)(2,1)S(1)}, bf16[2,16,16,128]{3,2,1,0:T(8,128)(2,1)S(1)}, u32[]{:S(2)}, u32[]{:S(2)}) %collective-permute-start.12) | collective-permute-done | bytes 131104 | tf_op jit(solution)/shard_map/ppermute | solution.py:380
  74.2 0.9 %shard_map.53 = f32[128,512]{1,0:T(8,128)} custom-call(f32[2,16,16,128]{3,2,1,0:T(8,128)S(1)} %get-tuple-element.42.own_ref, bf16[2,16,16,128]{3,2,1,0:T(8,128)(2,1)S(1)} %collective-permute-done.11.refs_0_, bf16[2,16,16,128]{3,2,1,0:T(8,128)(2,1)S(1)} %collective-permute-done.12.refs_1_), custom_call_target="tpu_custom_call" | custom-call | tf_op jit(solution)/shard_map/pallas_call | solution.py:392
  (37 shorter events, 6.9 us)
Async XLA Ops:
  0.0 13.3 %collective-permute-start.1 = (bf16[2,64,32,128]{3,2,1,0:T(8,128)(2,1)}, bf16[2,64,32,128]{3,2,1,0:T(8,128)(2,1)}, u32[]{:S(2)}, u32[]{:S(2)}) collective-permute-start(bf16[2,64,32,128]{3,2,1,0:T(8,128)(2,1)} %bitcast.32), channel_id=1, source_target_pairs={{0,8},{8,0},{16,24},{24,16},{32,40},{40,32},{48,56},{56,48},{64,72... | collective-permute-start | bytes 3145736 | tf_op jit(solution)/shard_map/ppermute | solution.py:33
  0.0 20.7 %collective-permute-start.2 = (bf16[2,64,32,128]{3,2,1,0:T(8,128)(2,1)}, bf16[2,64,32,128]{3,2,1,0:T(8,128)(2,1)S(1)}, u32[]{:S(2)}, u32[]{:S(2)}) collective-permute-start(bf16[2,64,32,128]{3,2,1,0:T(8,128)(2,1)} %bitcast.33), channel_id=1, source_target_pairs={{8,24},{16,0},{24,40},{32,16},{40,56},{48,32},{56,72},{64,48},{72,... | collective-permute-start | bytes 3145736 | tf_op jit(solution)/shard_map/ppermute | solution.py:28
  7.7 1.2 %copy-start.2 = (bf16[2,64,2,2048]{3,2,1,0:T(2,128)(2,1)S(1)}, bf16[2,64,2,2048]{3,2,1,0:T(2,128)(2,1)}, u32[]{:S(2)}) copy-start(bf16[2,64,2,2048]{3,2,1,0:T(2,128)(2,1)} %param.6) | copy-start | bytes 3145732
  11.4 22.1 %collective-permute-start.5 = (bf16[2,64,32,128]{3,2,1,0:T(8,128)(2,1)}, bf16[2,64,32,128]{3,2,1,0:T(8,128)(2,1)S(1)}, u32[]{:S(2)}, u32[]{:S(2)}) collective-permute-start(bf16[2,64,32,128]{3,2,1,0:T(8,128)(2,1)} %get-tuple-element.32), channel_id=1, source_target_pairs={{0,16},{16,32},{24,8},{32,48},{40,24},{48,64},{56,40},{64,80},{72,... | collective-permute-start | bytes 3145736 | tf_op jit(solution)/shard_map/ppermute | solution.py:28
  16.6 1.0 %copy-start = (bf16[2,64,32,128]{3,2,1,0:T(8,128)(2,1)}, bf16[2,64,32,128]{3,2,1,0:T(8,128)(2,1)S(1)}, u32[]{:S(2)}) copy-start(bf16[2,64,32,128]{3,2,1,0:T(8,128)(2,1)S(1)} %get-tuple-element.28.sib_ref) | copy-start | bytes 3145732
  17.6 1.3 %copy-start.3 = (bf16[32,128,256]{2,1,0:T(8,128)(2,1)}, bf16[32,128,256]{2,1,0:T(8,128)(2,1)S(1)}, u32[]{:S(2)}) copy-start(bf16[32,128,256]{2,1,0:T(8,128)(2,1)S(1)} %get-tuple-element.38.wave_ref) | copy-start | bytes 6291460
  23.4 10.1 %collective-permute-start.3 = (bf16[64,32,128]{2,1,0:T(8,128)(2,1)}, bf16[64,32,128]{2,1,0:T(8,128)(2,1)S(1)}, u32[]{:S(2)}, u32[]{:S(2)}) collective-permute-start(bf16[64,32,128]{2,1,0:T(8,128)(2,1)} %get-tuple-element.30.refs_0_), channel_id=1, source_target_pairs={{0,8},{8,0},{16,24},{24,16},{32,40},{40,32},{48,56},{56,48},{64,72... | collective-permute-start | bytes 1572872 | tf_op jit(solution)/shard_map/ppermute | solution.py:33
  23.4 10.1 %collective-permute-start.4 = (bf16[64,32,128]{2,1,0:T(8,128)(2,1)}, bf16[64,32,128]{2,1,0:T(8,128)(2,1)S(1)}, u32[]{:S(2)}, u32[]{:S(2)}) collective-permute-start(bf16[64,32,128]{2,1,0:T(8,128)(2,1)} %get-tuple-element.31.refs_1_), channel_id=1, source_target_pairs={{0,8},{8,0},{16,24},{24,16},{32,40},{40,32},{48,56},{56,48},{64,72... | collective-permute-start | bytes 1572872 | tf_op jit(solution)/shard_map/ppermute | solution.py:33
  24.6 14.6 %collective-permute-start.8 = (bf16[2,40,32,128]{3,2,1,0:T(8,128)(2,1)}, bf16[2,40,32,128]{3,2,1,0:T(8,128)(2,1)}, u32[]{:S(2)}, u32[]{:S(2)}) collective-permute-start(bf16[2,40,32,128]{3,2,1,0:T(8,128)(2,1)} %get-tuple-element.37), channel_id=1, source_target_pairs={{8,16},{16,8},{24,32},{32,24},{40,48},{48,40},{56,64},{64,56},{72,... | collective-permute-start | bytes 1966088 | tf_op jit(solution)/shard_map/ppermute | solution.py:28
  33.5 1.2 %copy-start.1 = (bf16[2,64,32,128]{3,2,1,0:T(8,128)(2,1)S(1)}, bf16[2,64,32,128]{3,2,1,0:T(8,128)(2,1)}, u32[]{:S(2)}) copy-start(bf16[2,64,32,128]{3,2,1,0:T(8,128)(2,1)} %copy-done) | copy-start | bytes 3145732
  34.7 3.4 %copy-start.5 = (f32[2048]{0:T(1024)S(1)}, f32[2048]{0:T(1024)}, u32[]{:S(2)}) copy-start(f32[2048]{0:T(1024)} %param.7) | copy-start | bytes 24580
  37.4 2.0 %collective-permute-start.6 = (bf16[64,32,128]{2,1,0:T(8,128)(2,1)S(1)}, bf16[64,32,128]{2,1,0:T(8,128)(2,1)S(1)}, u32[]{:S(2)}, u32[]{:S(2)}) collective-permute-start(bf16[64,32,128]{2,1,0:T(8,128)(2,1)S(1)} %get-tuple-element.35), channel_id=1, source_target_pairs={{0,8},{8,0},{16,24},{24,16},{32,40},{40,32},{48,56},{56,48},{64,72... | collective-permute-start | bytes 1572872 | tf_op jit(solution)/shard_map/ppermute | solution.py:33
  37.5 2.6 %collective-permute-start.7 = (bf16[64,32,128]{2,1,0:T(8,128)(2,1)S(1)}, bf16[64,32,128]{2,1,0:T(8,128)(2,1)S(1)}, u32[]{:S(2)}, u32[]{:S(2)}) collective-permute-start(bf16[64,32,128]{2,1,0:T(8,128)(2,1)S(1)} %get-tuple-element.36), channel_id=1, source_target_pairs={{0,8},{8,0},{16,24},{24,16},{32,40},{40,32},{48,56},{56,48},{64,72... | collective-permute-start | bytes 1572872 | tf_op jit(solution)/shard_map/ppermute | solution.py:33
  38.1 3.3 %copy-start.4 = (bf16[32,128,256]{2,1,0:T(8,128)(2,1)S(1)}, bf16[32,128,256]{2,1,0:T(8,128)(2,1)}, u32[]{:S(2)}) copy-start(bf16[32,128,256]{2,1,0:T(8,128)(2,1)} %copy-done.3) | copy-start | bytes 6291460
  45.8 13.9 %collective-permute-start.9 = (bf16[5,16,16,128]{3,2,1,0:T(8,128)(2,1)S(1)}, bf16[5,16,16,128]{3,2,1,0:T(8,128)(2,1)S(1)}, u32[]{:S(2)}, u32[]{:S(2)}) collective-permute-start(bf16[5,16,16,128]{3,2,1,0:T(8,128)(2,1)S(1)} %get-tuple-element.40), channel_id=1, source_target_pairs={{0,1},{1,2},{2,3},{3,4},{4,5},{5,6},{6,7},{7,0},{8,9},{9,10},{10,1... | collective-permute-start | bytes 983048 | tf_op jit(solution)/shard_map/ppermute | solution.py:380
  47.8 12.0 %collective-permute-start.10 = (bf16[5,16,16,128]{3,2,1,0:T(8,128)(2,1)S(1)}, bf16[5,16,16,128]{3,2,1,0:T(8,128)(2,1)S(1)}, u32[]{:S(2)}, u32[]{:S(2)}) collective-permute-start(bf16[5,16,16,128]{3,2,1,0:T(8,128)(2,1)S(1)} %get-tuple-element.41), channel_id=1, source_target_pairs={{0,7},{1,0},{2,1},{3,2},{4,3},{5,4},{6,5},{7,6},{8,15},{9,8},{10,9... | collective-permute-start | bytes 983048 | tf_op jit(solution)/shard_map/ppermute | solution.py:380
  59.9 12.0 %collective-permute-start.11 = (bf16[2,16,16,128]{3,2,1,0:T(8,128)(2,1)S(1)}, bf16[2,16,16,128]{3,2,1,0:T(8,128)(2,1)S(1)}, u32[]{:S(2)}, u32[]{:S(2)}) collective-permute-start(bf16[2,16,16,128]{3,2,1,0:T(8,128)(2,1)S(1)} %get-tuple-element.43), channel_id=1, source_target_pairs={{0,5},{1,6},{2,7},{3,0},{4,1},{5,2},{6,3},{7,4},{8,13},{9,14},{10,... | collective-permute-start | bytes 393224 | tf_op jit(solution)/shard_map/ppermute | solution.py:380
  63.3 10.9 %collective-permute-start.12 = (bf16[2,16,16,128]{3,2,1,0:T(8,128)(2,1)S(1)}, bf16[2,16,16,128]{3,2,1,0:T(8,128)(2,1)S(1)}, u32[]{:S(2)}, u32[]{:S(2)}) collective-permute-start(bf16[2,16,16,128]{3,2,1,0:T(8,128)(2,1)S(1)} %get-tuple-element.44), channel_id=1, source_target_pairs={{0,3},{1,4},{2,5},{3,6},{4,7},{5,0},{6,1},{7,2},{8,11},{9,12},{10,... | collective-permute-start | bytes 393224 | tf_op jit(solution)/shard_map/ppermute | solution.py:380

commit v5 on v4

--- a/solution.py
+++ b/solution.py
@@ -61,16 +61,30 @@
     whiten_into(own_ref, windows_of(out_ref))
 
 
+def lay(refs, out_ref, sem):
+    copies = []
+    at = 0
+    for n, ref in enumerate(refs):
+        copies.append(pltpu.make_async_copy(ref, out_ref.at[pl.ds(at, ref.shape[0])], sem.at[n]))
+        copies[-1].start()
+        at += ref.shape[0]
+    return copies, at
+
+
 def gather_kernel(own_ref, sib_ref, *refs):
     windows = own_ref.shape[0]
-    *in_refs, raw_ref, _, near_ref = refs[:-windows]
-    out_refs = refs[-windows:]
+    *in_refs, raw_ref, _, near_ref = refs[: -windows - 1]
+    out_refs, sem = refs[-windows - 1 : -1], refs[-1]
+    copies = []
+    for v in range(windows):
+        parts = (own_ref.at[v], sib_ref.at[v], *in_refs[v::windows])
+        more, at = lay(parts, near_ref.at[v], sem.at[v])
+        copies += more
     whiten_into(raw_ref, out_refs)
     for v in range(windows):
-        at = 0
-        for ref in (own_ref.at[v], sib_ref.at[v], *in_refs[v::windows], out_refs[v]):
-            near_ref[v, pl.ds(at, ref.shape[0])] = ref[...]
-            at += ref.shape[0]
+        near_ref[v, pl.ds(at, raw_ref.shape[1])] = out_refs[v][...]
+    for copy in copies:
+        copy.wait()
 
 
 def forward_kernel(order_ref, raw_ref, _, *refs):
@@ -85,12 +99,13 @@
 
 
 def late_kernel(*refs):
-    *swapped_refs, head_ref, tail_ref, out_ref = refs
+    *swapped_refs, head_ref, tail_ref, out_ref, sem = refs
+    copies = []
     for v in range(out_ref.shape[0]):
-        at = 0
-        for ref in (swapped_refs[v], head_ref.at[v], tail_ref.at[v]):
-            out_ref[v, pl.ds(at, ref.shape[0])] = ref[...]
-            at += ref.shape[0]
+        parts = (swapped_refs[v], head_ref.at[v], tail_ref.at[v])
+        copies += lay(parts, out_ref.at[v], sem.at[v])[0]
+    for copy in copies:
+        copy.wait()
 
 
 def corr_kernel(
@@ -328,16 +343,18 @@
             jax.ShapeDtypeStruct((win_dev, 5 * ch_dev, rows, LANES), BF),
         ]
         + [jax.ShapeDtypeStruct(x.shape[1:], BF)] * win_dev,
-        in_specs=[VM] * (3 + 2 * win_dev) + [ANY],
+        in_specs=[ANY] * (2 + 2 * win_dev) + [VM, ANY],
         out_specs=[VM] * (1 + win_dev),
+        scratch_shapes=[pltpu.SemaphoreType.DMA((win_dev, 4))],
         compiler_params=pltpu.CompilerParams(vmem_limit_bytes=24 << 20),
         cost_estimate=pl.CostEstimate(flops=0, bytes_accessed=0, transcendentals=0),
     )(own, sib, *ahead, *[swap(a) for a in ahead], back, tail)
     late = pl.pallas_call(
         late_kernel,
         out_shape=jax.ShapeDtypeStruct((win_dev, 2 * ch_dev, rows, LANES), BF),
-        in_specs=[VM] * (win_dev + 2),
+        in_specs=[ANY] * (win_dev + 2),
         out_specs=VM,
+        scratch_shapes=[pltpu.SemaphoreType.DMA((win_dev, 3))],
         compiler_params=pltpu.CompilerParams(vmem_limit_bytes=16 << 20),
         cost_estimate=pl.CostEstimate(
             flops=20 << 30, bytes_accessed=0, transcendentals=0

time: 76.5 us -> 76.4 us (level)
  the two profiles are of different devices: /device:TPU:6 before, /device:TPU:61 now
where the time goes in v5:
time: 76.4 us; the launch traced here: 76 us
  waiting for transfers between devices  28.8 us (38%)
  starting transfers between devices  19.5 us (26%)
  Pallas kernels  16.5 us (22%)
  local copies, waits for them, and re-layouts  6.27 us (8%)
  other arithmetic  3.3 us (4%)
  between operations  1.56 us (2%)
    ppermute x4, waiting for transfers between devices, along(): lax.ppermute(value, 'win', [(i, (i + step) % win_count) for i in range(wi...  22.3 us
    ppermute x3, starting transfers between devices, moved(): lax.ppermute(value, 'pair', [(a, b) for a, b in pairs if 0 <= b < count])  7.17 us
    ppermute x4, starting transfers between devices, along(): lax.ppermute(value, 'win', [(i, (i + step) % win_count) for i in range(wi...  6.74 us
    ppermute x3, waiting for transfers between devices, moved(): lax.ppermute(value, 'pair', [(a, b) for a, b in pairs if 0 <= b < count])  6.53 us
    ppermute x5, starting transfers between devices, swap(): return lax.ppermute(value, 'pair', [(i, i ^ 1) for i in range(count)])  5.61 us
    unnamed x12, local copies, waits for them, and re-layouts  4.77 us
    pallas_call x1, Pallas kernels, local(): pl.pallas_call(corr_kernel, out_shape=[jax.ShapeDtypeStruct((6, half, wid...  4.36 us
    pallas_call x1, Pallas kernels, local(): pl.pallas_call(table_kernel, out_shape=[jax.ShapeDtypeStruct((2 * LOW * G...  3.32 us
  transfers between devices with their start and end apart: 12, of which 6 were waited for; matrix products, arithmetic and copies ran while one was open for 6% of the time, Pallas kernels for 13%

profile of v5, /device:TPU:61, one launch (start us, length us, event | category | flops | bytes accessed | tf_op | source)
XLA Modules:
  0.0 76.0 jit_solution(4709096755318637178)
XLA Ops:
  0.7 2.5 %collective-permute-start.2 = (bf16[2,64,32,128]{3,2,1,0:T(8,128)(2,1)}, bf16[2,64,32,128]{3,2,1,0:T(8,128)(2,1)S(1)}, u32[]{:S(2)}, u32[]{:S(2)}) collective-permute-start(bf16[2,64,32,128]{3,2,1,0:T(8,128)(2,1)} %bitcast.33), channel_id=1, source_target_pairs={{8,24},{16,0},{24,40},{32,16},{40,56},{48,32},{56,72},{64,48},{72,... | collective-permute-start | bytes 3145736 | tf_op jit(solution)/shard_map/ppermute | solution.py:28
  3.2 0.9 %compare_select_fusion = s32[32,128,1]{1,2,0:T(1,128)S(1)} fusion(s32[32,128,2]{1,2,0:T(2,128)} %param.8, s32[32]{0:T(128)S(1)} %fusion.5), kind=kLoop, calls=%fused_computation.4 | loop fusion | flops 94208 | bytes 32896 | tf_op jit(solution)/shard_map/jit(_where)/select_n | solution.py:269
  5.7 1.2 %copy-done.2 = bf16[2,64,2,2048]{3,2,1,0:T(2,128)(2,1)S(1)} copy-done((bf16[2,64,2,2048]{3,2,1,0:T(2,128)(2,1)S(1)}, bf16[2,64,2,2048]{3,2,1,0:T(2,128)(2,1)}, u32[]{:S(2)}) %copy-start.2) | copy-done | bytes 1048600
  6.9 2.4 %shard_map.46 = (bf16[2,64,32,128]{3,2,1,0:T(8,128)(2,1)}, bf16[2,64,32,128]{3,2,1,0:T(8,128)(2,1)S(1)}) custom-call(bf16[2,64,32,128]{3,2,1,0:T(8,128)(2,1)S(1)} %bitcast.34, s32[64]{0:T(128)S(1)} %select_reduce_fusion._.order_ref), custom_call_target="tpu_custom_call" | custom-call | flops 1073741824 | bytes 2097152 | tf_op jit(solution)/shard_map/pallas_call | solution.py:297
  9.4 2.8 %collective-permute-start.5 = (bf16[2,64,32,128]{3,2,1,0:T(8,128)(2,1)}, bf16[2,64,32,128]{3,2,1,0:T(8,128)(2,1)S(1)}, u32[]{:S(2)}, u32[]{:S(2)}) collective-permute-start(bf16[2,64,32,128]{3,2,1,0:T(8,128)(2,1)} %get-tuple-element.32), channel_id=1, source_target_pairs={{0,16},{16,32},{24,8},{32,48},{40,24},{48,64},{56,40},{64,80},{72,... | collective-permute-start | bytes 3145736 | tf_op jit(solution)/shard_map/ppermute | solution.py:28
  12.2 3.3 %shard_map.47 = (bf16[512,256]{1,0:T(8,128)(2,1)S(1)}, bf16[32,128,256]{2,1,0:T(8,128)(2,1)S(1)}, bf16[2,64,32,128]{3,2,1,0:T(8,128)(2,1)S(1)}) custom-call(bf16[2,64,32,128]{3,2,1,0:T(8,128)(2,1)} %collective-permute-done.1.sib_ref, bf16[2,64,32,128]{3,2,1,0:T(8,128)(2,1)S(1)} %get-tuple-element.27._.own_ref), custom_call_target="tpu_custom_call" | custom-call | flops 1073741824 | bytes 2097152 | tf_op jit(solution)/shard_map/pallas_call | solution.py:307
  15.5 1.0 %copy-done = bf16[2,64,32,128]{3,2,1,0:T(8,128)(2,1)} copy-done((bf16[2,64,32,128]{3,2,1,0:T(8,128)(2,1)}, bf16[2,64,32,128]{3,2,1,0:T(8,128)(2,1)S(1)}, u32[]{:S(2)}) %copy-start) | copy-done | bytes 1048600
  16.5 1.3 %copy-done.3 = bf16[32,128,256]{2,1,0:T(8,128)(2,1)} copy-done((bf16[32,128,256]{2,1,0:T(8,128)(2,1)}, bf16[32,128,256]{2,1,0:T(8,128)(2,1)S(1)}, u32[]{:S(2)}) %copy-start.3) | copy-done | bytes 2097176
  18.6 2.6 %shard_map.48 = (bf16[64,32,128]{2,1,0:T(8,128)(2,1)}, bf16[64,32,128]{2,1,0:T(8,128)(2,1)}, bf16[2,40,32,128]{3,2,1,0:T(8,128)(2,1)}, bf16[2,24,32,128]{3,2,1,0:T(8,128)(2,1)}) custom-call(s32[64]{0:T(128)S(1)} %select_reduce_fusion._.order_ref, bf16[2,64,32,128]{3,2,1,0:T(8,128)(2,1)S(1)} %collective-permute-done.2.raw_ref, ...), custom_call_target="tpu_custom_call" | custom-call | tf_op jit(solution)/shard_map/pallas_call | solution.py:322
  21.2 4.1 %collective-permute-start.3 = (bf16[64,32,128]{2,1,0:T(8,128)(2,1)}, bf16[64,32,128]{2,1,0:T(8,128)(2,1)S(1)}, u32[]{:S(2)}, u32[]{:S(2)}) collective-permute-start(bf16[64,32,128]{2,1,0:T(8,128)(2,1)} %get-tuple-element.30.refs_0_), channel_id=1, source_target_pairs={{0,8},{8,0},{16,24},{24,16},{32,40},{40,32},{48,56},{56,48},{64,72... | collective-permute-start | bytes 1572872 | tf_op jit(solution)/shard_map/ppermute | solution.py:33
  25.9 1.9 %collective-permute-start.8 = (bf16[2,40,32,128]{3,2,1,0:T(8,128)(2,1)}, bf16[2,40,32,128]{3,2,1,0:T(8,128)(2,1)}, u32[]{:S(2)}, u32[]{:S(2)}) collective-permute-start(bf16[2,40,32,128]{3,2,1,0:T(8,128)(2,1)} %get-tuple-element.37), channel_id=1, source_target_pairs={{8,16},{16,8},{24,32},{32,24},{40,48},{48,40},{56,64},{64,56},{72,... | collective-permute-start | bytes 1966088 | tf_op jit(solution)/shard_map/ppermute | solution.py:28
  29.9 0.8 %conditional.1 = (bf16[2,24,32,128]{3,2,1,0:T(8,128)(2,1)}) conditional(s32[]{:T(128)} %convert_element_type.11, () %tuple.11, bf16[2,24,32,128]{3,2,1,0:T(8,128)(2,1)} %get-tuple-element.33), branch_computations={%region_6.7_spmd, %region_7.8_spmd} | conditional | bytes 1572912 | solution.py:339
  30.8 1.2 %copy-done.1 = bf16[2,64,32,128]{3,2,1,0:T(8,128)(2,1)S(1)} copy-done((bf16[2,64,32,128]{3,2,1,0:T(8,128)(2,1)S(1)}, bf16[2,64,32,128]{3,2,1,0:T(8,128)(2,1)}, u32[]{:S(2)}) %copy-start.1) | copy-done | bytes 1048600
  32.0 1.5 %shard_map.49 = (bf16[2,320,32,128]{3,2,1,0:T(8,128)(2,1)S(1)}, bf16[64,32,128]{2,1,0:T(8,128)(2,1)S(1)}, bf16[64,32,128]{2,1,0:T(8,128)(2,1)S(1)}) custom-call(bf16[2,64,32,128]{3,2,1,0:T(8,128)(2,1)S(1)} %get-tuple-element.27._.own_ref, bf16[2,64,32,128]{3,2,1,0:T(8,128)(2,1)S(1)} %copy-done.1, bf16[64,32,128]{2,1,0:T(8,128)(2,1)} %get-tuple-element.30.refs_0_, ...), custom_call_target="tpu_custom_call" | custom-call | tf_op jit(solution)/shard_map/pallas_call | solution.py:340
  34.5 5.8 %collective-permute-done.8.refs_2_ = bf16[2,40,32,128]{3,2,1,0:T(8,128)(2,1)} collective-permute-done((bf16[2,40,32,128]{3,2,1,0:T(8,128)(2,1)}, bf16[2,40,32,128]{3,2,1,0:T(8,128)(2,1)}, u32[]{:S(2)}, u32[]{:S(2)}) %collective-permute-start.8) | collective-permute-done | bytes 655392 | tf_op jit(solution)/shard_map/ppermute | solution.py:28
  40.3 1.3 %shard_map.50.late_ref = bf16[2,128,32,128]{3,2,1,0:T(8,128)(2,1)S(1)} custom-call(bf16[64,32,128]{2,1,0:T(8,128)(2,1)S(1)} %collective-permute-done.6.refs_0_, bf16[64,32,128]{2,1,0:T(8,128)(2,1)S(1)} %collective-permute-done.7.refs_1_, bf16[2,40,32,128]{3,2,1,0:T(8,128)(2,1)} %collective-permute-done.8.refs_2_, ...), custom_call_target="tpu_custom_call" | custom-call | flops 21474836480 | tf_op jit(solution)/shard_map/pallas_call | solution.py:352
  41.6 4.4 %shard_map.51 = (f32[6,16,16,128]{3,2,1,0:T(8,128)S(1)}, bf16[5,16,16,128]{3,2,1,0:T(8,128)(2,1)S(1)}, bf16[5,16,16,128]{3,2,1,0:T(8,128)(2,1)S(1)}) custom-call(s32[128]{0:T(128)S(1)} %get-tuple-element.48.first_ref, s32[128]{0:T(128)S(1)} %get-tuple-element.47.second_ref, s32[1]{0:T(128)S(6)} %copy.9.live_ref, s32[1]{0:T(128)} %bitcast.6.z_ref, ...), custom_call_target="tpu_custom_call" | custom-call | flops 8589934592 | bytes 8388608 | tf_op jit(solution)/shard_map/pallas_call | solution.py:380
  46.0 1.7 %collective-permute-start.9 = (bf16[5,16,16,128]{3,2,1,0:T(8,128)(2,1)S(1)}, bf16[5,16,16,128]{3,2,1,0:T(8,128)(2,1)S(1)}, u32[]{:S(2)}, u32[]{:S(2)}) collective-permute-start(bf16[5,16,16,128]{3,2,1,0:T(8,128)(2,1)S(1)} %get-tuple-element.40), channel_id=1, source_target_pairs={{0,1},{1,2},{2,3},{3,4},{4,5},{5,6},{6,7},{7,0},{8,9},{9,10},{10,1... | collective-permute-start | bytes 983048 | tf_op jit(solution)/shard_map/ppermute | solution.py:397
  47.7 6.9 %collective-permute-done.9.left_ref = bf16[5,16,16,128]{3,2,1,0:T(8,128)(2,1)S(1)} collective-permute-done((bf16[5,16,16,128]{3,2,1,0:T(8,128)(2,1)S(1)}, bf16[5,16,16,128]{3,2,1,0:T(8,128)(2,1)S(1)}, u32[]{:S(2)}, u32[]{:S(2)}) %collective-permute-start.9) | collective-permute-done | bytes 327712 | tf_op jit(solution)/shard_map/ppermute | solution.py:397
  54.6 1.6 %collective-permute-done.10.right_ref = bf16[5,16,16,128]{3,2,1,0:T(8,128)(2,1)S(1)} collective-permute-done((bf16[5,16,16,128]{3,2,1,0:T(8,128)(2,1)S(1)}, bf16[5,16,16,128]{3,2,1,0:T(8,128)(2,1)S(1)}, u32[]{:S(2)}, u32[]{:S(2)}) %collective-permute-start.10) | collective-permute-done | bytes 327712 | tf_op jit(solution)/shard_map/ppermute | solution.py:397
  56.4 4.7 %collective-permute-start.11 = (bf16[2,16,16,128]{3,2,1,0:T(8,128)(2,1)S(1)}, bf16[2,16,16,128]{3,2,1,0:T(8,128)(2,1)S(1)}, u32[]{:S(2)}, u32[]{:S(2)}) collective-permute-start(bf16[2,16,16,128]{3,2,1,0:T(8,128)(2,1)S(1)} %get-tuple-element.43), channel_id=1, source_target_pairs={{0,5},{1,6},{2,7},{3,0},{4,1},{5,2},{6,3},{7,4},{8,13},{9,14},{10,... | collective-permute-start | bytes 393224 | tf_op jit(solution)/shard_map/ppermute | solution.py:397
  61.4 4.7 %collective-permute-done.11.refs_0_ = bf16[2,16,16,128]{3,2,1,0:T(8,128)(2,1)S(1)} collective-permute-done((bf16[2,16,16,128]{3,2,1,0:T(8,128)(2,1)S(1)}, bf16[2,16,16,128]{3,2,1,0:T(8,128)(2,1)S(1)}, u32[]{:S(2)}, u32[]{:S(2)}) %collective-permute-start.11) | collective-permute-done | bytes 131104 | tf_op jit(solution)/shard_map/ppermute | solution.py:397
  66.1 9.0 %collective-permute-done.12.refs_1_ = bf16[2,16,16,128]{3,2,1,0:T(8,128)(2,1)S(1)} collective-permute-done((bf16[2,16,16,128]{3,2,1,0:T(8,128)(2,1)S(1)}, bf16[2,16,16,128]{3,2,1,0:T(8,128)(2,1)S(1)}, u32[]{:S(2)}, u32[]{:S(2)}) %collective-permute-start.12) | collective-permute-done | bytes 131104 | tf_op jit(solution)/shard_map/ppermute | solution.py:397
  75.1 0.9 %shard_map.53 = f32[128,512]{1,0:T(8,128)} custom-call(f32[2,16,16,128]{3,2,1,0:T(8,128)S(1)} %get-tuple-element.42.own_ref, bf16[2,16,16,128]{3,2,1,0:T(8,128)(2,1)S(1)} %collective-permute-done.11.refs_0_, bf16[2,16,16,128]{3,2,1,0:T(8,128)(2,1)S(1)} %collective-permute-done.12.refs_1_), custom_call_target="tpu_custom_call" | custom-call | tf_op jit(solution)/shard_map/pallas_call | solution.py:409
  (37 shorter events, 6.6 us)
Async XLA Ops:
  0.0 12.2 %collective-permute-start.1 = (bf16[2,64,32,128]{3,2,1,0:T(8,128)(2,1)}, bf16[2,64,32,128]{3,2,1,0:T(8,128)(2,1)}, u32[]{:S(2)}, u32[]{:S(2)}) collective-permute-start(bf16[2,64,32,128]{3,2,1,0:T(8,128)(2,1)} %bitcast.32), channel_id=1, source_target_pairs={{0,8},{8,0},{16,24},{24,16},{32,40},{40,32},{48,56},{56,48},{64,72... | collective-permute-start | bytes 3145736 | tf_op jit(solution)/shard_map/ppermute | solution.py:33
  0.7 17.9 %collective-permute-start.2 = (bf16[2,64,32,128]{3,2,1,0:T(8,128)(2,1)}, bf16[2,64,32,128]{3,2,1,0:T(8,128)(2,1)S(1)}, u32[]{:S(2)}, u32[]{:S(2)}) collective-permute-start(bf16[2,64,32,128]{3,2,1,0:T(8,128)(2,1)} %bitcast.33), channel_id=1, source_target_pairs={{8,24},{16,0},{24,40},{32,16},{40,56},{48,32},{56,72},{64,48},{72,... | collective-permute-start | bytes 3145736 | tf_op jit(solution)/shard_map/ppermute | solution.py:28
  5.7 1.2 %copy-start.2 = (bf16[2,64,2,2048]{3,2,1,0:T(2,128)(2,1)S(1)}, bf16[2,64,2,2048]{3,2,1,0:T(2,128)(2,1)}, u32[]{:S(2)}) copy-start(bf16[2,64,2,2048]{3,2,1,0:T(2,128)(2,1)} %param.6) | copy-start | bytes 3145732
  9.4 21.4 %collective-permute-start.5 = (bf16[2,64,32,128]{3,2,1,0:T(8,128)(2,1)}, bf16[2,64,32,128]{3,2,1,0:T(8,128)(2,1)S(1)}, u32[]{:S(2)}, u32[]{:S(2)}) collective-permute-start(bf16[2,64,32,128]{3,2,1,0:T(8,128)(2,1)} %get-tuple-element.32), channel_id=1, source_target_pairs={{0,16},{16,32},{24,8},{32,48},{40,24},{48,64},{56,40},{64,80},{72,... | collective-permute-start | bytes 3145736 | tf_op jit(solution)/shard_map/ppermute | solution.py:28
  15.5 1.0 %copy-start = (bf16[2,64,32,128]{3,2,1,0:T(8,128)(2,1)}, bf16[2,64,32,128]{3,2,1,0:T(8,128)(2,1)S(1)}, u32[]{:S(2)}) copy-start(bf16[2,64,32,128]{3,2,1,0:T(8,128)(2,1)S(1)} %get-tuple-element.28.sib_ref) | copy-start | bytes 3145732
  16.5 1.3 %copy-start.3 = (bf16[32,128,256]{2,1,0:T(8,128)(2,1)}, bf16[32,128,256]{2,1,0:T(8,128)(2,1)S(1)}, u32[]{:S(2)}) copy-start(bf16[32,128,256]{2,1,0:T(8,128)(2,1)S(1)} %get-tuple-element.38.wave_ref) | copy-start | bytes 6291460
  21.2 9.6 %collective-permute-start.3 = (bf16[64,32,128]{2,1,0:T(8,128)(2,1)}, bf16[64,32,128]{2,1,0:T(8,128)(2,1)S(1)}, u32[]{:S(2)}, u32[]{:S(2)}) collective-permute-start(bf16[64,32,128]{2,1,0:T(8,128)(2,1)} %get-tuple-element.30.refs_0_), channel_id=1, source_target_pairs={{0,8},{8,0},{16,24},{24,16},{32,40},{40,32},{48,56},{56,48},{64,72... | collective-permute-start | bytes 1572872 | tf_op jit(solution)/shard_map/ppermute | solution.py:33
  25.3 5.5 %collective-permute-start.4 = (bf16[64,32,128]{2,1,0:T(8,128)(2,1)}, bf16[64,32,128]{2,1,0:T(8,128)(2,1)S(1)}, u32[]{:S(2)}, u32[]{:S(2)}) collective-permute-start(bf16[64,32,128]{2,1,0:T(8,128)(2,1)} %get-tuple-element.31.refs_1_), channel_id=1, source_target_pairs={{0,8},{8,0},{16,24},{24,16},{32,40},{40,32},{48,56},{56,48},{64,72... | collective-permute-start | bytes 1572872 | tf_op jit(solution)/shard_map/ppermute | solution.py:33
  25.9 14.3 %collective-permute-start.8 = (bf16[2,40,32,128]{3,2,1,0:T(8,128)(2,1)}, bf16[2,40,32,128]{3,2,1,0:T(8,128)(2,1)}, u32[]{:S(2)}, u32[]{:S(2)}) collective-permute-start(bf16[2,40,32,128]{3,2,1,0:T(8,128)(2,1)} %get-tuple-element.37), channel_id=1, source_target_pairs={{8,16},{16,8},{24,32},{32,24},{40,48},{48,40},{56,64},{64,56},{72,... | collective-permute-start | bytes 1966088 | tf_op jit(solution)/shard_map/ppermute | solution.py:28
  30.8 1.2 %copy-start.1 = (bf16[2,64,32,128]{3,2,1,0:T(8,128)(2,1)S(1)}, bf16[2,64,32,128]{3,2,1,0:T(8,128)(2,1)}, u32[]{:S(2)}) copy-start(bf16[2,64,32,128]{3,2,1,0:T(8,128)(2,1)} %copy-done) | copy-start | bytes 3145732
  32.0 2.5 %copy-start.5 = (f32[2048]{0:T(1024)S(1)}, f32[2048]{0:T(1024)}, u32[]{:S(2)}) copy-start(f32[2048]{0:T(1024)} %param.7) | copy-start | bytes 24580
  33.5 6.8 %collective-permute-start.6 = (bf16[64,32,128]{2,1,0:T(8,128)(2,1)S(1)}, bf16[64,32,128]{2,1,0:T(8,128)(2,1)S(1)}, u32[]{:S(2)}, u32[]{:S(2)}) collective-permute-start(bf16[64,32,128]{2,1,0:T(8,128)(2,1)S(1)} %get-tuple-element.35), channel_id=1, source_target_pairs={{0,8},{8,0},{16,24},{24,16},{32,40},{40,32},{48,56},{56,48},{64,72... | collective-permute-start | bytes 1572872 | tf_op jit(solution)/shard_map/ppermute | solution.py:33
  34.1 6.2 %collective-permute-start.7 = (bf16[64,32,128]{2,1,0:T(8,128)(2,1)S(1)}, bf16[64,32,128]{2,1,0:T(8,128)(2,1)S(1)}, u32[]{:S(2)}, u32[]{:S(2)}) collective-permute-start(bf16[64,32,128]{2,1,0:T(8,128)(2,1)S(1)} %get-tuple-element.36), channel_id=1, source_target_pairs={{0,8},{8,0},{16,24},{24,16},{32,40},{40,32},{48,56},{56,48},{64,72... | collective-permute-start | bytes 1572872 | tf_op jit(solution)/shard_map/ppermute | solution.py:33
  34.5 7.1 %copy-start.4 = (bf16[32,128,256]{2,1,0:T(8,128)(2,1)S(1)}, bf16[32,128,256]{2,1,0:T(8,128)(2,1)}, u32[]{:S(2)}) copy-start(bf16[32,128,256]{2,1,0:T(8,128)(2,1)} %copy-done.3) | copy-start | bytes 6291460
  46.0 8.7 %collective-permute-start.9 = (bf16[5,16,16,128]{3,2,1,0:T(8,128)(2,1)S(1)}, bf16[5,16,16,128]{3,2,1,0:T(8,128)(2,1)S(1)}, u32[]{:S(2)}, u32[]{:S(2)}) collective-permute-start(bf16[5,16,16,128]{3,2,1,0:T(8,128)(2,1)S(1)} %get-tuple-element.40), channel_id=1, source_target_pairs={{0,1},{1,2},{2,3},{3,4},{4,5},{5,6},{6,7},{7,0},{8,9},{9,10},{10,1... | collective-permute-start | bytes 983048 | tf_op jit(solution)/shard_map/ppermute | solution.py:397
  47.7 8.6 %collective-permute-start.10 = (bf16[5,16,16,128]{3,2,1,0:T(8,128)(2,1)S(1)}, bf16[5,16,16,128]{3,2,1,0:T(8,128)(2,1)S(1)}, u32[]{:S(2)}, u32[]{:S(2)}) collective-permute-start(bf16[5,16,16,128]{3,2,1,0:T(8,128)(2,1)S(1)} %get-tuple-element.41), channel_id=1, source_target_pairs={{0,7},{1,0},{2,1},{3,2},{4,3},{5,4},{6,5},{7,6},{8,15},{9,8},{10,9... | collective-permute-start | bytes 983048 | tf_op jit(solution)/shard_map/ppermute | solution.py:397
  56.4 9.7 %collective-permute-start.11 = (bf16[2,16,16,128]{3,2,1,0:T(8,128)(2,1)S(1)}, bf16[2,16,16,128]{3,2,1,0:T(8,128)(2,1)S(1)}, u32[]{:S(2)}, u32[]{:S(2)}) collective-permute-start(bf16[2,16,16,128]{3,2,1,0:T(8,128)(2,1)S(1)} %get-tuple-element.43), channel_id=1, source_target_pairs={{0,5},{1,6},{2,7},{3,0},{4,1},{5,2},{6,3},{7,4},{8,13},{9,14},{10,... | collective-permute-start | bytes 393224 | tf_op jit(solution)/shard_map/ppermute | solution.py:397
  61.1 14.0 %collective-permute-start.12 = (bf16[2,16,16,128]{3,2,1,0:T(8,128)(2,1)S(1)}, bf16[2,16,16,128]{3,2,1,0:T(8,128)(2,1)S(1)}, u32[]{:S(2)}, u32[]{:S(2)}) collective-permute-start(bf16[2,16,16,128]{3,2,1,0:T(8,128)(2,1)S(1)} %get-tuple-element.44), channel_id=1, source_target_pairs={{0,3},{1,4},{2,5},{3,6},{4,7},{5,0},{6,1},{7,2},{8,11},{9,12},{10,... | collective-permute-start | bytes 393224 | tf_op jit(solution)/shard_map/ppermute | solution.py:397

commit v6 on v5

--- a/solution.py
+++ b/solution.py
@@ -229,7 +229,7 @@
         out_ref[:, pl.ds(g * LANES, LANES)] = jnp.concatenate(rows, axis=0).T
 
 
-def table_kernel(sib_ref, _, fold_ref, wave_ref, sib_out_ref):
+def table_kernel(sib_ref, _own, _first, _second, fold_ref, wave_ref, sib_out_ref):
     def turns(rows, cols, period):
         r = lax.broadcasted_iota(jnp.int32, (rows, cols), 0)
         c = lax.broadcasted_iota(jnp.int32, (rows, cols), 1)
@@ -291,6 +291,17 @@
     channel = jnp.arange(ch_dev, dtype=jnp.int32)
     order = lax.dynamic_index_in_dim(place, target, 0, keepdims=False)
     order = jnp.sum(jnp.where(order[None, :] == channel[:, None], channel[None, :], 0), axis=1)
+
+    ends = lax.dynamic_index_in_dim(pair_ends, me, 0, keepdims=False)
+    first = ends[:, 0] % ch_dev
+    away = (ends[:, 1] // ch_dev - me) * (1 - 2 * odd)
+    row = ends[:, 1] % ch_dev
+    mine = lax.dynamic_index_in_dim(place, me, 0, keepdims=False)
+    mine = jnp.sum(jnp.where(row[:, None] == channel[None, :], mine[None, :], 0), axis=1)
+    row = jnp.where(away == -HALF, mine, row)
+    second = jnp.zeros_like(away)
+    for n, d in enumerate((0, 1, 2, -1, -2, 3, -3)):
+        second = jnp.where(away == d, n * ch_dev + row, second)
 
     ahead = moved(x, lambda i: i - 2 if i % 2 == 0 else i + 2)
     sib = swap(x)
@@ -311,13 +322,13 @@
             jax.ShapeDtypeStruct((LOW, LANES, 2 * LANES), BF),
             jax.ShapeDtypeStruct(x.shape, BF),
         ],
-        in_specs=[VM, ANY],
+        in_specs=[VM, ANY, SM, SM],
         out_specs=[VM] * 3,
         compiler_params=pltpu.CompilerParams(vmem_limit_bytes=16 << 20),
         cost_estimate=pl.CostEstimate(
             flops=1 << 30, bytes_accessed=2 << 20, transcendentals=0
         ),
-    )(sib, own)
+    )(sib, own, first, second)
     back = moved(again, lambda i: i + 2 if i % 2 == 0 else i - 2)
     *ahead, head, tail = pl.pallas_call(
         forward_kernel,
@@ -361,17 +372,6 @@
         ),
     )(*[swap(b) for b in back], head, tail)
 
-    ends = lax.dynamic_index_in_dim(pair_ends, me, 0, keepdims=False)
-    first = ends[:, 0] % ch_dev
-    away = (ends[:, 1] // ch_dev - me) * (1 - 2 * odd)
-    row = ends[:, 1] % ch_dev
-    mine = lax.dynamic_index_in_dim(place, me, 0, keepdims=False)
-    mine = jnp.sum(jnp.where(row[:, None] == channel[None, :], mine[None, :], 0), axis=1)
-    row = jnp.where(away == -HALF, mine, row)
-    second = jnp.zeros_like(away)
-    for n, d in enumerate((0, 1, 2, -1, -2, 3, -3)):
-        second = jnp.where(away == d, n * ch_dev + row, second)
-
     factor = jnp.where(jnp.arange(bins) == 0, 1.0, 2.0).astype(F32)
     weight = (passband * factor).reshape(SUBS, LANES)
 

time: 76.4 us -> 78.2 us (1.024)
  the two profiles are of different devices: /device:TPU:61 before, /device:TPU:6 now
where the time goes in v6:
time: 78.2 us; the launch traced here: 77.8 us
  starting transfers between devices  24 us (31%)
  waiting for transfers between devices  22.5 us (29%)
  Pallas kernels  18 us (23%)
  local copies, waits for them, and re-layouts  8.6 us (11%)
  other arithmetic  3.24 us (4%)
  between operations  1.54 us (2%)
    ppermute x4, waiting for transfers between devices, along(): lax.ppermute(value, 'win', [(i, (i + step) % win_count) for i in range(wi...  19.8 us
    ppermute x3, starting transfers between devices, moved(): lax.ppermute(value, 'pair', [(a, b) for a, b in pairs if 0 <= b < count])  13.1 us
    ppermute x4, starting transfers between devices, along(): lax.ppermute(value, 'win', [(i, (i + step) % win_count) for i in range(wi...  9.85 us
    unnamed x18, local copies, waits for them, and re-layouts  7.1 us
    pallas_call x1, Pallas kernels, local(): pl.pallas_call(corr_kernel, out_shape=[jax.ShapeDtypeStruct((6, half, wid...  4.43 us
    pallas_call x1, Pallas kernels, local(): pl.pallas_call(table_kernel, out_shape=[jax.ShapeDtypeStruct((2 * LOW * G...  3.31 us
    pallas_call x1, Pallas kernels, local(): pl.pallas_call(forward_kernel, out_shape=[jax.ShapeDtypeStruct(x.shape[1:...  2.67 us
    pallas_call x1, Pallas kernels, local(): pl.pallas_call(gather_kernel, out_shape=[jax.ShapeDtypeStruct((win_dev, 5...  2.43 us
  transfers between devices with their start and end apart: 12, of which 7 were waited for; matrix products, arithmetic and copies ran while one was open for 6% of the time, Pallas kernels for 14%

profile of v6, /device:TPU:6, one launch (start us, length us, event | category | flops | bytes accessed | tf_op | source)
XLA Modules:
  0.0 77.8 jit_solution(5288321098120307048)
XLA Ops:
  0.0 5.2 %collective-permute-start.2 = (bf16[2,64,32,128]{3,2,1,0:T(8,128)(2,1)}, bf16[2,64,32,128]{3,2,1,0:T(8,128)(2,1)S(1)}, u32[]{:S(2)}, u32[]{:S(2)}) collective-permute-start(bf16[2,64,32,128]{3,2,1,0:T(8,128)(2,1)} %bitcast.35), channel_id=1, source_target_pairs={{8,24},{16,0},{24,40},{32,16},{40,56},{48,32},{56,72},{64,48},{72,... | collective-permute-start | bytes 3145736 | tf_op jit(solution)/shard_map/ppermute | solution.py:28
  5.2 0.9 %compare_select_fusion = s32[32,128,1]{1,2,0:T(1,128)S(1)} fusion(s32[32,128,2]{1,2,0:T(2,128)} %param.8, s32[32]{0:T(128)S(1)} %fusion.5), kind=kLoop, calls=%fused_computation.4 | loop fusion | flops 94208 | bytes 32896 | tf_op jit(solution)/shard_map/jit(_where)/select_n | solution.py:269
  7.7 1.2 %copy-done.3 = bf16[2,64,2,2048]{3,2,1,0:T(2,128)(2,1)S(1)} copy-done((bf16[2,64,2,2048]{3,2,1,0:T(2,128)(2,1)S(1)}, bf16[2,64,2,2048]{3,2,1,0:T(2,128)(2,1)}, u32[]{:S(2)}) %copy-start.3) | copy-done | bytes 1048600
  8.9 2.4 %shard_map.46 = (bf16[2,64,32,128]{3,2,1,0:T(8,128)(2,1)}, bf16[2,64,32,128]{3,2,1,0:T(8,128)(2,1)S(1)}) custom-call(bf16[2,64,32,128]{3,2,1,0:T(8,128)(2,1)S(1)} %bitcast.36, s32[64]{0:T(128)S(1)} %select_reduce_fusion._.order_ref), custom_call_target="tpu_custom_call" | custom-call | flops 1073741824 | bytes 2097152 | tf_op jit(solution)/shard_map/pallas_call | solution.py:308
  11.4 1.9 %collective-permute-start.5 = (bf16[2,64,32,128]{3,2,1,0:T(8,128)(2,1)}, bf16[2,64,32,128]{3,2,1,0:T(8,128)(2,1)S(1)}, u32[]{:S(2)}, u32[]{:S(2)}) collective-permute-start(bf16[2,64,32,128]{3,2,1,0:T(8,128)(2,1)} %get-tuple-element.32), channel_id=1, source_target_pairs={{0,16},{16,32},{24,8},{32,48},{40,24},{48,64},{56,40},{64,80},{72,... | collective-permute-start | bytes 3145736 | tf_op jit(solution)/shard_map/ppermute | solution.py:28
  14.1 3.3 %shard_map.47 = (bf16[512,256]{1,0:T(8,128)(2,1)S(1)}, bf16[32,128,256]{2,1,0:T(8,128)(2,1)S(1)}, bf16[2,64,32,128]{3,2,1,0:T(8,128)(2,1)S(1)}) custom-call(bf16[2,64,32,128]{3,2,1,0:T(8,128)(2,1)} %collective-permute-done.1.sib_ref, bf16[2,64,32,128]{3,2,1,0:T(8,128)(2,1)S(1)} %get-tuple-element.27._own.own_ref, s32[128]{0:T(128)S(1)} %get-tuple-element.48._first.first_ref, ...), custom_call_target="tpu_custom_call" | custom-call | flops 1073741824 | bytes 2097152 | tf_op jit(solution)/shard_map/pallas_call | solution.py:318
  17.4 1.0 %copy-done = bf16[2,64,32,128]{3,2,1,0:T(8,128)(2,1)} copy-done((bf16[2,64,32,128]{3,2,1,0:T(8,128)(2,1)}, bf16[2,64,32,128]{3,2,1,0:T(8,128)(2,1)S(1)}, u32[]{:S(2)}) %copy-start) | copy-done | bytes 1048600
  18.4 1.4 %copy-done.4 = bf16[32,128,256]{2,1,0:T(8,128)(2,1)} copy-done((bf16[32,128,256]{2,1,0:T(8,128)(2,1)}, bf16[32,128,256]{2,1,0:T(8,128)(2,1)S(1)}, u32[]{:S(2)}) %copy-start.4) | copy-done | bytes 2097176
  19.8 1.0 %collective-permute-done.2.raw_ref = bf16[2,64,32,128]{3,2,1,0:T(8,128)(2,1)S(1)} collective-permute-done((bf16[2,64,32,128]{3,2,1,0:T(8,128)(2,1)}, bf16[2,64,32,128]{3,2,1,0:T(8,128)(2,1)S(1)}, u32[]{:S(2)}, u32[]{:S(2)}) %collective-permute-start.2) | collective-permute-done | bytes 1048608 | tf_op jit(solution)/shard_map/ppermute | solution.py:28
  20.8 2.7 %shard_map.48 = (bf16[64,32,128]{2,1,0:T(8,128)(2,1)}, bf16[64,32,128]{2,1,0:T(8,128)(2,1)}, bf16[2,40,32,128]{3,2,1,0:T(8,128)(2,1)}, bf16[2,24,32,128]{3,2,1,0:T(8,128)(2,1)}) custom-call(s32[64]{0:T(128)S(1)} %select_reduce_fusion._.order_ref, bf16[2,64,32,128]{3,2,1,0:T(8,128)(2,1)S(1)} %collective-permute-done.2.raw_ref, ...), custom_call_target="tpu_custom_call" | custom-call | tf_op jit(solution)/shard_map/pallas_call | solution.py:333
  24.0 6.0 %collective-permute-start.8 = (bf16[2,40,32,128]{3,2,1,0:T(8,128)(2,1)}, bf16[2,40,32,128]{3,2,1,0:T(8,128)(2,1)}, u32[]{:S(2)}, u32[]{:S(2)}) collective-permute-start(bf16[2,40,32,128]{3,2,1,0:T(8,128)(2,1)} %get-tuple-element.37), channel_id=1, source_target_pairs={{8,16},{16,8},{24,32},{32,24},{40,48},{48,40},{56,64},{64,56},{72,... | collective-permute-start | bytes 1966088 | tf_op jit(solution)/shard_map/ppermute | solution.py:28
  32.1 1.2 %copy-done.1 = bf16[2,64,32,128]{3,2,1,0:T(8,128)(2,1)S(1)} copy-done((bf16[2,64,32,128]{3,2,1,0:T(8,128)(2,1)S(1)}, bf16[2,64,32,128]{3,2,1,0:T(8,128)(2,1)}, u32[]{:S(2)}) %copy-start.1) | copy-done | bytes 1048600
  33.3 2.4 %shard_map.49 = (bf16[2,320,32,128]{3,2,1,0:T(8,128)(2,1)S(1)}, bf16[64,32,128]{2,1,0:T(8,128)(2,1)}, bf16[64,32,128]{2,1,0:T(8,128)(2,1)}) custom-call(bf16[2,64,32,128]{3,2,1,0:T(8,128)(2,1)S(1)} %get-tuple-element.27._own.own_ref, bf16[2,64,32,128]{3,2,1,0:T(8,128)(2,1)S(1)} %copy-done.1, bf16[64,32,128]{2,1,0:T(8,128)(2,1)} %get-tuple-element.30.refs_0_, ...), custom_call_target="tpu_custom_call" | custom-call | tf_op jit(solution)/shard_map/pallas_call | solution.py:351
  35.8 2.3 %copy-done.2 = bf16[2,320,32,128]{3,2,1,0:T(8,128)(2,1)} copy-done((bf16[2,320,32,128]{3,2,1,0:T(8,128)(2,1)}, bf16[2,320,32,128]{3,2,1,0:T(8,128)(2,1)S(1)}, u32[]{:S(2)}) %copy-start.2) | copy-done | bytes 5242904
  39.3 0.9 %collective-permute-done.6.refs_0_ = bf16[64,32,128]{2,1,0:T(8,128)(2,1)S(1)} collective-permute-done((bf16[64,32,128]{2,1,0:T(8,128)(2,1)}, bf16[64,32,128]{2,1,0:T(8,128)(2,1)S(1)}, u32[]{:S(2)}, u32[]{:S(2)}) %collective-permute-start.6) | collective-permute-done | bytes 524320 | tf_op jit(solution)/shard_map/ppermute | solution.py:33
  40.9 1.7 %shard_map.50.late_ref = bf16[2,128,32,128]{3,2,1,0:T(8,128)(2,1)S(1)} custom-call(bf16[64,32,128]{2,1,0:T(8,128)(2,1)S(1)} %collective-permute-done.6.refs_0_, bf16[64,32,128]{2,1,0:T(8,128)(2,1)S(1)} %collective-permute-done.7.refs_1_, bf16[2,40,32,128]{3,2,1,0:T(8,128)(2,1)} %collective-permute-done.8.refs_2_, ...), custom_call_target="tpu_custom_call" | custom-call | flops 21474836480 | tf_op jit(solution)/shard_map/pallas_call | solution.py:363
  42.7 4.4 %shard_map.51 = (f32[6,16,16,128]{3,2,1,0:T(8,128)S(1)}, bf16[5,16,16,128]{3,2,1,0:T(8,128)(2,1)S(1)}, bf16[5,16,16,128]{3,2,1,0:T(8,128)(2,1)S(1)}) custom-call(s32[128]{0:T(128)S(1)} %get-tuple-element.48._first.first_ref, s32[128]{0:T(128)S(1)} %get-tuple-element.47._second.second_ref, s32[1]{0:T(128)S(6)} %copy.9.live_ref, s32[1]{0:T(128)} %bitcast.6.z_ref, ...), custom_call_target="tpu_custom_call" | custom-call | flops 8589934592 | bytes 8388608 | tf_op jit(solution)/shard_map/pallas_call | solution.py:380
  47.2 5.9 %collective-permute-start.10 = (bf16[5,16,16,128]{3,2,1,0:T(8,128)(2,1)S(1)}, bf16[5,16,16,128]{3,2,1,0:T(8,128)(2,1)S(1)}, u32[]{:S(2)}, u32[]{:S(2)}) collective-permute-start(bf16[5,16,16,128]{3,2,1,0:T(8,128)(2,1)S(1)} %get-tuple-element.41), channel_id=1, source_target_pairs={{0,7},{1,0},{2,1},{3,2},{4,3},{5,4},{6,5},{7,6},{8,15},{9,8},{10,9... | collective-permute-start | bytes 983048 | tf_op jit(solution)/shard_map/ppermute | solution.py:397
  53.1 7.1 %collective-permute-done.10.right_ref = bf16[5,16,16,128]{3,2,1,0:T(8,128)(2,1)S(1)} collective-permute-done((bf16[5,16,16,128]{3,2,1,0:T(8,128)(2,1)S(1)}, bf16[5,16,16,128]{3,2,1,0:T(8,128)(2,1)S(1)}, u32[]{:S(2)}, u32[]{:S(2)}) %collective-permute-start.10) | collective-permute-done | bytes 327712 | tf_op jit(solution)/shard_map/ppermute | solution.py:397
  60.2 3.4 %collective-permute-done.9.left_ref = bf16[5,16,16,128]{3,2,1,0:T(8,128)(2,1)S(1)} collective-permute-done((bf16[5,16,16,128]{3,2,1,0:T(8,128)(2,1)S(1)}, bf16[5,16,16,128]{3,2,1,0:T(8,128)(2,1)S(1)}, u32[]{:S(2)}, u32[]{:S(2)}) %collective-permute-start.9) | collective-permute-done | bytes 327712 | tf_op jit(solution)/shard_map/ppermute | solution.py:397
  64.5 3.1 %collective-permute-start.12 = (bf16[2,16,16,128]{3,2,1,0:T(8,128)(2,1)S(1)}, bf16[2,16,16,128]{3,2,1,0:T(8,128)(2,1)S(1)}, u32[]{:S(2)}, u32[]{:S(2)}) collective-permute-start(bf16[2,16,16,128]{3,2,1,0:T(8,128)(2,1)S(1)} %get-tuple-element.44), channel_id=1, source_target_pairs={{0,3},{1,4},{2,5},{3,6},{4,7},{5,0},{6,1},{7,2},{8,11},{9,12},{10,... | collective-permute-start | bytes 393224 | tf_op jit(solution)/shard_map/ppermute | solution.py:397
  67.6 6.4 %collective-permute-done.11.refs_0_ = bf16[2,16,16,128]{3,2,1,0:T(8,128)(2,1)S(1)} collective-permute-done((bf16[2,16,16,128]{3,2,1,0:T(8,128)(2,1)S(1)}, bf16[2,16,16,128]{3,2,1,0:T(8,128)(2,1)S(1)}, u32[]{:S(2)}, u32[]{:S(2)}) %collective-permute-start.11) | collective-permute-done | bytes 131104 | tf_op jit(solution)/shard_map/ppermute | solution.py:397
  74.1 2.9 %collective-permute-done.12.refs_1_ = bf16[2,16,16,128]{3,2,1,0:T(8,128)(2,1)S(1)} collective-permute-done((bf16[2,16,16,128]{3,2,1,0:T(8,128)(2,1)S(1)}, bf16[2,16,16,128]{3,2,1,0:T(8,128)(2,1)S(1)}, u32[]{:S(2)}, u32[]{:S(2)}) %collective-permute-start.12) | collective-permute-done | bytes 131104 | tf_op jit(solution)/shard_map/ppermute | solution.py:397
  76.9 0.9 %shard_map.53 = f32[128,512]{1,0:T(8,128)} custom-call(f32[2,16,16,128]{3,2,1,0:T(8,128)S(1)} %get-tuple-element.42.own_ref, bf16[2,16,16,128]{3,2,1,0:T(8,128)(2,1)S(1)} %collective-permute-done.11.refs_0_, bf16[2,16,16,128]{3,2,1,0:T(8,128)(2,1)S(1)} %collective-permute-done.12.refs_1_), custom_call_target="tpu_custom_call" | custom-call | tf_op jit(solution)/shard_map/pallas_call | solution.py:409
  (44 shorter events, 7.3 us)
Async XLA Ops:
  0.0 14.1 %collective-permute-start.1 = (bf16[2,64,32,128]{3,2,1,0:T(8,128)(2,1)}, bf16[2,64,32,128]{3,2,1,0:T(8,128)(2,1)}, u32[]{:S(2)}, u32[]{:S(2)}) collective-permute-start(bf16[2,64,32,128]{3,2,1,0:T(8,128)(2,1)} %bitcast.34), channel_id=1, source_target_pairs={{0,8},{8,0},{16,24},{24,16},{32,40},{40,32},{48,56},{56,48},{64,72... | collective-permute-start | bytes 3145736 | tf_op jit(solution)/shard_map/ppermute | solution.py:33
  0.0 20.8 %collective-permute-start.2 = (bf16[2,64,32,128]{3,2,1,0:T(8,128)(2,1)}, bf16[2,64,32,128]{3,2,1,0:T(8,128)(2,1)S(1)}, u32[]{:S(2)}, u32[]{:S(2)}) collective-permute-start(bf16[2,64,32,128]{3,2,1,0:T(8,128)(2,1)} %bitcast.35), channel_id=1, source_target_pairs={{8,24},{16,0},{24,40},{32,16},{40,56},{48,32},{56,72},{64,48},{72,... | collective-permute-start | bytes 3145736 | tf_op jit(solution)/shard_map/ppermute | solution.py:28
  7.7 1.2 %copy-start.3 = (bf16[2,64,2,2048]{3,2,1,0:T(2,128)(2,1)S(1)}, bf16[2,64,2,2048]{3,2,1,0:T(2,128)(2,1)}, u32[]{:S(2)}) copy-start(bf16[2,64,2,2048]{3,2,1,0:T(2,128)(2,1)} %param.6) | copy-start | bytes 3145732
  11.4 20.7 %collective-permute-start.5 = (bf16[2,64,32,128]{3,2,1,0:T(8,128)(2,1)}, bf16[2,64,32,128]{3,2,1,0:T(8,128)(2,1)S(1)}, u32[]{:S(2)}, u32[]{:S(2)}) collective-permute-start(bf16[2,64,32,128]{3,2,1,0:T(8,128)(2,1)} %get-tuple-element.32), channel_id=1, source_target_pairs={{0,16},{16,32},{24,8},{32,48},{40,24},{48,64},{56,40},{64,80},{72,... | collective-permute-start | bytes 3145736 | tf_op jit(solution)/shard_map/ppermute | solution.py:28
  17.4 1.0 %copy-start = (bf16[2,64,32,128]{3,2,1,0:T(8,128)(2,1)}, bf16[2,64,32,128]{3,2,1,0:T(8,128)(2,1)S(1)}, u32[]{:S(2)}) copy-start(bf16[2,64,32,128]{3,2,1,0:T(8,128)(2,1)S(1)} %get-tuple-element.28.sib_ref) | copy-start | bytes 3145732
  18.4 1.4 %copy-start.4 = (bf16[32,128,256]{2,1,0:T(8,128)(2,1)}, bf16[32,128,256]{2,1,0:T(8,128)(2,1)S(1)}, u32[]{:S(2)}) copy-start(bf16[32,128,256]{2,1,0:T(8,128)(2,1)S(1)} %get-tuple-element.38.wave_ref) | copy-start | bytes 6291460
  23.5 8.6 %collective-permute-start.3 = (bf16[64,32,128]{2,1,0:T(8,128)(2,1)}, bf16[64,32,128]{2,1,0:T(8,128)(2,1)S(1)}, u32[]{:S(2)}, u32[]{:S(2)}) collective-permute-start(bf16[64,32,128]{2,1,0:T(8,128)(2,1)} %get-tuple-element.30.refs_0_), channel_id=1, source_target_pairs={{0,8},{8,0},{16,24},{24,16},{32,40},{40,32},{48,56},{56,48},{64,72... | collective-permute-start | bytes 1572872 | tf_op jit(solution)/shard_map/ppermute | solution.py:33
  23.5 8.6 %collective-permute-start.4 = (bf16[64,32,128]{2,1,0:T(8,128)(2,1)}, bf16[64,32,128]{2,1,0:T(8,128)(2,1)S(1)}, u32[]{:S(2)}, u32[]{:S(2)}) collective-permute-start(bf16[64,32,128]{2,1,0:T(8,128)(2,1)} %get-tuple-element.31.refs_1_), channel_id=1, source_target_pairs={{0,8},{8,0},{16,24},{24,16},{32,40},{40,32},{48,56},{56,48},{64,72... | collective-permute-start | bytes 1572872 | tf_op jit(solution)/shard_map/ppermute | solution.py:33
  24.0 15.3 %collective-permute-start.8 = (bf16[2,40,32,128]{3,2,1,0:T(8,128)(2,1)}, bf16[2,40,32,128]{3,2,1,0:T(8,128)(2,1)}, u32[]{:S(2)}, u32[]{:S(2)}) collective-permute-start(bf16[2,40,32,128]{3,2,1,0:T(8,128)(2,1)} %get-tuple-element.37), channel_id=1, source_target_pairs={{8,16},{16,8},{24,32},{32,24},{40,48},{48,40},{56,64},{64,56},{72,... | collective-permute-start | bytes 1966088 | tf_op jit(solution)/shard_map/ppermute | solution.py:28
  32.1 1.2 %copy-start.1 = (bf16[2,64,32,128]{3,2,1,0:T(8,128)(2,1)S(1)}, bf16[2,64,32,128]{3,2,1,0:T(8,128)(2,1)}, u32[]{:S(2)}) copy-start(bf16[2,64,32,128]{3,2,1,0:T(8,128)(2,1)} %copy-done) | copy-start | bytes 3145732
  33.3 5.9 %copy-start.6 = (f32[2048]{0:T(1024)S(1)}, f32[2048]{0:T(1024)}, u32[]{:S(2)}) copy-start(f32[2048]{0:T(1024)} %param.7) | copy-start | bytes 24580
  35.7 2.3 %copy-start.2 = (bf16[2,320,32,128]{3,2,1,0:T(8,128)(2,1)}, bf16[2,320,32,128]{3,2,1,0:T(8,128)(2,1)S(1)}, u32[]{:S(2)}) copy-start(bf16[2,320,32,128]{3,2,1,0:T(8,128)(2,1)S(1)} %get-tuple-element.34.near_ref) | copy-start | bytes 15728644
  38.1 2.1 %collective-permute-start.6 = (bf16[64,32,128]{2,1,0:T(8,128)(2,1)}, bf16[64,32,128]{2,1,0:T(8,128)(2,1)S(1)}, u32[]{:S(2)}, u32[]{:S(2)}) collective-permute-start(bf16[64,32,128]{2,1,0:T(8,128)(2,1)} %get-tuple-element.35), channel_id=1, source_target_pairs={{0,8},{8,0},{16,24},{24,16},{32,40},{40,32},{48,56},{56,48},{64,72... | collective-permute-start | bytes 1572872 | tf_op jit(solution)/shard_map/ppermute | solution.py:33
  38.1 2.9 %collective-permute-start.7 = (bf16[64,32,128]{2,1,0:T(8,128)(2,1)}, bf16[64,32,128]{2,1,0:T(8,128)(2,1)S(1)}, u32[]{:S(2)}, u32[]{:S(2)}) collective-permute-start(bf16[64,32,128]{2,1,0:T(8,128)(2,1)} %get-tuple-element.36), channel_id=1, source_target_pairs={{0,8},{8,0},{16,24},{24,16},{32,40},{40,32},{48,56},{56,48},{64,72... | collective-permute-start | bytes 1572872 | tf_op jit(solution)/shard_map/ppermute | solution.py:33
  39.2 3.4 %slice-start = ((s8[5242880]{0:T(1024)(128)(4,1)}), s8[4194304]{0:T(1024)(128)(4,1)S(1)}, s32[]{:S(2)}) async-start(s8[5242880]{0:T(1024)(128)(4,1)} %bitcast.32), calls=%async_computation | async-start | bytes 8388608
  39.3 3.4 %slice-start.1 = ((s8[5242880]{0:T(1024)(128)(4,1)}), s8[1048576]{0:T(1024)(128)(4,1)S(1)}, s32[]{:S(2)}) async-start(s8[5242880]{0:T(1024)(128)(4,1)} %bitcast.32), calls=%async_computation.1 | async-start | bytes 2097152
  39.3 3.4 %copy-start.5 = (bf16[32,128,256]{2,1,0:T(8,128)(2,1)S(1)}, bf16[32,128,256]{2,1,0:T(8,128)(2,1)}, u32[]{:S(2)}) copy-start(bf16[32,128,256]{2,1,0:T(8,128)(2,1)} %copy-done.4) | copy-start | bytes 6291460
  47.2 13.1 %collective-permute-start.10 = (bf16[5,16,16,128]{3,2,1,0:T(8,128)(2,1)S(1)}, bf16[5,16,16,128]{3,2,1,0:T(8,128)(2,1)S(1)}, u32[]{:S(2)}, u32[]{:S(2)}) collective-permute-start(bf16[5,16,16,128]{3,2,1,0:T(8,128)(2,1)S(1)} %get-tuple-element.41), channel_id=1, source_target_pairs={{0,7},{1,0},{2,1},{3,2},{4,3},{5,4},{6,5},{7,6},{8,15},{9,8},{10,9... | collective-permute-start | bytes 983048 | tf_op jit(solution)/shard_map/ppermute | solution.py:397
  53.1 10.5 %collective-permute-start.9 = (bf16[5,16,16,128]{3,2,1,0:T(8,128)(2,1)S(1)}, bf16[5,16,16,128]{3,2,1,0:T(8,128)(2,1)S(1)}, u32[]{:S(2)}, u32[]{:S(2)}) collective-permute-start(bf16[5,16,16,128]{3,2,1,0:T(8,128)(2,1)S(1)} %get-tuple-element.40), channel_id=1, source_target_pairs={{0,1},{1,2},{2,3},{3,4},{4,5},{5,6},{6,7},{7,0},{8,9},{9,10},{10,1... | collective-permute-start | bytes 983048 | tf_op jit(solution)/shard_map/ppermute | solution.py:397
  63.7 10.3 %collective-permute-start.11 = (bf16[2,16,16,128]{3,2,1,0:T(8,128)(2,1)S(1)}, bf16[2,16,16,128]{3,2,1,0:T(8,128)(2,1)S(1)}, u32[]{:S(2)}, u32[]{:S(2)}) collective-permute-start(bf16[2,16,16,128]{3,2,1,0:T(8,128)(2,1)S(1)} %get-tuple-element.43), channel_id=1, source_target_pairs={{0,5},{1,6},{2,7},{3,0},{4,1},{5,2},{6,3},{7,4},{8,13},{9,14},{10,... | collective-permute-start | bytes 393224 | tf_op jit(solution)/shard_map/ppermute | solution.py:397
  64.5 12.4 %collective-permute-start.12 = (bf16[2,16,16,128]{3,2,1,0:T(8,128)(2,1)S(1)}, bf16[2,16,16,128]{3,2,1,0:T(8,128)(2,1)S(1)}, u32[]{:S(2)}, u32[]{:S(2)}) collective-permute-start(bf16[2,16,16,128]{3,2,1,0:T(8,128)(2,1)S(1)} %get-tuple-element.44), channel_id=1, source_target_pairs={{0,3},{1,4},{2,5},{3,6},{4,7},{5,0},{6,1},{7,2},{8,11},{9,12},{10,... | collective-permute-start | bytes 393224 | tf_op jit(solution)/shard_map/ppermute | solution.py:397

commit v7 on v6

--- a/solution.py
+++ b/solution.py
@@ -98,33 +98,33 @@
             tail_ref[v, p] = out_ref[order_ref[head + p]]
 
 
-def late_kernel(*refs):
-    *swapped_refs, head_ref, tail_ref, out_ref, sem = refs
-    copies = []
-    for v in range(out_ref.shape[0]):
-        parts = (swapped_refs[v], head_ref.at[v], tail_ref.at[v])
-        copies += lay(parts, out_ref.at[v], sem.at[v])[0]
-    for copy in copies:
-        copy.wait()
-
-
 def corr_kernel(
     first_ref,
     second_ref,
     live_ref,
     z_ref,
     near_ref,
-    late_ref,
+    swapped_refs,
+    head_ref,
+    tail_ref,
     weight_ref,
     fold_ref,
     wave_ref,
     keep_ref,
     up_ref,
     down_ref,
+    late_ref,
     cross,
     mid,
     corr,
+    sem,
 ):
+    copies = []
+    for v, ref in enumerate(swapped_refs):
+        parts = (ref, head_ref.at[v], tail_ref.at[v])
+        copies += lay(parts, late_ref.at[v], sem.at[v])[0]
+    for copy in copies:
+        copy.wait()
     windows, early = near_ref.shape[:2]
     slots = mid.shape[1] // windows
     weight = weight_ref[...]
@@ -360,17 +360,7 @@
         compiler_params=pltpu.CompilerParams(vmem_limit_bytes=24 << 20),
         cost_estimate=pl.CostEstimate(flops=0, bytes_accessed=0, transcendentals=0),
     )(own, sib, *ahead, *[swap(a) for a in ahead], back, tail)
-    late = pl.pallas_call(
-        late_kernel,
-        out_shape=jax.ShapeDtypeStruct((win_dev, 2 * ch_dev, rows, LANES), BF),
-        in_specs=[ANY] * (win_dev + 2),
-        out_specs=VM,
-        scratch_shapes=[pltpu.SemaphoreType.DMA((win_dev, 3))],
-        compiler_params=pltpu.CompilerParams(vmem_limit_bytes=16 << 20),
-        cost_estimate=pl.CostEstimate(
-            flops=20 << 30, bytes_accessed=0, transcendentals=0
-        ),
-    )(*[swap(b) for b in back], head, tail)
+    swapped = [swap(b) for b in back]
 
     factor = jnp.where(jnp.arange(bins) == 0, 1.0, 2.0).astype(F32)
     weight = (passband * factor).reshape(SUBS, LANES)
@@ -380,18 +370,20 @@
     keep, up, down = pl.pallas_call(
         corr_kernel,
         out_shape=[jax.ShapeDtypeStruct((6, half, wide, slots), F32), give, give],
-        in_specs=[SM] * 4 + [VM] * 5,
+        in_specs=[SM] * 4 + [VM, [ANY] * win_dev, ANY, ANY] + [VM] * 3,
         out_specs=[VM] * 3,
         scratch_shapes=[
+            pltpu.VMEM((win_dev, 2 * ch_dev, rows, LANES), BF),
             pltpu.VMEM((2, GROUP * rows, 2 * LANES), BF),
             pltpu.VMEM((LOW, win_dev * slots, 2 * LANES), BF),
             pltpu.VMEM((LOW, LANES, win_dev * slots), F32),
+            pltpu.SemaphoreType.DMA((win_dev, 3)),
         ],
         compiler_params=pltpu.CompilerParams(vmem_limit_bytes=32 << 20),
         cost_estimate=pl.CostEstimate(
             flops=8 << 30, bytes_accessed=8 << 20, transcendentals=0
         ),
-    )(first, second, live_pairs, z.reshape(1), near, late, weight, fold, wave)
+    )(first, second, live_pairs, z.reshape(1), near, swapped, head, tail, weight, fold, wave)
 
     def along(value, step):
         return lax.ppermute(

time: 78.2 us -> 82 us (1.049)
  local copies, waits for them, and re-layouts: 8.6 us -> 12.7 us
    unnamed x18 -> x16, local copies, waits for them, and re-layouts: 7.1 us -> 11.2 us
    pallas_call x1 -> x0, Pallas kernels: 1.74 us -> none  [local(): pl.pallas_call(late_kernel, out_shape=jax.ShapeDtypeStruct((win_dev, 2 *...]
    pallas_call x1, Pallas kernels: 4.43 us -> 5.7 us  [local(): pl.pallas_call(corr_kernel, out_shape=[jax.ShapeDtypeStruct((6, half, wid...]
  transfers between devices with their start and end apart: 12 -> 12, of which waited for: 7 -> 7; matrix products, arithmetic and copies ran while one was open for 6% -> 6% of each run, Pallas kernels for 14% -> 13%
where the time goes in v7:
time: 82 us; the launch traced here: 81.6 us
  starting transfers between devices  23.9 us (29%)
  waiting for transfers between devices  22.6 us (28%)
  Pallas kernels  17.6 us (21%)
  local copies, waits for them, and re-layouts  12.7 us (15%)
  other arithmetic  3.24 us (4%)
  between operations  1.48 us (2%)
    ppermute x4, waiting for transfers between devices, along(): lax.ppermute(value, 'win', [(i, (i + step) % win_count) for i in range(wi...  19.9 us
    ppermute x3, starting transfers between devices, moved(): lax.ppermute(value, 'pair', [(a, b) for a, b in pairs if 0 <= b < count])  13.1 us
    unnamed x16, local copies, waits for them, and re-layouts  11.2 us
    ppermute x4, starting transfers between devices, along(): lax.ppermute(value, 'win', [(i, (i + step) % win_count) for i in range(wi...  9.84 us
    pallas_call x1, Pallas kernels, local(): pl.pallas_call(corr_kernel, out_shape=[jax.ShapeDtypeStruct((6, half, wid...  5.7 us
    pallas_call x1, Pallas kernels, local(): pl.pallas_call(table_kernel, out_shape=[jax.ShapeDtypeStruct((2 * LOW * G...  3.32 us
    pallas_call x1, Pallas kernels, local(): pl.pallas_call(forward_kernel, out_shape=[jax.ShapeDtypeStruct(x.shape[1:...  2.71 us
    pallas_call x1, Pallas kernels, local(): pl.pallas_call(gather_kernel, out_shape=[jax.ShapeDtypeStruct((win_dev, 5...  2.47 us
  transfers between devices with their start and end apart: 12, of which 7 were waited for; matrix products, arithmetic and copies ran while one was open for 6% of the time, Pallas kernels for 13%

profile of v7, /device:TPU:6, one launch (start us, length us, event | category | flops | bytes accessed | tf_op | source)
XLA Modules:
  0.0 81.6 jit_solution(5543546934713553407)
XLA Ops:
  0.0 5.2 %collective-permute-start.2 = (bf16[2,64,32,128]{3,2,1,0:T(8,128)(2,1)}, bf16[2,64,32,128]{3,2,1,0:T(8,128)(2,1)S(1)}, u32[]{:S(2)}, u32[]{:S(2)}) collective-permute-start(bf16[2,64,32,128]{3,2,1,0:T(8,128)(2,1)} %bitcast.33), channel_id=1, source_target_pairs={{8,24},{16,0},{24,40},{32,16},{40,56},{48,32},{56,72},{64,48},{72,... | collective-permute-start | bytes 3145736 | tf_op jit(solution)/shard_map/ppermute | solution.py:28
  5.2 0.9 %compare_select_fusion = s32[32,128,1]{1,2,0:T(1,128)S(1)} fusion(s32[32,128,2]{1,2,0:T(2,128)} %param.8, s32[32]{0:T(128)S(1)} %fusion.5), kind=kLoop, calls=%fused_computation.4 | loop fusion | flops 94208 | bytes 32896 | tf_op jit(solution)/shard_map/jit(_where)/select_n | solution.py:269
  7.7 1.2 %copy-done.4 = bf16[2,64,2,2048]{3,2,1,0:T(2,128)(2,1)S(1)} copy-done((bf16[2,64,2,2048]{3,2,1,0:T(2,128)(2,1)S(1)}, bf16[2,64,2,2048]{3,2,1,0:T(2,128)(2,1)}, u32[]{:S(2)}) %copy-start.4) | copy-done | bytes 1048600
  8.9 2.4 %shard_map.46 = (bf16[2,64,32,128]{3,2,1,0:T(8,128)(2,1)}, bf16[2,64,32,128]{3,2,1,0:T(8,128)(2,1)S(1)}) custom-call(bf16[2,64,32,128]{3,2,1,0:T(8,128)(2,1)S(1)} %bitcast.34, s32[64]{0:T(128)S(1)} %select_reduce_fusion._.order_ref), custom_call_target="tpu_custom_call" | custom-call | flops 1073741824 | bytes 2097152 | tf_op jit(solution)/shard_map/pallas_call | solution.py:308
  11.4 1.9 %collective-permute-start.5 = (bf16[2,64,32,128]{3,2,1,0:T(8,128)(2,1)}, bf16[2,64,32,128]{3,2,1,0:T(8,128)(2,1)S(1)}, u32[]{:S(2)}, u32[]{:S(2)}) collective-permute-start(bf16[2,64,32,128]{3,2,1,0:T(8,128)(2,1)} %get-tuple-element.32), channel_id=1, source_target_pairs={{0,16},{16,32},{24,8},{32,48},{40,24},{48,64},{56,40},{64,80},{72,... | collective-permute-start | bytes 3145736 | tf_op jit(solution)/shard_map/ppermute | solution.py:28
  14.1 3.3 %shard_map.47 = (bf16[512,256]{1,0:T(8,128)(2,1)S(1)}, bf16[32,128,256]{2,1,0:T(8,128)(2,1)S(1)}, bf16[2,64,32,128]{3,2,1,0:T(8,128)(2,1)S(1)}) custom-call(bf16[2,64,32,128]{3,2,1,0:T(8,128)(2,1)} %collective-permute-done.1.sib_ref, bf16[2,64,32,128]{3,2,1,0:T(8,128)(2,1)S(1)} %get-tuple-element.27._own.own_ref, s32[128]{0:T(128)S(1)} %get-tuple-element.48._first.first_ref, ...), custom_call_target="tpu_custom_call" | custom-call | flops 1073741824 | bytes 2097152 | tf_op jit(solution)/shard_map/pallas_call | solution.py:318
  17.4 1.0 %copy-done = bf16[2,64,32,128]{3,2,1,0:T(8,128)(2,1)} copy-done((bf16[2,64,32,128]{3,2,1,0:T(8,128)(2,1)}, bf16[2,64,32,128]{3,2,1,0:T(8,128)(2,1)S(1)}, u32[]{:S(2)}) %copy-start) | copy-done | bytes 1048600
  18.4 1.4 %copy-done.5 = bf16[32,128,256]{2,1,0:T(8,128)(2,1)} copy-done((bf16[32,128,256]{2,1,0:T(8,128)(2,1)}, bf16[32,128,256]{2,1,0:T(8,128)(2,1)S(1)}, u32[]{:S(2)}) %copy-start.5) | copy-done | bytes 2097176
  19.8 1.0 %collective-permute-done.2.raw_ref = bf16[2,64,32,128]{3,2,1,0:T(8,128)(2,1)S(1)} collective-permute-done((bf16[2,64,32,128]{3,2,1,0:T(8,128)(2,1)}, bf16[2,64,32,128]{3,2,1,0:T(8,128)(2,1)S(1)}, u32[]{:S(2)}, u32[]{:S(2)}) %collective-permute-start.2) | collective-permute-done | bytes 1048608 | tf_op jit(solution)/shard_map/ppermute | solution.py:28
  20.8 2.7 %shard_map.48 = (bf16[64,32,128]{2,1,0:T(8,128)(2,1)}, bf16[64,32,128]{2,1,0:T(8,128)(2,1)}, bf16[2,40,32,128]{3,2,1,0:T(8,128)(2,1)}, bf16[2,24,32,128]{3,2,1,0:T(8,128)(2,1)}) custom-call(s32[64]{0:T(128)S(1)} %select_reduce_fusion._.order_ref, bf16[2,64,32,128]{3,2,1,0:T(8,128)(2,1)S(1)} %collective-permute-done.2.raw_ref, ...), custom_call_target="tpu_custom_call" | custom-call | tf_op jit(solution)/shard_map/pallas_call | solution.py:333
  24.0 6.0 %collective-permute-start.8 = (bf16[2,40,32,128]{3,2,1,0:T(8,128)(2,1)}, bf16[2,40,32,128]{3,2,1,0:T(8,128)(2,1)}, u32[]{:S(2)}, u32[]{:S(2)}) collective-permute-start(bf16[2,40,32,128]{3,2,1,0:T(8,128)(2,1)} %get-tuple-element.37), channel_id=1, source_target_pairs={{8,16},{16,8},{24,32},{32,24},{40,48},{48,40},{56,64},{64,56},{72,... | collective-permute-start | bytes 1966088 | tf_op jit(solution)/shard_map/ppermute | solution.py:28
  32.1 1.2 %copy-done.1 = bf16[2,64,32,128]{3,2,1,0:T(8,128)(2,1)S(1)} copy-done((bf16[2,64,32,128]{3,2,1,0:T(8,128)(2,1)S(1)}, bf16[2,64,32,128]{3,2,1,0:T(8,128)(2,1)}, u32[]{:S(2)}) %copy-start.1) | copy-done | bytes 1048600
  33.3 2.5 %shard_map.49 = (bf16[2,320,32,128]{3,2,1,0:T(8,128)(2,1)S(1)}, bf16[64,32,128]{2,1,0:T(8,128)(2,1)}, bf16[64,32,128]{2,1,0:T(8,128)(2,1)}) custom-call(bf16[2,64,32,128]{3,2,1,0:T(8,128)(2,1)S(1)} %get-tuple-element.27._own.own_ref, bf16[2,64,32,128]{3,2,1,0:T(8,128)(2,1)S(1)} %copy-done.1, bf16[64,32,128]{2,1,0:T(8,128)(2,1)} %get-tuple-element.30.refs_0_, ...), custom_call_target="tpu_custom_call" | custom-call | tf_op jit(solution)/shard_map/pallas_call | solution.py:351
  35.8 2.3 %copy-done.2 = bf16[2,320,32,128]{3,2,1,0:T(8,128)(2,1)} copy-done((bf16[2,320,32,128]{3,2,1,0:T(8,128)(2,1)}, bf16[2,320,32,128]{3,2,1,0:T(8,128)(2,1)S(1)}, u32[]{:S(2)}) %copy-start.2) | copy-done | bytes 5242904
  39.3 0.9 %collective-permute-done.6.swapped_refs_0_ = bf16[64,32,128]{2,1,0:T(8,128)(2,1)S(1)} collective-permute-done((bf16[64,32,128]{2,1,0:T(8,128)(2,1)}, bf16[64,32,128]{2,1,0:T(8,128)(2,1)S(1)}, u32[]{:S(2)}, u32[]{:S(2)}) %collective-permute-start.6) | collective-permute-done | bytes 524320 | tf_op jit(solution)/shard_map/ppermute | solution.py:33
  41.0 2.5 %copy-done.3 = bf16[2,320,32,128]{3,2,1,0:T(8,128)(2,1)S(1)} copy-done((bf16[2,320,32,128]{3,2,1,0:T(8,128)(2,1)S(1)}, bf16[2,320,32,128]{3,2,1,0:T(8,128)(2,1)}, u32[]{:S(2)}) %copy-start.3) | copy-done | bytes 5242904
  43.5 1.6 %copy-done.6 = bf16[32,128,256]{2,1,0:T(8,128)(2,1)S(1)} copy-done((bf16[32,128,256]{2,1,0:T(8,128)(2,1)S(1)}, bf16[32,128,256]{2,1,0:T(8,128)(2,1)}, u32[]{:S(2)}) %copy-start.6) | copy-done | bytes 2097176
  45.1 5.7 %shard_map.50 = (f32[6,16,16,128]{3,2,1,0:T(8,128)S(1)}, bf16[5,16,16,128]{3,2,1,0:T(8,128)(2,1)S(1)}, bf16[5,16,16,128]{3,2,1,0:T(8,128)(2,1)S(1)}) custom-call(s32[128]{0:T(128)S(1)} %get-tuple-element.48._first.first_ref, s32[128]{0:T(128)S(1)} %get-tuple-element.47._second.second_ref, s32[1]{0:T(128)S(6)} %copy.9.live_ref, s32[1]{0:T(128)} %bitcast.6.z_ref, ...), custom_call_target="tpu_custom_call" | custom-call | flops 8589934592 | bytes 8388608 | tf_op jit(solution)/shard_map/pallas_call | solution.py:370
  50.8 5.9 %collective-permute-start.10 = (bf16[5,16,16,128]{3,2,1,0:T(8,128)(2,1)S(1)}, bf16[5,16,16,128]{3,2,1,0:T(8,128)(2,1)S(1)}, u32[]{:S(2)}, u32[]{:S(2)}) collective-permute-start(bf16[5,16,16,128]{3,2,1,0:T(8,128)(2,1)S(1)} %get-tuple-element.41), channel_id=1, source_target_pairs={{0,7},{1,0},{2,1},{3,2},{4,3},{5,4},{6,5},{7,6},{8,15},{9,8},{10,9... | collective-permute-start | bytes 983048 | tf_op jit(solution)/shard_map/ppermute | solution.py:389
  56.7 7.3 %collective-permute-done.10.right_ref = bf16[5,16,16,128]{3,2,1,0:T(8,128)(2,1)S(1)} collective-permute-done((bf16[5,16,16,128]{3,2,1,0:T(8,128)(2,1)S(1)}, bf16[5,16,16,128]{3,2,1,0:T(8,128)(2,1)S(1)}, u32[]{:S(2)}, u32[]{:S(2)}) %collective-permute-start.10) | collective-permute-done | bytes 327712 | tf_op jit(solution)/shard_map/ppermute | solution.py:389
  64.0 3.4 %collective-permute-done.9.left_ref = bf16[5,16,16,128]{3,2,1,0:T(8,128)(2,1)S(1)} collective-permute-done((bf16[5,16,16,128]{3,2,1,0:T(8,128)(2,1)S(1)}, bf16[5,16,16,128]{3,2,1,0:T(8,128)(2,1)S(1)}, u32[]{:S(2)}, u32[]{:S(2)}) %collective-permute-start.9) | collective-permute-done | bytes 327712 | tf_op jit(solution)/shard_map/ppermute | solution.py:389
  68.3 3.1 %collective-permute-start.12 = (bf16[2,16,16,128]{3,2,1,0:T(8,128)(2,1)S(1)}, bf16[2,16,16,128]{3,2,1,0:T(8,128)(2,1)S(1)}, u32[]{:S(2)}, u32[]{:S(2)}) collective-permute-start(bf16[2,16,16,128]{3,2,1,0:T(8,128)(2,1)S(1)} %get-tuple-element.44), channel_id=1, source_target_pairs={{0,3},{1,4},{2,5},{3,6},{4,7},{5,0},{6,1},{7,2},{8,11},{9,12},{10,... | collective-permute-start | bytes 393224 | tf_op jit(solution)/shard_map/ppermute | solution.py:389
  71.4 6.4 %collective-permute-done.11.refs_0_ = bf16[2,16,16,128]{3,2,1,0:T(8,128)(2,1)S(1)} collective-permute-done((bf16[2,16,16,128]{3,2,1,0:T(8,128)(2,1)S(1)}, bf16[2,16,16,128]{3,2,1,0:T(8,128)(2,1)S(1)}, u32[]{:S(2)}, u32[]{:S(2)}) %collective-permute-start.11) | collective-permute-done | bytes 131104 | tf_op jit(solution)/shard_map/ppermute | solution.py:389
  77.8 2.9 %collective-permute-done.12.refs_1_ = bf16[2,16,16,128]{3,2,1,0:T(8,128)(2,1)S(1)} collective-permute-done((bf16[2,16,16,128]{3,2,1,0:T(8,128)(2,1)S(1)}, bf16[2,16,16,128]{3,2,1,0:T(8,128)(2,1)S(1)}, u32[]{:S(2)}, u32[]{:S(2)}) %collective-permute-start.12) | collective-permute-done | bytes 131104 | tf_op jit(solution)/shard_map/ppermute | solution.py:389
  (40 shorter events, 8.2 us)
Async XLA Ops:
  0.0 14.1 %collective-permute-start.1 = (bf16[2,64,32,128]{3,2,1,0:T(8,128)(2,1)}, bf16[2,64,32,128]{3,2,1,0:T(8,128)(2,1)}, u32[]{:S(2)}, u32[]{:S(2)}) collective-permute-start(bf16[2,64,32,128]{3,2,1,0:T(8,128)(2,1)} %bitcast.32), channel_id=1, source_target_pairs={{0,8},{8,0},{16,24},{24,16},{32,40},{40,32},{48,56},{56,48},{64,72... | collective-permute-start | bytes 3145736 | tf_op jit(solution)/shard_map/ppermute | solution.py:33
  0.0 20.8 %collective-permute-start.2 = (bf16[2,64,32,128]{3,2,1,0:T(8,128)(2,1)}, bf16[2,64,32,128]{3,2,1,0:T(8,128)(2,1)S(1)}, u32[]{:S(2)}, u32[]{:S(2)}) collective-permute-start(bf16[2,64,32,128]{3,2,1,0:T(8,128)(2,1)} %bitcast.33), channel_id=1, source_target_pairs={{8,24},{16,0},{24,40},{32,16},{40,56},{48,32},{56,72},{64,48},{72,... | collective-permute-start | bytes 3145736 | tf_op jit(solution)/shard_map/ppermute | solution.py:28
  7.7 1.2 %copy-start.4 = (bf16[2,64,2,2048]{3,2,1,0:T(2,128)(2,1)S(1)}, bf16[2,64,2,2048]{3,2,1,0:T(2,128)(2,1)}, u32[]{:S(2)}) copy-start(bf16[2,64,2,2048]{3,2,1,0:T(2,128)(2,1)} %param.6) | copy-start | bytes 3145732
  11.4 20.8 %collective-permute-start.5 = (bf16[2,64,32,128]{3,2,1,0:T(8,128)(2,1)}, bf16[2,64,32,128]{3,2,1,0:T(8,128)(2,1)S(1)}, u32[]{:S(2)}, u32[]{:S(2)}) collective-permute-start(bf16[2,64,32,128]{3,2,1,0:T(8,128)(2,1)} %get-tuple-element.32), channel_id=1, source_target_pairs={{0,16},{16,32},{24,8},{32,48},{40,24},{48,64},{56,40},{64,80},{72,... | collective-permute-start | bytes 3145736 | tf_op jit(solution)/shard_map/ppermute | solution.py:28
  14.1 25.2 %copy-start.7 = (f32[2048]{0:T(1024)S(1)}, f32[2048]{0:T(1024)}, u32[]{:S(2)}) copy-start(f32[2048]{0:T(1024)} %param.7) | copy-start | bytes 24580
  17.4 1.0 %copy-start = (bf16[2,64,32,128]{3,2,1,0:T(8,128)(2,1)}, bf16[2,64,32,128]{3,2,1,0:T(8,128)(2,1)S(1)}, u32[]{:S(2)}) copy-start(bf16[2,64,32,128]{3,2,1,0:T(8,128)(2,1)S(1)} %get-tuple-element.28.sib_ref) | copy-start | bytes 3145732
  18.4 1.4 %copy-start.5 = (bf16[32,128,256]{2,1,0:T(8,128)(2,1)}, bf16[32,128,256]{2,1,0:T(8,128)(2,1)S(1)}, u32[]{:S(2)}) copy-start(bf16[32,128,256]{2,1,0:T(8,128)(2,1)S(1)} %get-tuple-element.38.wave_ref) | copy-start | bytes 6291460
  23.5 8.6 %collective-permute-start.3 = (bf16[64,32,128]{2,1,0:T(8,128)(2,1)}, bf16[64,32,128]{2,1,0:T(8,128)(2,1)S(1)}, u32[]{:S(2)}, u32[]{:S(2)}) collective-permute-start(bf16[64,32,128]{2,1,0:T(8,128)(2,1)} %get-tuple-element.30.refs_0_), channel_id=1, source_target_pairs={{0,8},{8,0},{16,24},{24,16},{32,40},{40,32},{48,56},{56,48},{64,72... | collective-permute-start | bytes 1572872 | tf_op jit(solution)/shard_map/ppermute | solution.py:33
  23.5 8.6 %collective-permute-start.4 = (bf16[64,32,128]{2,1,0:T(8,128)(2,1)}, bf16[64,32,128]{2,1,0:T(8,128)(2,1)S(1)}, u32[]{:S(2)}, u32[]{:S(2)}) collective-permute-start(bf16[64,32,128]{2,1,0:T(8,128)(2,1)} %get-tuple-element.31.refs_1_), channel_id=1, source_target_pairs={{0,8},{8,0},{16,24},{24,16},{32,40},{40,32},{48,56},{56,48},{64,72... | collective-permute-start | bytes 1572872 | tf_op jit(solution)/shard_map/ppermute | solution.py:33
  24.0 15.3 %collective-permute-start.8 = (bf16[2,40,32,128]{3,2,1,0:T(8,128)(2,1)}, bf16[2,40,32,128]{3,2,1,0:T(8,128)(2,1)}, u32[]{:S(2)}, u32[]{:S(2)}) collective-permute-start(bf16[2,40,32,128]{3,2,1,0:T(8,128)(2,1)} %get-tuple-element.37), channel_id=1, source_target_pairs={{8,16},{16,8},{24,32},{32,24},{40,48},{48,40},{56,64},{64,56},{72,... | collective-permute-start | bytes 1966088 | tf_op jit(solution)/shard_map/ppermute | solution.py:28
  32.1 1.2 %copy-start.1 = (bf16[2,64,32,128]{3,2,1,0:T(8,128)(2,1)S(1)}, bf16[2,64,32,128]{3,2,1,0:T(8,128)(2,1)}, u32[]{:S(2)}) copy-start(bf16[2,64,32,128]{3,2,1,0:T(8,128)(2,1)} %copy-done) | copy-start | bytes 3145732
  35.8 2.3 %copy-start.2 = (bf16[2,320,32,128]{3,2,1,0:T(8,128)(2,1)}, bf16[2,320,32,128]{3,2,1,0:T(8,128)(2,1)S(1)}, u32[]{:S(2)}) copy-start(bf16[2,320,32,128]{3,2,1,0:T(8,128)(2,1)S(1)} %get-tuple-element.34.near_ref) | copy-start | bytes 15728644
  38.1 2.1 %collective-permute-start.6 = (bf16[64,32,128]{2,1,0:T(8,128)(2,1)}, bf16[64,32,128]{2,1,0:T(8,128)(2,1)S(1)}, u32[]{:S(2)}, u32[]{:S(2)}) collective-permute-start(bf16[64,32,128]{2,1,0:T(8,128)(2,1)} %get-tuple-element.35), channel_id=1, source_target_pairs={{0,8},{8,0},{16,24},{24,16},{32,40},{40,32},{48,56},{56,48},{64,72... | collective-permute-start | bytes 1572872 | tf_op jit(solution)/shard_map/ppermute | solution.py:33
  38.1 2.9 %collective-permute-start.7 = (bf16[64,32,128]{2,1,0:T(8,128)(2,1)}, bf16[64,32,128]{2,1,0:T(8,128)(2,1)S(1)}, u32[]{:S(2)}, u32[]{:S(2)}) collective-permute-start(bf16[64,32,128]{2,1,0:T(8,128)(2,1)} %get-tuple-element.36), channel_id=1, source_target_pairs={{0,8},{8,0},{16,24},{24,16},{32,40},{40,32},{48,56},{56,48},{64,72... | collective-permute-start | bytes 1572872 | tf_op jit(solution)/shard_map/ppermute | solution.py:33
  41.0 2.5 %copy-start.3 = (bf16[2,320,32,128]{3,2,1,0:T(8,128)(2,1)S(1)}, bf16[2,320,32,128]{3,2,1,0:T(8,128)(2,1)}, u32[]{:S(2)}) copy-start(bf16[2,320,32,128]{3,2,1,0:T(8,128)(2,1)} %copy-done.2) | copy-start | bytes 15728644
  43.5 1.6 %copy-start.6 = (bf16[32,128,256]{2,1,0:T(8,128)(2,1)S(1)}, bf16[32,128,256]{2,1,0:T(8,128)(2,1)}, u32[]{:S(2)}) copy-start(bf16[32,128,256]{2,1,0:T(8,128)(2,1)} %copy-done.5) | copy-start | bytes 6291460
  50.8 13.2 %collective-permute-start.10 = (bf16[5,16,16,128]{3,2,1,0:T(8,128)(2,1)S(1)}, bf16[5,16,16,128]{3,2,1,0:T(8,128)(2,1)S(1)}, u32[]{:S(2)}, u32[]{:S(2)}) collective-permute-start(bf16[5,16,16,128]{3,2,1,0:T(8,128)(2,1)S(1)} %get-tuple-element.41), channel_id=1, source_target_pairs={{0,7},{1,0},{2,1},{3,2},{4,3},{5,4},{6,5},{7,6},{8,15},{9,8},{10,9... | collective-permute-start | bytes 983048 | tf_op jit(solution)/shard_map/ppermute | solution.py:389
  56.7 10.7 %collective-permute-start.9 = (bf16[5,16,16,128]{3,2,1,0:T(8,128)(2,1)S(1)}, bf16[5,16,16,128]{3,2,1,0:T(8,128)(2,1)S(1)}, u32[]{:S(2)}, u32[]{:S(2)}) collective-permute-start(bf16[5,16,16,128]{3,2,1,0:T(8,128)(2,1)S(1)} %get-tuple-element.40), channel_id=1, source_target_pairs={{0,1},{1,2},{2,3},{3,4},{4,5},{5,6},{6,7},{7,0},{8,9},{9,10},{10,1... | collective-permute-start | bytes 983048 | tf_op jit(solution)/shard_map/ppermute | solution.py:389
  67.5 10.3 %collective-permute-start.11 = (bf16[2,16,16,128]{3,2,1,0:T(8,128)(2,1)S(1)}, bf16[2,16,16,128]{3,2,1,0:T(8,128)(2,1)S(1)}, u32[]{:S(2)}, u32[]{:S(2)}) collective-permute-start(bf16[2,16,16,128]{3,2,1,0:T(8,128)(2,1)S(1)} %get-tuple-element.43), channel_id=1, source_target_pairs={{0,5},{1,6},{2,7},{3,0},{4,1},{5,2},{6,3},{7,4},{8,13},{9,14},{10,... | collective-permute-start | bytes 393224 | tf_op jit(solution)/shard_map/ppermute | solution.py:389
  68.3 12.4 %collective-permute-start.12 = (bf16[2,16,16,128]{3,2,1,0:T(8,128)(2,1)S(1)}, bf16[2,16,16,128]{3,2,1,0:T(8,128)(2,1)S(1)}, u32[]{:S(2)}, u32[]{:S(2)}) collective-permute-start(bf16[2,16,16,128]{3,2,1,0:T(8,128)(2,1)S(1)} %get-tuple-element.44), channel_id=1, source_target_pairs={{0,3},{1,4},{2,5},{3,6},{4,7},{5,0},{6,1},{7,2},{8,11},{9,12},{10,... | collective-permute-start | bytes 393224 | tf_op jit(solution)/shard_map/ppermute | solution.py:389
